TPU v7x, 32 devices: a whole 2x2x4 slice. The times are simulated.
32 devices in a mesh: dp: 8 (over y, x, core), ctx: 4 (over z).
Axes of the slice: x: 2, y: 2, z: 4, core: 2. Of those that a mesh axis runs over, the one named last changes fastest.
Arguments:
- inputs: bfloat16 [8192, 2048], P(('dp', 'ctx')), may hold values from -6 to 6
- cotangent: bfloat16 [8192, 2048], P(('dp', 'ctx')), may hold values from -6 to 6
- segment_ids: int32 [8, 1024], P('dp'), may hold values from 0 to 4, as said below
- real_entry_flags: int32 [8, 1024], P('dp'), may hold values from 0 to 1, as said below
- attention_gain: float32 [2048], P(('dp', 'ctx')), may hold values from 0.1 to 1.9
- feedforward_gain: float32 [2048], P(('dp', 'ctx')), may hold values from 0.1 to 1.9
- query_weight: float32 [2048, 2048], P(('dp', 'ctx')), may hold values from -0.125 to 0.125
- key_weight: float32 [2048, 512], P(('dp', 'ctx')), may hold values from -0.125 to 0.125
- value_weight: float32 [2048, 512], P(('dp', 'ctx')), may hold values from -0.125 to 0.125
- output_weight: float32 [2048, 2048], P(('dp', 'ctx')), may hold values from -0.5 to 0.5
- gate_weight: float32 [2048, 8192], P(('dp', 'ctx')), may hold values from -0.125 to 0.125
- up_weight: float32 [2048, 8192], P(('dp', 'ctx')), may hold values from -0.125 to 0.125
- down_weight: float32 [8192, 2048], P(('dp', 'ctx')), may hold values from -0.0625 to 0.0625
Outputs:
- block_output: bfloat16 [8192, 2048], P(('dp', 'ctx'))
- input_grad: bfloat16 [8192, 2048], P(('dp', 'ctx'))
- attention_gain_grad: float32 [2048], P(('dp', 'ctx'))
- feedforward_gain_grad: float32 [2048], P(('dp', 'ctx'))
- query_weight_grad: float32 [2048, 2048], P(('dp', 'ctx'))
- key_weight_grad: float32 [2048, 512], P(('dp', 'ctx'))
- value_weight_grad: float32 [2048, 512], P(('dp', 'ctx'))
- output_weight_grad: float32 [2048, 2048], P(('dp', 'ctx'))
- gate_weight_grad: float32 [2048, 8192], P(('dp', 'ctx'))
- up_weight_grad: float32 [2048, 8192], P(('dp', 'ctx'))
- down_weight_grad: float32 [8192, 2048], P(('dp', 'ctx'))
Inputs may be any that keep to these rules, and one draw needn't show every extreme that they name: `segment_ids`: along each sequence the ids never fall and start at 0 or 1; a sequence has at most 5 documents; in every sequence one document begins before position 256 and its last token is at or after position 895. `real_entry_flags`: each row is ones followed by 1 to 64 zeros; the padding tokens carry the id of the sequence's last document.
All inputs are finite; a program needn't handle non-finite values.
Results may differ from a plain program's by a relative error of at most 0.015.
Values may be sent and summed in bfloat16 or wider, within the bound.
No kernel may reach another device: no remote copies, remote signals or barrier semaphores. Data moves between devices by JAX's collectives and lax.ppermute only.
A program may use at most 488 MiB of HBM per device.

v0:
```python
import jax
import jax.numpy as jnp
from jax import lax
from jax.sharding import PartitionSpec as P

HEAD_DIM = 64


EPSILON = 1e-05
ROPE_BASE = 500000.0
MASKED_SCORE = -1e30


def matmul(left, right):
    return jnp.dot(left, right, preferred_element_type=jnp.float32)


def matmul_left_t(left, right):
    return lax.dot_general(
        left, right, (((0,), (0,)), ((), ())), preferred_element_type=jnp.float32
    )


def matmul_right_t(left, right):
    return lax.dot_general(
        left, right, (((1,), (1,)), ((), ())), preferred_element_type=jnp.float32
    )


def inverse_root(values):
    return lax.rsqrt(jnp.mean(values * values, axis=-1, keepdims=True) + EPSILON)


def norm_back(values, grad_normed):
    scaled = inverse_root(values)
    unit_rows = values * scaled
    return scaled * (
        grad_normed - unit_rows * jnp.mean(grad_normed * unit_rows, axis=-1, keepdims=True)
    )


def turn(values, cosine, sine_table):
    half_dim = values.shape[-1] // 2
    first_half = values[..., :half_dim]
    second_half = values[..., half_dim:]
    return jnp.concatenate(
        [
            first_half * cosine - second_half * sine_table,
            second_half * cosine + first_half * sine_table,
        ],
        -1,
    )


def angles(packed_text_spans, opening_entry_index, entry_count, head_dim):
    places = opening_entry_index + jnp.arange(entry_count, dtype=jnp.int32)
    device_span_labels = lax.dynamic_slice_in_dim(
        packed_text_spans, opening_entry_index, entry_count
    )
    doc_starts = jnp.sum(
        (packed_text_spans[None, :] < device_span_labels[:, None]).astype(jnp.int32), axis=1
    )
    offsets = (places - doc_starts).astype(jnp.float32)
    half_dim = head_dim // 2
    frequency = ROPE_BASE ** (-(jnp.arange(half_dim, dtype=jnp.float32) * 2.0 / head_dim))
    angle_table = offsets[:, None, None] * frequency[None, None, :]
    return (jnp.cos(angle_table), jnp.sin(angle_table))


def allowed_couplings(packed_text_spans, entry_reality, opening_entry_index, entry_count):
    overall_extent = packed_text_spans.shape[0]
    asking_entry_indices = opening_entry_index + jnp.arange(entry_count, dtype=jnp.int32)
    attended_indices = jnp.arange(overall_extent, dtype=jnp.int32)
    device_span_labels = lax.dynamic_slice_in_dim(
        packed_text_spans, opening_entry_index, entry_count
    )
    same_text_span = (
        (device_span_labels[:, None] == packed_text_spans[None, :])
        & (attended_indices[None, :] <= asking_entry_indices[:, None])
        & (entry_reality[None, :] == 1)
    )
    return same_text_span | (attended_indices[None, :] == asking_entry_indices[:, None])


def attention_scores(query_groups, keys_heads, causal_allowance, score_scale):
    raw_scores = (
        jnp.einsum("ikgd,jkd->kgij", query_groups, keys_heads, preferred_element_type=jnp.float32)
        * score_scale
    )
    return jnp.where(causal_allowance[None, None], raw_scores, MASKED_SCORE)


def attention_forward(query_groups, keys_heads, values_heads, causal_allowance, score_scale):
    scores = attention_scores(query_groups, keys_heads, causal_allowance, score_scale)
    row_top = jnp.max(scores, axis=-1, keepdims=True)
    exponent = jnp.exp(scores - row_top)
    row_total = jnp.sum(exponent, axis=-1, keepdims=True)
    log_total = row_top + jnp.log(row_total)
    probs_low = (exponent / row_total).astype(jnp.bfloat16)
    attended = jnp.einsum(
        "kgij,jkd->ikgd", probs_low, values_heads, preferred_element_type=jnp.float32
    )
    return (probs_low, log_total, attended)


def attention_backward(
    grad_attended,
    query_groups,
    keys_heads,
    values_heads,
    causal_allowance,
    probs_low,
    log_total,
    score_scale,
):
    attention_probs = jnp.exp(
        attention_scores(query_groups, keys_heads, causal_allowance, score_scale) - log_total
    )
    grad_probs = jnp.einsum(
        "ikgd,jkd->kgij", grad_attended, values_heads, preferred_element_type=jnp.float32
    )
    row_delta = jnp.sum(attention_probs * grad_probs, axis=-1, keepdims=True)
    grad_scores = (attention_probs * (grad_probs - row_delta)).astype(jnp.bfloat16)
    grad_queries_rot = (
        jnp.einsum("kgij,jkd->ikgd", grad_scores, keys_heads, preferred_element_type=jnp.float32)
        * score_scale
    )
    key_part = (
        jnp.einsum("kgij,ikgd->jkd", grad_scores, query_groups, preferred_element_type=jnp.float32)
        * score_scale
    )
    value_part = jnp.einsum(
        "kgij,ikgd->jkd", probs_low, grad_attended, preferred_element_type=jnp.float32
    )
    return (grad_queries_rot, key_part, value_part)


def gate_grads(grad_active, gate_value, up_value):
    sigmoid_gate = jax.nn.sigmoid(gate_value)
    grad_gate = (
        grad_active * up_value * sigmoid_gate * (1.0 + gate_value * (1.0 - sigmoid_gate))
    ).astype(jnp.bfloat16)
    grad_up = (grad_active * gate_value * sigmoid_gate).astype(jnp.bfloat16)
    return (grad_gate, grad_up)


def per_device(
    inputs,
    cotangent,
    segment_ids,
    real_entry_flags,
    attention_gain,
    feedforward_gain,
    query_weight,
    key_weight,
    value_weight,
    output_weight,
    gate_weight,
    up_weight,
    down_weight,
):
    low_type = jnp.bfloat16
    entry_count = inputs.shape[0]
    packed_text_spans = segment_ids[0]
    entry_reality = real_entry_flags[0]
    head_dim = HEAD_DIM
    pair_width = key_weight.shape[1]
    pair_heads = pair_width // head_dim
    query_heads = query_weight.shape[1] // head_dim
    group_size = query_heads // pair_heads
    score_scale = head_dim ** (-0.5)
    hidden_units = gate_weight.shape[1]
    first_gain_low = attention_gain.astype(low_type)
    second_gain_low = feedforward_gain.astype(low_type)
    query_low = query_weight.astype(low_type)
    key_low = key_weight.astype(low_type)
    value_low = value_weight.astype(low_type)
    output_low = output_weight.astype(low_type)
    gate_low = gate_weight.astype(low_type)
    up_low = up_weight.astype(low_type)
    down_low = down_weight.astype(low_type)
    tokens_wide = inputs.astype(jnp.float32)
    unit_first = tokens_wide * inverse_root(tokens_wide)
    opening_entry_index = lax.axis_index("ctx") * entry_count
    cosine, sine_table = angles(packed_text_spans, opening_entry_index, entry_count, head_dim)
    causal_allowance = allowed_couplings(
        packed_text_spans, entry_reality, opening_entry_index, entry_count
    )
    gain_first, gain_second, query_full, key_full, value_full, output_full = (
        lax.all_gather(first_gain_low, ("dp", "ctx"), axis=0, tiled=True),
        lax.all_gather(second_gain_low, ("dp", "ctx"), axis=0, tiled=True),
        lax.all_gather(query_low, ("dp", "ctx"), axis=0, tiled=True),
        lax.all_gather(key_low, ("dp", "ctx"), axis=0, tiled=True),
        lax.all_gather(value_low, ("dp", "ctx"), axis=0, tiled=True),
        lax.all_gather(output_low, ("dp", "ctx"), axis=0, tiled=True),
    )
    gain_first = gain_first.astype(jnp.float32)
    gain_second = gain_second.astype(jnp.float32)
    first_hidden = (unit_first * gain_first).astype(low_type)
    queries = turn(
        matmul(first_hidden, query_full).reshape(entry_count, query_heads, head_dim),
        cosine,
        sine_table,
    ).astype(low_type)
    keys_local = (
        turn(
            matmul(first_hidden, key_full).reshape(entry_count, pair_heads, head_dim),
            cosine,
            sine_table,
        )
        .astype(low_type)
        .reshape(entry_count, pair_width)
    )
    values_local = matmul(first_hidden, value_full).astype(low_type)
    keys_all, values_all = (
        lax.all_gather(keys_local, "ctx", axis=0, tiled=True),
        lax.all_gather(values_local, "ctx", axis=0, tiled=True),
    )
    seq_length = keys_all.shape[0]
    keys_heads = keys_all.reshape(seq_length, pair_heads, head_dim)
    values_heads = values_all.reshape(seq_length, pair_heads, head_dim)
    query_groups = queries.reshape(entry_count, pair_heads, group_size, head_dim)
    probs_low, log_total, attended_heads = attention_forward(
        query_groups, keys_heads, values_heads, causal_allowance, score_scale
    )
    attended = attended_heads.reshape(entry_count, query_heads * head_dim).astype(low_type)
    residual = tokens_wide + matmul(attended, output_full)
    unit_second = residual * inverse_root(residual)
    second_hidden = (unit_second * gain_second).astype(low_type)
    columns = second_hidden
    gate_value = matmul(columns, lax.all_gather(gate_low, ("dp", "ctx"), axis=0, tiled=True))
    up_value = matmul(columns, lax.all_gather(up_low, ("dp", "ctx"), axis=0, tiled=True))
    active = (jax.nn.silu(gate_value) * up_value).astype(low_type)
    columns = active
    down_value = matmul(columns, lax.all_gather(down_low, ("dp", "ctx"), axis=0, tiled=True))
    block_output = (residual + down_value).astype(low_type)
    down_weight_grad = lax.psum_scatter(
        matmul_left_t(active, cotangent), ("dp", "ctx"), scatter_dimension=0, tiled=True
    )
    grad_active = matmul_right_t(
        cotangent, lax.all_gather(down_low, ("dp", "ctx"), axis=0, tiled=True)
    )
    grad_gate, grad_up = gate_grads(grad_active, gate_value, up_value)
    joined_grads = jnp.concatenate([grad_gate, grad_up], 1)
    both_grads = lax.psum_scatter(
        matmul_left_t(second_hidden, joined_grads), ("dp", "ctx"), scatter_dimension=0, tiled=True
    )
    gate_weight_grad = both_grads[:, :hidden_units]
    up_weight_grad = both_grads[:, hidden_units:]
    stacked_low = jnp.stack((gate_low, up_low))
    weight_piece = lax.all_gather(stacked_low, ("dp", "ctx"), axis=1, tiled=True)
    grad_second = matmul_right_t(grad_gate, weight_piece[0]) + matmul_right_t(
        grad_up, weight_piece[1]
    )
    second_gain_term = jnp.sum(grad_second * unit_second, axis=0)
    grad_residual = cotangent.astype(jnp.float32) + norm_back(residual, grad_second * gain_second)
    grad_branch = grad_residual.astype(low_type)
    output_term = matmul_left_t(attended, grad_branch)
    query_back, key_back, value_back, output_back = (
        lax.all_gather(query_low, ("dp", "ctx"), axis=0, tiled=True),
        lax.all_gather(key_low, ("dp", "ctx"), axis=0, tiled=True),
        lax.all_gather(value_low, ("dp", "ctx"), axis=0, tiled=True),
        lax.all_gather(output_low, ("dp", "ctx"), axis=0, tiled=True),
    )
    grad_attended = (
        matmul_right_t(grad_branch, output_back)
        .astype(low_type)
        .reshape(entry_count, pair_heads, group_size, head_dim)
    )
    grad_queries_rot, key_part, value_part = attention_backward(
        grad_attended,
        query_groups,
        keys_heads,
        values_heads,
        causal_allowance,
        probs_low,
        log_total,
        score_scale,
    )
    grad_keys_rot, grad_values = (
        lax.psum_scatter(
            key_part.reshape(seq_length, pair_width).astype(jnp.bfloat16),
            "ctx",
            scatter_dimension=0,
            tiled=True,
        ).astype(jnp.float32),
        lax.psum_scatter(
            value_part.reshape(seq_length, pair_width).astype(jnp.bfloat16),
            "ctx",
            scatter_dimension=0,
            tiled=True,
        ).astype(jnp.float32),
    )
    grad_query = (
        turn(grad_queries_rot.reshape(entry_count, query_heads, head_dim), cosine, -sine_table)
        .astype(low_type)
        .reshape(entry_count, query_heads * head_dim)
    )
    grad_key = (
        turn(grad_keys_rot.reshape(entry_count, pair_heads, head_dim), cosine, -sine_table)
        .astype(low_type)
        .reshape(entry_count, pair_width)
    )
    grad_value = grad_values.astype(low_type)
    grad_first = (
        matmul_right_t(grad_query, query_back)
        + matmul_right_t(grad_key, key_back)
        + matmul_right_t(grad_value, value_back)
    )
    query_weight_grad, key_weight_grad, value_weight_grad = (
        lax.psum_scatter(
            matmul_left_t(first_hidden, grad_query), ("dp", "ctx"), scatter_dimension=0, tiled=True
        ),
        lax.psum_scatter(
            matmul_left_t(first_hidden, grad_key), ("dp", "ctx"), scatter_dimension=0, tiled=True
        ),
        lax.psum_scatter(
            matmul_left_t(first_hidden, grad_value), ("dp", "ctx"), scatter_dimension=0, tiled=True
        ),
    )
    first_gain_term = jnp.sum(grad_first * unit_first, axis=0)
    input_grad = (grad_residual + norm_back(tokens_wide, grad_first * gain_first)).astype(low_type)
    output_weight_grad, feedforward_gain_grad, attention_gain_grad = (
        lax.psum_scatter(output_term, ("dp", "ctx"), scatter_dimension=0, tiled=True),
        lax.psum_scatter(second_gain_term, ("dp", "ctx"), scatter_dimension=0, tiled=True),
        lax.psum_scatter(first_gain_term, ("dp", "ctx"), scatter_dimension=0, tiled=True),
    )
    return (
        block_output,
        input_grad,
        attention_gain_grad,
        feedforward_gain_grad,
        query_weight_grad,
        key_weight_grad,
        value_weight_grad,
        output_weight_grad,
        gate_weight_grad,
        up_weight_grad,
        down_weight_grad,
    )


def solution(mesh):
    in_specs = (
        P(("dp", "ctx"), None),
        P(("dp", "ctx"), None),
        P("dp", None),
        P("dp", None),
        P(("dp", "ctx")),
        P(("dp", "ctx")),
        P(("dp", "ctx"), None),
        P(("dp", "ctx"), None),
        P(("dp", "ctx"), None),
        P(("dp", "ctx"), None),
        P(("dp", "ctx"), None),
        P(("dp", "ctx"), None),
        P(("dp", "ctx"), None),
    )
    out_specs = (
        P(("dp", "ctx"), None),
        P(("dp", "ctx"), None),
        P(("dp", "ctx")),
        P(("dp", "ctx")),
        P(("dp", "ctx"), None),
        P(("dp", "ctx"), None),
        P(("dp", "ctx"), None),
        P(("dp", "ctx"), None),
        P(("dp", "ctx"), None),
        P(("dp", "ctx"), None),
        P(("dp", "ctx"), None),
    )
    return jax.shard_map(
        per_device, mesh=mesh, in_specs=in_specs, out_specs=out_specs, check_vma=False
    )
```

profile of v0, /device:TPU:0, one launch (start us, length us, event | category | flops | bytes accessed | tf_op | source)
XLA Modules:
  0.0 5787.9 jit_solution(10395696622471814782)
XLA Ops:
  12.3 42.1 all-reduce.6
  76.2 53.5 all-gather.15.cloned.1.call-done
  160.2 78.8 %all-gather.19.cloned.1.call-done = bf16[2048,2048]{1,0:T(8,128)(2,1)} async-done(((bf16[64,2048]{1,0:T(8,128)(2,1)}), bf16[2048,2048]{1,0:T(8,128)(2,1)}) %all-gather.19.cloned.1.call-update) | async-done | bytes 8388624 | tf_op jit(solution)/shard_map/all_gather | solution.py:192
  246.2 23.6 all-gather.17.cloned.1.call-done
  327.2 21.7 all-gather.21.cloned.1.call-done
  355.3 190.4 %all-gather.27.cloned.1.call-done = bf16[8192,2048]{1,0:T(8,128)(2,1)} async-done(((bf16[256,2048]{1,0:T(8,128)(2,1)}), bf16[8192,2048]{1,0:T(8,128)(2,1)}) %all-gather.27.cloned.1.call-update) | async-done | bytes 33554448 | tf_op jit(solution)/shard_map/all_gather | solution.py:235
  545.8 19.1 fusion.50
  564.9 177.4 %all-gather.25.cloned.1.call-done = bf16[2048,8192]{1,0:T(8,128)(2,1)} async-done(((bf16[64,8192]{1,0:T(8,128)(2,1)}), bf16[2048,8192]{1,0:T(8,128)(2,1)}) %all-gather.25.cloned.1.call-update) | async-done | bytes 33554448 | tf_op jit(solution)/shard_map/all_gather | solution.py:232
  760.1 178.1 %all-gather.23.cloned.1.call-done = bf16[2048,8192]{1,0:T(8,128)(2,1)} async-done(((bf16[64,8192]{1,0:T(8,128)(2,1)}), bf16[2048,8192]{1,0:T(8,128)(2,1)}) %all-gather.23.cloned.1.call-update) | async-done | bytes 33554448 | tf_op jit(solution)/shard_map/all_gather | solution.py:231
  938.2 29.6 multiply_convert_fusion.1
  967.8 328.2 %all-gather.29.cloned.1.call-done = bf16[2,2048,8192]{2,1,0:T(8,128)(2,1)} async-done(((bf16[2,64,8192]{2,1,0:T(8,128)(2,1)}), bf16[2,2048,8192]{2,1,0:T(8,128)(2,1)}) %all-gather.29.cloned.1.call-update) | async-done | bytes 67108880 | tf_op jit(solution)/shard_map/all_gather | solution.py:251
  1313.2 18.3 multiply_reduce_fusion
  1350.6 23.9 fusion.2
  1374.6 28.1 fusion.4
  1414.7 48.3 fusion.7
  1501.9 29.0 fusion.52
  1531.0 18.5 fusion.16
  1556.8 1782.5 %all-reduce.9.cloned.1.call-done = f32[2048,16384]{1,0:T(8,128)} async-done(((f32[2048,16384]{1,0:T(8,128)}), f32[2048,16384]{1,0:T(8,128)}) %all-reduce.9.cloned.1.call-update) | async-done | bytes 134217744
  3348.5 40.4 all-reduce.5
  3393.2 96.1 %reduce-scatter.16.cloned.1.call-done = f32[64,512]{1,0:T(8,128)} async-done(((f32[2048,512]{1,0:T(8,128)}), f32[64,512]{1,0:T(8,128)}) %reduce-scatter.16.cloned.1.call-update) | async-done | bytes 131088 | tf_op jit(solution)/shard_map/reduce_scatter | solution.py:317
  3489.3 149.5 %reduce-scatter.14.cloned.1.call-done = f32[64,512]{1,0:T(8,128)} async-done(((f32[2048,512]{1,0:T(8,128)}), f32[64,512]{1,0:T(8,128)}) %reduce-scatter.14.cloned.1.call-update) | async-done | bytes 131088 | tf_op jit(solution)/shard_map/reduce_scatter | solution.py:314
  3638.8 365.6 %reduce-scatter.18.cloned.1.call-done = f32[64,2048]{1,0:T(8,128)} async-done(((f32[2048,2048]{1,0:T(8,128)}), f32[64,2048]{1,0:T(8,128)}) %reduce-scatter.18.cloned.1.call-update) | async-done | bytes 524304 | tf_op jit(solution)/shard_map/reduce_scatter | solution.py:324
  4004.3 364.9 %reduce-scatter.12.cloned.1.call-done = f32[64,2048]{1,0:T(8,128)} async-done(((f32[2048,2048]{1,0:T(8,128)}), f32[64,2048]{1,0:T(8,128)}) %reduce-scatter.12.cloned.1.call-update) | async-done | bytes 524304 | tf_op jit(solution)/shard_map/reduce_scatter | solution.py:311
  4369.2 1411.4 %reduce-scatter.20.cloned.1.call-done = f32[256,2048]{1,0:T(8,128)} async-done(((f32[8192,2048]{1,0:T(8,128)}), f32[256,2048]{1,0:T(8,128)}) %reduce-scatter.20.cloned.1.call-update) | async-done | bytes 2097168 | tf_op jit(solution)/shard_map/reduce_scatter | solution.py:237
  (176 shorter events, 253.6 us)
Async XLA Ops:
  7.2 63.7 %all-gather.11.cloned.1.call-start = ((), (), s32[]{:S(2)}) async-start(), calls=%async_computation.7 | async-start | bytes 2162688 | tf_op jit(solution)/shard_map/all_gather | solution.py:194
  8.9 120.8 %all-gather.15.cloned.1.call-start = ((), (), s32[]{:S(2)}) async-start(), calls=%async_computation.9 | async-start | bytes 2162688 | tf_op jit(solution)/shard_map/all_gather | solution.py:193
  10.5 148.2 %all-gather.13.cloned.1.call-start = ((), (), s32[]{:S(2)}) async-start(), calls=%async_computation.8 | async-start | bytes 1310720 | tf_op jit(solution)/shard_map/all_gather | solution.py:217
  54.4 184.6 %copy-start.19 = (f32[2048]{0:T(1024)}, f32[2048]{0:T(1024)S(1)}, u32[]{:S(2)}) copy-start(f32[2048]{0:T(1024)S(1)} %convert_element_type.134) | copy-start | bytes 24580
  56.0 183.0 %copy-start.26 = (f32[256]{0:T(256)}, f32[256]{0:T(256)S(1)}, u32[]{:S(2)}) copy-start(f32[256]{0:T(256)S(1)} %add_rsqrt_fusion.1) | copy-start | bytes 3076
  74.3 164.7 %all-gather.19.cloned.1.call-start = ((), (), s32[]{:S(2)}) async-start(), calls=%async_computation.11 | async-start | bytes 8650752 | tf_op jit(solution)/shard_map/all_gather | solution.py:192
  75.1 194.7 %all-gather.17.cloned.1.call-start = ((), (), s32[]{:S(2)}) async-start(), calls=%async_computation.10 | async-start | bytes 1310720 | tf_op jit(solution)/shard_map/all_gather | solution.py:216
  76.2 169.6 %copy-start.21 = (f32[256,32]{0,1:T(8,128)}, f32[256,32]{0,1:T(8,128)S(1)}, u32[]{:S(2)}) copy-start(f32[256,32]{0,1:T(8,128)S(1)} %get-tuple-element.34) | copy-start | bytes 98308
  133.2 215.7 %all-gather.21.cloned.1.call-start = ((), (), s32[]{:S(2)}) async-start(), calls=%async_computation.12 | async-start | bytes 8650752 | tf_op jit(solution)/shard_map/all_gather | solution.py:195
  134.0 411.8 %all-gather.27.cloned.1.call-start = ((), (), s32[]{:S(2)}) async-start(), calls=%async_computation.15 | async-start | bytes 34603008 | tf_op jit(solution)/shard_map/all_gather | solution.py:235
  136.9 605.3 %all-gather.25.cloned.1.call-start = ((), (), s32[]{:S(2)}) async-start(), calls=%async_computation.14 | async-start | bytes 34603008 | tf_op jit(solution)/shard_map/all_gather | solution.py:232
  139.8 798.4 %all-gather.23.cloned.1.call-start = ((), (), s32[]{:S(2)}) async-start(), calls=%async_computation.13 | async-start | bytes 34603008 | tf_op jit(solution)/shard_map/all_gather | solution.py:231
  140.9 1155.1 %all-gather.29.cloned.1.call-start = ((), (), s32[]{:S(2)}) async-start(), calls=%async_computation.16 | async-start | bytes 69206016 | tf_op jit(solution)/shard_map/all_gather | solution.py:251
  144.2 1319.1 %reduce-scatter.10.cloned.1.call-start = ((), (), s32[]{:S(2)}) async-start(), calls=%async_computation.18 | async-start | bytes 1310720 | tf_op jit(solution)/shard_map/reduce_scatter | solution.py:287
  160.2 156.1 %copy-start.4 = (bf16[1024,512]{0,1:T(8,128)(2,1)}, bf16[1024,512]{0,1:T(8,128)(2,1)S(1)}, u32[]{:S(2)}) copy-start(bf16[1024,512]{0,1:T(8,128)(2,1)S(1)} %copy.46) | copy-start | bytes 3145732
  355.0 958.2 %copy-start.3 = (f32[256,2048]{1,0:T(8,128)}, f32[256,2048]{1,0:T(8,128)S(1)}, u32[]{:S(2)}) copy-start(f32[256,2048]{1,0:T(8,128)S(1)} %get-tuple-element.38) | copy-start | bytes 6291460
  355.3 582.9 %copy-start.12 = (bf16[256,2048]{1,0:T(8,128)(2,1)}, bf16[256,2048]{1,0:T(8,128)(2,1)S(1)}, u32[]{:S(2)}) copy-start(bf16[256,2048]{1,0:T(8,128)(2,1)S(1)} %multiply_convert_fusion.3) | copy-start | bytes 3145732
  1350.6 118.3 %reduce-scatter.8.cloned.1.call-start = ((), (), s32[]{:S(2)}) async-start(), calls=%async_computation.17 | async-start | bytes 1310720 | tf_op jit(solution)/shard_map/reduce_scatter | solution.py:281
  1414.6 1924.7 %all-reduce.9.cloned.1.call-start = ((), (), s32[]{:S(2)}) async-start(), calls=%async_computation.24 | async-start | bytes 268435456
  1463.0 2026.2 %reduce-scatter.16.cloned.1.call-start = ((), (), s32[]{:S(2)}) async-start(), calls=%async_computation.21 | async-start | bytes 4325376 | tf_op jit(solution)/shard_map/reduce_scatter | solution.py:317
  1468.8 2170.0 %reduce-scatter.14.cloned.1.call-start = ((), (), s32[]{:S(2)}) async-start(), calls=%async_computation.20 | async-start | bytes 4325376 | tf_op jit(solution)/shard_map/reduce_scatter | solution.py:314
  1472.9 2531.5 %reduce-scatter.18.cloned.1.call-start = ((), (), s32[]{:S(2)}) async-start(), calls=%async_computation.22 | async-start | bytes 17301504 | tf_op jit(solution)/shard_map/reduce_scatter | solution.py:324
  1482.4 2886.9 %reduce-scatter.12.cloned.1.call-start = ((), (), s32[]{:S(2)}) async-start(), calls=%async_computation.19 | async-start | bytes 17301504 | tf_op jit(solution)/shard_map/reduce_scatter | solution.py:311
  1501.6 4279.0 %reduce-scatter.20.cloned.1.call-start = ((), (), s32[]{:S(2)}) async-start(), calls=%async_computation.23 | async-start | bytes 69206016 | tf_op jit(solution)/shard_map/reduce_scatter | solution.py:237
  (27 other events, 580.2 us)
Sparse Core Ops, SparseCore 0:
  11.5 59.2 all-gather.10
  74.4 55.3 all-gather.14
  131.9 26.7 all-gather.12
  162.1 76.8 all-gather.18
  241.0 28.7 all-gather.16
  273.1 75.6 all-gather.20
  352.4 193.3 all-gather.26
  549.3 192.9 all-gather.24
  745.2 192.9 all-gather.22
  941.6 354.3 all-gather.28
  1350.7 25.3 reduce-scatter.9
  1414.7 25.3 reduce-scatter.7
  1463.2 1876.0 all-reduce.8
  3342.0 147.2 reduce-scatter.15
  3492.0 146.7 reduce-scatter.13
  3641.5 362.7 reduce-scatter.17
  4007.0 362.1 reduce-scatter.11
  4372.0 1408.5 reduce-scatter.19
where the time goes:
time: 5790 us
  waiting for transfers between devices  5250 us (91%)
  matrix products  339 us (6%)
  blocking collectives  82.5 us (1%)
  other arithmetic  80.6 us (1%)
    unnamed x19, waiting for transfers between devices  1780 us
    reduce_scatter x1, waiting for transfers between devices, per_device(): lax.psum_scatter(matmul_left_t(active, cotangent), ('dp', 'ctx'), scatter...  1410 us
    reduce_scatter x1, waiting for transfers between devices, per_device(): lax.psum_scatter(output_term, ('dp', 'ctx'), scatter_dimension=0, tiled=T...  366 us
    reduce_scatter x1, waiting for transfers between devices, per_device(): lax.psum_scatter(matmul_left_t(first_hidden, grad_query), ('dp', 'ctx'),...  365 us
    all_gather x1, waiting for transfers between devices, per_device(): lax.all_gather(stacked_low, ('dp', 'ctx'), axis=1, tiled=True)  328 us
    all_gather x1, waiting for transfers between devices, per_device(): lax.all_gather(down_low, ('dp', 'ctx'), axis=0, tiled=True)  190 us
    all_gather x1, waiting for transfers between devices, per_device(): lax.all_gather(gate_low, ('dp', 'ctx'), axis=0, tiled=True)  178 us
    all_gather x1, waiting for transfers between devices, per_device(): lax.all_gather(up_low, ('dp', 'ctx'), axis=0, tiled=True)  177 us
  transfers between devices with their start and end apart: 18, of which 16 were waited for; matrix products, arithmetic and copies ran while one was open for 6% of the time, Pallas kernels for 0%

commit v1 on v0

v1 whole, which is shorter than its diff:
```python
import math

import jax
import jax.numpy as jnp
from jax import lax
from jax.sharding import Mesh
from jax.sharding import PartitionSpec as P

HEAD_DIM = 64
EPSILON = 1e-05
ROPE_BASE = 500000.0
MASKED_SCORE = -1e30
LANES = 128

LOW = jnp.bfloat16
WIDE = jnp.float32


def matmul(left, right):
    return jnp.dot(left, right, preferred_element_type=WIDE)


def matmul_left_t(left, right):
    return lax.dot_general(left, right, (((0,), (0,)), ((), ())), preferred_element_type=WIDE)


def matmul_right_t(left, right):
    return lax.dot_general(left, right, (((1,), (1,)), ((), ())), preferred_element_type=WIDE)


def inverse_root(values):
    return lax.rsqrt(jnp.mean(values * values, axis=-1, keepdims=True) + EPSILON)


def norm_back(values, grad_normed):
    scaled = inverse_root(values)
    unit_rows = values * scaled
    return scaled * (
        grad_normed - unit_rows * jnp.mean(grad_normed * unit_rows, axis=-1, keepdims=True)
    )


def turn(values, cosine, sine):
    half_dim = values.shape[-1] // 2
    first_half = values[..., :half_dim]
    second_half = values[..., half_dim:]
    return jnp.concatenate(
        [
            first_half * cosine - second_half * sine,
            second_half * cosine + first_half * sine,
        ],
        -1,
    )


def after(values, *earlier):
    return lax.optimization_barrier((values, *earlier))[0]


def shift(values, count, step, senders):
    pairs = [(i, i + step) for i in senders if 0 <= i + step < count]
    return lax.ppermute(values, "ctx", pairs)


def rotate(values, count, step):
    return lax.ppermute(values, "ctx", [(i, (i + step) % count) for i in range(count)])


def line_gather(own, count, me):
    up, down = [own], [own]
    for s in range(1, count):
        up.append(shift(up[-1], count, 1, range(s - 1, count)))
        down.append(shift(down[-1], count, -1, range(0, count - s + 1)))
    return [own] + [jnp.where(me >= r, up[r], down[count - r]) for r in range(1, count)]


def line_gather_up(own, count):
    slots = [own]
    for s in range(1, count):
        slots.append(shift(slots[-1], count, 1, range(s - 1, count)))
    return slots


def line_scatter(slots, count):
    up = down = None
    for s in range(1, count):
        up_now = slots[s]
        down_now = slots[count - s]
        if up is not None:
            up_now = up_now + up.astype(WIDE)
            down_now = down_now + down.astype(WIDE)
        up = shift(up_now.astype(LOW), count, 1, range(0, s))
        down = shift(down_now.astype(LOW), count, -1, range(count - s, count))
    return slots[0] + up.astype(WIDE) + down.astype(WIDE)


def line_scatter_down(slots, count):
    down = None
    for s in range(1, count):
        down_now = slots[count - s]
        if down is not None:
            down_now = down_now + down.astype(WIDE)
        down = shift(down_now.astype(LOW), count, -1, range(count - s, count))
    return slots[0] + down.astype(WIDE)


def in_order(slots, count, me):
    out = jnp.zeros((count, *slots[0].shape), slots[0].dtype)
    for r in range(count):
        out = lax.dynamic_update_index_in_dim(out, slots[r], lax.rem(me - r + count, count), 0)
    return out


def per_device(
    inputs,
    cotangent,
    segment_ids,
    real_entry_flags,
    attention_gain,
    feedforward_gain,
    query_weight,
    key_weight,
    value_weight,
    output_weight,
    gate_weight,
    up_weight,
    down_weight,
):
    chips = ("y", "x")
    planes = ("y", "x", "core")
    n_ctx = lax.axis_size("ctx")
    n_chips = lax.axis_size(chips)
    n_core = lax.axis_size("core")
    n_dp = n_chips * n_core
    me = lax.axis_index("ctx")
    core = lax.axis_index("core")
    entry_count, width = inputs.shape
    head_dim = HEAD_DIM
    query_width = query_weight.shape[1]
    pair_width = key_weight.shape[1]
    pair_heads = pair_width // head_dim
    query_heads = query_width // head_dim
    group_size = query_heads // pair_heads
    score_scale = head_dim ** (-0.5)
    hidden_units = gate_weight.shape[1]
    rows = gate_weight.shape[0]
    hidden_rows = down_weight.shape[0]
    hidden_chunk = hidden_units // n_ctx
    attention_width = query_width + 2 * pair_width

    def ctx_rows_gather(values):
        slots = [values] + [rotate(values, n_ctx, r) for r in range(1, n_ctx)]
        return in_order(slots, n_ctx, me).reshape(n_ctx * rows, -1)

    def plane_gather(values):
        return lax.all_gather(values, planes, axis=0, tiled=True)

    def plane_scatter(values):
        parts = values.reshape(n_chips, n_core, -1, values.shape[1])
        kept = lax.dynamic_index_in_dim(parts, core, 1, keepdims=False)
        if n_core == 2:
            sent = lax.dynamic_index_in_dim(parts, 1 - core, 1, keepdims=False).astype(LOW)
            came = lax.ppermute(sent, "core", [(0, 1), (1, 0)])
            kept = (kept.astype(WIDE) + came.astype(WIDE)).astype(LOW)
        return lax.psum_scatter(
            kept.reshape(-1, values.shape[1]), chips, scatter_dimension=0, tiled=True
        )

    gains = jnp.stack([attention_gain, feedforward_gain], 1)
    gains = jnp.pad(gains, ((0, 0), (0, LANES - 2)))
    first_low = jnp.concatenate([query_weight, key_weight, value_weight, gains], 1).astype(LOW)
    first_rows = ctx_rows_gather(first_low)
    first_full = plane_gather(first_rows)

    both = jnp.stack([gate_weight, up_weight], 1).astype(LOW)
    both = both.reshape(rows, 2, n_dp, n_ctx, hidden_rows)
    both = after(both, first_rows)

    def chunk_for(place):
        part = lax.dynamic_index_in_dim(both, place, 3, keepdims=False)
        return part.reshape(rows, 2 * hidden_chunk)

    both_slots = [chunk_for(me)] + [
        rotate(chunk_for(lax.rem(me + r, n_ctx)), n_ctx, r) for r in range(1, n_ctx)
    ]
    both_rows = in_order(both_slots, n_ctx, me).reshape(n_ctx * rows, 2 * hidden_chunk)

    output_rows = ctx_rows_gather(after(output_weight.astype(LOW), both_rows))
    output_full = plane_gather(output_rows)
    both_full = plane_gather(both_rows)
    down_full = plane_gather(after(down_weight.astype(LOW), both_rows))

    query_full = first_full[:, :query_width]
    key_full = first_full[:, query_width : query_width + pair_width]
    value_full = first_full[:, query_width + pair_width : attention_width]
    gain_first = first_full[:, attention_width].astype(WIDE)
    gain_second = first_full[:, attention_width + 1].astype(WIDE)

    spans = segment_ids[0]
    reality = real_entry_flags[0]
    opening = me * entry_count
    places = opening + jnp.arange(entry_count, dtype=jnp.int32)
    own_spans = lax.dynamic_slice_in_dim(spans, opening, entry_count)
    doc_starts = jnp.sum((spans[None, :] < own_spans[:, None]).astype(jnp.int32), axis=1)
    offsets = (places - doc_starts).astype(WIDE)
    half_dim = head_dim // 2
    frequency = ROPE_BASE ** (-(jnp.arange(half_dim, dtype=WIDE) * 2.0 / head_dim))
    angle = offsets[:, None, None] * frequency[None, None, :]
    cosine, sine = jnp.cos(angle), jnp.sin(angle)
    key_places, key_spans, key_reality = [], [], []
    for r in range(n_ctx):
        start = (me - r) * entry_count
        key_places.append(start + jnp.arange(entry_count, dtype=jnp.int32))
        start = jnp.maximum(start, 0)
        key_spans.append(lax.dynamic_slice_in_dim(spans, start, entry_count))
        key_reality.append(lax.dynamic_slice_in_dim(reality, start, entry_count))
    key_places = jnp.concatenate(key_places)
    key_spans = jnp.concatenate(key_spans)
    key_reality = jnp.concatenate(key_reality)
    allowed = (
        (own_spans[:, None] == key_spans[None, :])
        & (key_places[None, :] <= places[:, None])
        & (key_places[None, :] >= 0)
        & (key_reality[None, :] == 1)
    ) | (key_places[None, :] == places[:, None])

    tokens_wide = inputs.astype(WIDE)
    unit_first = tokens_wide * inverse_root(tokens_wide)
    first_hidden = (unit_first * gain_first).astype(LOW)
    keys_own = turn(
        matmul(first_hidden, key_full).reshape(entry_count, pair_heads, head_dim), cosine, sine
    )
    values_own = matmul(first_hidden, value_full)
    pair_own = jnp.concatenate(
        [keys_own.reshape(entry_count, pair_width).astype(LOW), values_own.astype(LOW)], 1
    )
    pair_slots = line_gather_up(pair_own, n_ctx)
    pair_all = jnp.concatenate(pair_slots, 0)
    seq_length = pair_all.shape[0]
    keys = pair_all[:, :pair_width].reshape(seq_length, pair_heads, head_dim)
    values = pair_all[:, pair_width:].reshape(seq_length, pair_heads, head_dim)
    queries = (
        turn(
            matmul(first_hidden, query_full).reshape(entry_count, query_heads, head_dim),
            cosine,
            sine,
        )
        .astype(LOW)
        .reshape(entry_count, pair_heads, group_size, head_dim)
    )

    def scores_of():
        raw = jnp.einsum("ikgd,jkd->kgij", queries, keys, preferred_element_type=WIDE)
        return jnp.where(allowed[None, None], raw * score_scale, MASKED_SCORE)

    scores = scores_of()
    row_top = jnp.max(scores, axis=-1, keepdims=True)
    exponent = jnp.exp(scores - row_top)
    row_total = jnp.sum(exponent, axis=-1, keepdims=True)
    log_total = row_top + jnp.log(row_total)
    probs_low = (exponent / row_total).astype(LOW)
    attended = (
        jnp.einsum("kgij,jkd->ikgd", probs_low, values, preferred_element_type=WIDE)
        .reshape(entry_count, query_width)
        .astype(LOW)
    )

    residual = tokens_wide + matmul(attended, output_full)
    unit_second = residual * inverse_root(residual)
    second_hidden = (unit_second * gain_second).astype(LOW)
    cot_slots = line_gather(after(cotangent, output_rows, pair_all), n_ctx, me)
    cot_all = jnp.concatenate(cot_slots, 0)
    hidden_all = jnp.concatenate(line_gather(second_hidden, n_ctx, me), 0)
    grad_active = matmul_right_t(cot_all, down_full)
    gate_value = matmul(hidden_all, both_full[:, :hidden_chunk])
    up_value = matmul(hidden_all, both_full[:, hidden_chunk:])
    sigmoid_gate = jax.nn.sigmoid(gate_value)
    active = (gate_value * sigmoid_gate * up_value).astype(LOW)
    grad_gate = (
        grad_active * up_value * sigmoid_gate * (1.0 + gate_value * (1.0 - sigmoid_gate))
    ).astype(LOW)
    grad_up = (grad_active * gate_value * sigmoid_gate).astype(LOW)
    grad_both = jnp.concatenate([grad_gate, grad_up], 1)

    second_parts = matmul_right_t(grad_both, both_full)
    grad_second = line_scatter(
        [second_parts[r * entry_count : (r + 1) * entry_count] for r in range(n_ctx)], n_ctx
    )
    down_parts = matmul(after(active, grad_second), down_full)
    down_value = line_scatter(
        [down_parts[r * entry_count : (r + 1) * entry_count] for r in range(n_ctx)], n_ctx
    )
    block_output = (residual + down_value).astype(LOW)

    down_weight_grad = plane_scatter(matmul_left_t(active, cot_all).astype(LOW)).astype(WIDE)
    both_grad_rows = plane_scatter(matmul_left_t(hidden_all, grad_both).astype(LOW))
    both_grad_parts = both_grad_rows.reshape(n_ctx, rows, 2 * hidden_chunk)
    part_for = lambda place: lax.dynamic_index_in_dim(both_grad_parts, place, 0, keepdims=False)
    grad_slots = [part_for(me)] + [
        rotate(part_for(lax.rem(me + r, n_ctx)), n_ctx, r) for r in range(1, n_ctx)
    ]
    both_grad = in_order(grad_slots, n_ctx, me).reshape(n_ctx, rows, 2, n_dp, hidden_rows)
    both_grad = both_grad.transpose(2, 1, 3, 0, 4).reshape(2, rows, hidden_units).astype(WIDE)
    gate_weight_grad, up_weight_grad = both_grad[0], both_grad[1]

    second_gain_term = jnp.sum(grad_second * unit_second, axis=0)
    grad_residual = cotangent.astype(WIDE) + norm_back(residual, grad_second * gain_second)
    grad_branch = grad_residual.astype(LOW)
    grad_attended = (
        matmul_right_t(grad_branch, output_full)
        .astype(LOW)
        .reshape(entry_count, pair_heads, group_size, head_dim)
    )
    probs = jnp.exp(scores_of() - log_total)
    grad_probs = jnp.einsum("ikgd,jkd->kgij", grad_attended, values, preferred_element_type=WIDE)
    row_delta = jnp.sum(probs * grad_probs, axis=-1, keepdims=True)
    grad_scores = (probs * (grad_probs - row_delta)).astype(LOW)
    key_part = (
        jnp.einsum("kgij,ikgd->jkd", grad_scores, queries, preferred_element_type=WIDE)
        * score_scale
    ).reshape(seq_length, pair_width)
    value_part = jnp.einsum(
        "kgij,ikgd->jkd", probs_low, grad_attended, preferred_element_type=WIDE
    ).reshape(seq_length, pair_width)
    pair_part = jnp.concatenate([key_part, value_part], 1)
    pair_grad = line_scatter_down(
        [pair_part[r * entry_count : (r + 1) * entry_count] for r in range(n_ctx)], n_ctx
    )
    grad_queries_rot = (
        jnp.einsum("kgij,jkd->ikgd", grad_scores, keys, preferred_element_type=WIDE) * score_scale
    )
    grad_query = (
        turn(grad_queries_rot.reshape(entry_count, query_heads, head_dim), cosine, -sine)
        .astype(LOW)
        .reshape(entry_count, query_width)
    )
    grad_key = (
        turn(
            pair_grad[:, :pair_width].reshape(entry_count, pair_heads, head_dim), cosine, -sine
        )
        .astype(LOW)
        .reshape(entry_count, pair_width)
    )
    grad_value = pair_grad[:, pair_width:].astype(LOW)
    grad_qkv = jnp.concatenate([grad_query, grad_key, grad_value], 1)
    grad_first = matmul_right_t(grad_qkv, first_full[:, :attention_width])
    first_gain_term = jnp.sum(grad_first * unit_first, axis=0)
    input_grad = (grad_residual + norm_back(tokens_wide, grad_first * gain_first)).astype(LOW)

    def ctx_rows_scatter(values):
        parts = values.reshape(n_ctx, rows, values.shape[1])
        get = lambda place: lax.dynamic_index_in_dim(parts, place, 0, keepdims=False)
        total = get(me).astype(WIDE)
        for r in range(1, n_ctx):
            total = total + rotate(get(lax.rem(me + r, n_ctx)), n_ctx, r).astype(WIDE)
        return total

    output_weight_grad = ctx_rows_scatter(
        plane_scatter(matmul_left_t(attended, grad_branch).astype(LOW))
    )
    gain_terms = jnp.pad(
        jnp.stack([first_gain_term, second_gain_term], 1), ((0, 0), (0, LANES - 2))
    )
    first_grad = ctx_rows_scatter(
        plane_scatter(
            jnp.concatenate([matmul_left_t(first_hidden, grad_qkv), gain_terms], 1).astype(LOW)
        )
    )
    return (
        block_output,
        input_grad,
        first_grad[:, attention_width],
        first_grad[:, attention_width + 1],
        first_grad[:, :query_width],
        first_grad[:, query_width : query_width + pair_width],
        first_grad[:, query_width + pair_width : attention_width],
        output_weight_grad,
        gate_weight_grad,
        up_weight_grad,
        down_weight_grad,
    )


def solution(mesh):
    n_dp, n_ctx = mesh.shape["dp"], mesh.shape["ctx"]
    n_core = 2 if n_dp % 2 == 0 else 1
    n_chips = n_dp // n_core
    n_y = math.isqrt(n_chips)
    while n_chips % n_y:
        n_y -= 1
    axes = ("y", "x", "core", "ctx")
    fine = Mesh(mesh.devices.reshape(n_y, n_chips // n_y, n_core, n_ctx), axes)
    matrix = P(axes, None)
    vector = P(axes)
    per_sequence = P(("y", "x", "core"), None)
    return jax.shard_map(
        per_device,
        mesh=fine,
        in_specs=(matrix, matrix, per_sequence, per_sequence, vector, vector) + (matrix,) * 7,
        out_specs=(matrix, matrix, vector, vector) + (matrix,) * 7,
        check_vma=False,
    )
```

time: 5790 us -> 1040 us (0.18)
  waiting for transfers between devices: 5250 us -> 416 us
  starting transfers between devices: 1.39 us -> 128 us
  matrix products: 339 us -> 244 us
  blocking collectives: 82.5 us -> 0 us
  other arithmetic: 80.6 us -> 157 us
    reduce_scatter x7 -> x4, waiting for transfers between devices: 2390 us -> 2.56 us  [plane_scatter(): lax.psum_scatter(kept.reshape(-1, values.shape[1]), chips, scatter_dimens...]
    unnamed x19 -> x8, waiting for transfers between devices: 1780 us -> 0.64 us
    all_gather x10 -> x4, waiting for transfers between devices: 1080 us -> 0.01 us  [plane_gather(): return lax.all_gather(values, planes, axis=0, tiled=True)]
    ppermute x0 -> x52, waiting for transfers between devices: none -> 413 us  [the longest x30 265 us: shift(): return lax.ppermute(values, 'ctx', pairs)]
    ppermute x0 -> x52, starting transfers between devices: none -> 127 us  [the longest x30 82.6 us: shift(): return lax.ppermute(values, 'ctx', pairs)]
    unnamed x2 -> x0, blocking collectives: 82.5 us -> none
    dot_general x6 -> x4, matrix products: 102 us -> 42.3 us  [matmul_left_t(): lax.dot_general(left, right, (((0,), (0,)), ((), ())), preferred_element_...]
  transfers between devices with their start and end apart: 18 -> 60, of which waited for: 16 -> 29; matrix products, arithmetic and copies ran while one was open for 6% -> 35% of each run, Pallas kernels for 0% -> 0%
where the time goes in v1:
time: 1040 us
  waiting for transfers between devices  416 us (40%)
  matrix products  244 us (23%)
  other arithmetic  157 us (15%)
  starting transfers between devices  128 us (12%)
  local copies, waits for them, and re-layouts  74.3 us (7%)
  between operations  15.8 us (2%)
    ppermute x30, waiting for transfers between devices, shift(): return lax.ppermute(values, 'ctx', pairs)  265 us
    ppermute x18, waiting for transfers between devices, rotate(): lax.ppermute(values, 'ctx', [(i, (i + step) % count) for i in range(count)])  132 us
    ppermute x30, starting transfers between devices, shift(): return lax.ppermute(values, 'ctx', pairs)  82.6 us
    dot_general x7, matrix products, matmul(): return jnp.dot(left, right, preferred_element_type=WIDE)  68.4 us
    dot_general x4, matrix products, matmul_right_t(): lax.dot_general(left, right, (((1,), (1,)), ((), ())), preferred_element_...  52.8 us
    ppermute x18, starting transfers between devices, rotate(): lax.ppermute(values, 'ctx', [(i, (i + step) % count) for i in range(count)])  44 us
    dot_general x4, matrix products, matmul_left_t(): lax.dot_general(left, right, (((0,), (0,)), ((), ())), preferred_element_...  42.3 us
    convert_element_type x4, other arithmetic, plane_scatter(): kept = (kept.astype(WIDE) + came.astype(WIDE)).astype(LOW)  35.9 us
  transfers between devices with their start and end apart: 60, of which 29 were waited for; matrix products, arithmetic and copies ran while one was open for 35% of the time, Pallas kernels for 0%

profile of v1, /device:TPU:0, one launch (start us, length us, event | category | flops | bytes accessed | tf_op | source)
XLA Modules:
  0.0 1035.1 jit_solution(13716916809203994520)
XLA Ops:
  26.5 16.7 %collective-permute-done.1 = bf16[64,3200]{1,0:T(8,128)(2,1)S(1)} collective-permute-done((bf16[64,3200]{1,0:T(8,128)(2,1)S(1)}, bf16[64,3200]{1,0:T(8,128)(2,1)S(1)}, u32[]{:S(2)}, u32[]{:S(2)}) %collective-permute-start.1) | collective-permute-done | bytes 409632 | tf_op jit(solution)/shard_map/ppermute | solution.py:66
  75.0 19.6 %collective-permute-done.7 = bf16[64,4096]{1,0:T(8,128)(2,1)} collective-permute-done((bf16[64,4096]{1,0:T(8,128)(2,1)}, bf16[64,4096]{1,0:T(8,128)(2,1)}, u32[]{:S(2)}, u32[]{:S(2)}) %collective-permute-start.7) | collective-permute-done | bytes 524320 | tf_op jit(solution)/shard_map/ppermute | solution.py:66
  171.8 16.6 %collective-permute-start.18 = (bf16[256,2048]{1,0:T(8,128)(2,1)}, bf16[256,2048]{1,0:T(8,128)(2,1)}, u32[]{:S(2)}, u32[]{:S(2)}) collective-permute-start(bf16[256,2048]{1,0:T(8,128)(2,1)} %param.14), channel_id=1, source_target_pairs={{0,1},{1,2},{2,3},{4,5},{5,6},{6,7},{8,9},{9,10},{10,11},{12,13},{... | collective-permute-start | bytes 3145736 | tf_op jit(solution)/shard_map/ppermute | solution.py:62
  208.4 16.2 %fusion.3 = f32[8,4,256]{2,1,0:T(4,128)S(1)} fusion(f32[8,1024,256,4]{2,1,3,0:T(8,128)} %get-tuple-element.86, f32[8,4,256]{2,1,0:T(4,128)S(1)} %get-tuple-element.85, pred[256,1024]{0,1:T(8,128)(4,1)S(1)} %compare_or_fusion), kind=kLoop, calls=%fused_computation.9 | loop fusion | flops 33546240 | bytes 33882112 | tf_op jit(solution)/shard_map/reduce_sum | solution.py:259
  270.6 15.3 %collective-permute-done.12 = bf16[256,2048]{1,0:T(8,128)(2,1)} collective-permute-done((bf16[256,2048]{1,0:T(8,128)(2,1)S(1)}, bf16[256,2048]{1,0:T(8,128)(2,1)}, u32[]{:S(2)}, u32[]{:S(2)}) %collective-permute-start.12) | collective-permute-done | bytes 1048608 | tf_op jit(solution)/shard_map/ppermute | solution.py:62
  296.5 20.4 %collective-permute-done.20 = bf16[256,2048]{1,0:T(8,128)(2,1)} collective-permute-done((bf16[256,2048]{1,0:T(8,128)(2,1)}, bf16[256,2048]{1,0:T(8,128)(2,1)}, u32[]{:S(2)}, u32[]{:S(2)}) %collective-permute-start.20) | collective-permute-done | bytes 1048608 | tf_op jit(solution)/shard_map/ppermute | solution.py:62
  318.9 20.4 %collective-permute-done.14 = bf16[256,2048]{1,0:T(8,128)(2,1)} collective-permute-done((bf16[256,2048]{1,0:T(8,128)(2,1)}, bf16[256,2048]{1,0:T(8,128)(2,1)}, u32[]{:S(2)}, u32[]{:S(2)}) %collective-permute-start.14) | collective-permute-done | bytes 1048608 | tf_op jit(solution)/shard_map/ppermute | solution.py:62
  362.8 18.1 %collective-permute-done.15 = bf16[256,2048]{1,0:T(8,128)(2,1)S(1)} collective-permute-done((bf16[256,2048]{1,0:T(8,128)(2,1)}, bf16[256,2048]{1,0:T(8,128)(2,1)S(1)}, u32[]{:S(2)}, u32[]{:S(2)}) %collective-permute-start.15) | collective-permute-done | bytes 1048608 | tf_op jit(solution)/shard_map/ppermute | solution.py:62
  396.5 15.8 %fusion.9 = f32[1024,2048]{1,0:T(8,128)} fusion(bf16[2048,4096]{1,0:T(8,128)(2,1)} %all-gather.9.cloned.1.call-done, bf16[256,2048]{1,0:T(8,128)(2,1)} %broadcast_select_fusion.1, bf16[256,2048]{1,0:T(8,128)(2,1)} %broadcast_select_fusion.3, bf16[256,2048]{1,0:T(8,128)(2,1)} %broadcast_select_fusion.5, bf16[256,2048]{1,0:T(8,128)(2,1)S(1)} %multiply_convert_fusion.3), kind=kOutput, calls=%fused_computation.23 | convolution fusion | flops 8606711808 | bytes 20971520 | tf_op jit(solution)/shard_map/dot_general | solution.py:20
  412.3 22.3 %multiply_convert_fusion.1 = (bf16[1024,2048]{1,0:T(8,128)(2,1)}, bf16[1024,2048]{1,0:T(8,128)(2,1)}, bf16[1024,2048]{1,0:T(8,128)(2,1)}) fusion(f32[1024,2048]{1,0:T(8,128)} %fusion.56, f32[1024,2048]{1,0:T(8,128)} %fusion.9, bf16[2048,4096]{1,0:T(8,128)(2,1)} %all-gather.9.cloned.1.call-done, bf16[256,2048]{1,0:T(8,128)(2,1)} %broadcast_select_fusion.1, ...), kind=kOutput, calls=%fused_computation.36 | convolution fusion | flops 8640266240 | bytes 41943040 | tf_op jit(solution)/shard_map/dot_general | solution.py:20
  434.6 21.2 %fusion.21 = f32[1024,2048]{1,0:T(8,128)S(1)} fusion(bf16[2048,4096]{1,0:T(8,128)(2,1)} %all-gather.9.cloned.1.call-done, bf16[1024,2048]{1,0:T(8,128)(2,1)} %get-tuple-element.32, bf16[1024,2048]{1,0:T(8,128)(2,1)} %get-tuple-element.30), kind=kOutput, calls=%fused_computation.51 | convolution fusion | flops 17196646400 | bytes 33554432 | tf_op jit(solution)/shard_map/dot_general | solution.py:28
  459.7 18.5 %collective-permute-done.24 = bf16[256,2048]{1,0:T(8,128)(2,1)S(1)} collective-permute-done((bf16[256,2048]{1,0:T(8,128)(2,1)S(1)}, bf16[256,2048]{1,0:T(8,128)(2,1)S(1)}, u32[]{:S(2)}, u32[]{:S(2)}) %collective-permute-start.24) | collective-permute-done | bytes 1048608 | tf_op jit(solution)/shard_map/ppermute | solution.py:62
  483.0 18.3 %collective-permute-done.25 = bf16[256,2048]{1,0:T(8,128)(2,1)S(1)} collective-permute-done((bf16[256,2048]{1,0:T(8,128)(2,1)S(1)}, bf16[256,2048]{1,0:T(8,128)(2,1)S(1)}, u32[]{:S(2)}, u32[]{:S(2)}) %collective-permute-start.25) | collective-permute-done | bytes 1048608 | tf_op jit(solution)/shard_map/ppermute | solution.py:62
  510.2 15.4 %collective-permute-done.26 = bf16[256,2048]{1,0:T(8,128)(2,1)S(1)} collective-permute-done((bf16[256,2048]{1,0:T(8,128)(2,1)S(1)}, bf16[256,2048]{1,0:T(8,128)(2,1)S(1)}, u32[]{:S(2)}, u32[]{:S(2)}) %collective-permute-start.26) | collective-permute-done | bytes 1048608 | tf_op jit(solution)/shard_map/ppermute | solution.py:62
  525.7 20.4 %collective-permute-done.29 = bf16[256,2048]{1,0:T(8,128)(2,1)S(1)} collective-permute-done((bf16[256,2048]{1,0:T(8,128)(2,1)S(1)}, bf16[256,2048]{1,0:T(8,128)(2,1)S(1)}, u32[]{:S(2)}, u32[]{:S(2)}) %collective-permute-start.29) | collective-permute-done | bytes 1048608 | tf_op jit(solution)/shard_map/ppermute | solution.py:62
  565.5 17.8 %collective-permute-done.30 = bf16[256,2048]{1,0:T(8,128)(2,1)S(1)} collective-permute-done((bf16[256,2048]{1,0:T(8,128)(2,1)S(1)}, bf16[256,2048]{1,0:T(8,128)(2,1)S(1)}, u32[]{:S(2)}, u32[]{:S(2)}) %collective-permute-start.30) | collective-permute-done | bytes 1048608 | tf_op jit(solution)/shard_map/ppermute | solution.py:62
  588.1 15.6 %collective-permute-done.31 = bf16[256,2048]{1,0:T(8,128)(2,1)S(1)} collective-permute-done((bf16[256,2048]{1,0:T(8,128)(2,1)S(1)}, bf16[256,2048]{1,0:T(8,128)(2,1)S(1)}, u32[]{:S(2)}, u32[]{:S(2)}) %collective-permute-start.31) | collective-permute-done | bytes 1048608 | tf_op jit(solution)/shard_map/ppermute | solution.py:62
  625.5 20.6 %collective-permute-done.35 = bf16[256,2048]{1,0:T(8,128)(2,1)} collective-permute-done((bf16[256,2048]{1,0:T(8,128)(2,1)}, bf16[256,2048]{1,0:T(8,128)(2,1)}, u32[]{:S(2)}, u32[]{:S(2)}) %collective-permute-start.35) | collective-permute-done | bytes 1048608 | tf_op jit(solution)/shard_map/ppermute | solution.py:62
  661.4 20.6 %convolution_convert_fusion = bf16[2048,4096]{1,0:T(8,128)(2,1)} fusion(bf16[1024,2048]{1,0:T(8,128)(2,1)S(1)} %copy-done.48, bf16[1024,2048]{1,0:T(8,128)(2,1)S(1)} %copy-done.47, bf16[256,2048]{1,0:T(8,128)(2,1)S(1)} %copy-done.28, bf16[256,2048]{1,0:T(8,128)(2,1)S(1)} %copy-done.27, bf16[256,2048]{1,0:T(8,128)(2,1)S(1)} %copy-done.29, ...), kind=kOutput, calls=%fused_computation.15 | convolution fusion | flops 17221812224 | bytes 29360128 | tf_op jit(solution)/shard_map/dot_general | solution.py:24
  741.2 23.5 %fusion = (f32[8,4,256]{2,1,0:T(4,128)S(1)}, f32[8,1024,256,4]{2,1,3,0:T(8,128)}) fusion(f32[8,1024,256,4]{2,1,3,0:T(8,128)} %get-tuple-element.86, f32[8,4,256]{2,1,0:T(4,128)S(1)} %bitcast.262, pred[256,1024]{0,1:T(8,128)(4,1)S(1)} %copy-done.5, bf16[1024,8,64,1]{0,2,3,1:T(8,128)(2,1)S(1)} %bitcast.236, bf16[256,8,4,64]{0,3,2,1:T(8,128)(2,1)S(1)} %bitcast.233), kind=kOutput, calls=%fused_computation.2 | convolution fusion | flops 1115676672 | bytes 69533696 | tf_op jit(solution)/shard_map/ikgd,jkd->kgij/dot_general | solution.py:315
  764.7 30.8 %fusion.2 = bf16[8,4,256,1024]{2,3,1,0:T(8,128)(2,1)} fusion(f32[8,1024,256,4]{2,1,3,0:T(8,128)} %get-tuple-element.90, f32[8,1024,256,4]{2,1,3,0:T(8,128)} %get-tuple-element.86, f32[8,4,256]{2,1,0:T(4,128)S(1)} %get-tuple-element.89, f32[8,4,256]{2,1,0:T(4,128)S(1)} %bitcast.263, pred[256,1024]{0,1:T(8,128)(4,1)S(1)} %copy-done.5), kind=kLoop, calls=%fused_computation.4 | loop fusion | flops 50331648 | bytes 84213760 | tf_op jit(solution)/shard_map/convert_element_type | solution.py:317
  844.9 22.9 %collective-permute-done.38 = bf16[256,1024]{0,1:T(8,128)(2,1)S(1)} collective-permute-done((bf16[256,1024]{0,1:T(8,128)(2,1)S(1)}, bf16[256,1024]{0,1:T(8,128)(2,1)S(1)}, u32[]{:S(2)}, u32[]{:S(2)}) %collective-permute-start.38) | collective-permute-done | bytes 524320 | tf_op jit(solution)/shard_map/ppermute | solution.py:62
  927.7 33.8 %collective-permute-done.45 = bf16[64,2048]{1,0:T(8,128)(2,1)} collective-permute-done((bf16[64,2048]{1,0:T(8,128)(2,1)}, bf16[64,2048]{1,0:T(8,128)(2,1)}, u32[]{:S(2)}, u32[]{:S(2)}) %collective-permute-start.45) | collective-permute-done | bytes 262176 | tf_op jit(solution)/shard_map/ppermute | solution.py:66
  1002.5 21.8 %collective-permute-done.41 = bf16[64,3200]{1,0:T(8,128)(2,1)} collective-permute-done((bf16[64,3200]{1,0:T(8,128)(2,1)S(1)}, bf16[64,3200]{1,0:T(8,128)(2,1)}, u32[]{:S(2)}, u32[]{:S(2)}) %collective-permute-start.41) | collective-permute-done | bytes 409632 | tf_op jit(solution)/shard_map/ppermute | solution.py:66
  (360 shorter events, 536.6 us)
Async XLA Ops:
  7.2 125.8 %all-gather.5.cloned.1.call-start = ((), (), s32[]{:S(2)}) async-start(), calls=%async_computation.4 | async-start | bytes 14745600 | tf_op jit(solution)/shard_map/all_gather | solution.py:156
  44.5 206.4 %all-gather.7.cloned.1.call-start = ((), (), s32[]{:S(2)}) async-start(), calls=%async_computation.5 | async-start | bytes 9437184 | tf_op jit(solution)/shard_map/all_gather | solution.py:156
  128.0 254.0 %all-gather.11.cloned.1.call-start = ((), (), s32[]{:S(2)}) async-start(), calls=%async_computation.7 | async-start | bytes 9437184 | tf_op jit(solution)/shard_map/all_gather | solution.py:156
  130.8 265.6 %all-gather.9.cloned.1.call-start = ((), (), s32[]{:S(2)}) async-start(), calls=%async_computation.6 | async-start | bytes 18874368 | tf_op jit(solution)/shard_map/all_gather | solution.py:156
  131.4 778.8 %reduce-scatter.7.cloned.1.call-start = ((), (), s32[]{:S(2)}) async-start(), calls=%async_computation.9 | async-start | bytes 5242880 | tf_op jit(solution)/shard_map/reduce_scatter | solution.py:165
  171.8 95.9 %collective-permute-start.18 = (bf16[256,2048]{1,0:T(8,128)(2,1)}, bf16[256,2048]{1,0:T(8,128)(2,1)}, u32[]{:S(2)}, u32[]{:S(2)}) collective-permute-start(bf16[256,2048]{1,0:T(8,128)(2,1)} %param.14), channel_id=1, source_target_pairs={{0,1},{1,2},{2,3},{4,5},{5,6},{6,7},{8,9},{9,10},{10,11},{12,13},{... | collective-permute-start | bytes 3145736 | tf_op jit(solution)/shard_map/ppermute | solution.py:62
  188.4 80.9 %collective-permute-start.19 = (bf16[256,2048]{1,0:T(8,128)(2,1)}, bf16[256,2048]{1,0:T(8,128)(2,1)}, u32[]{:S(2)}, u32[]{:S(2)}) collective-permute-start(bf16[256,2048]{1,0:T(8,128)(2,1)} %param.14), channel_id=1, source_target_pairs={{1,0},{2,1},{3,2},{5,4},{6,5},{7,6},{9,8},{10,9},{11,10},{13,12},{... | collective-permute-start | bytes 3145736 | tf_op jit(solution)/shard_map/ppermute | solution.py:62
  269.3 47.6 %collective-permute-start.20 = (bf16[256,2048]{1,0:T(8,128)(2,1)}, bf16[256,2048]{1,0:T(8,128)(2,1)}, u32[]{:S(2)}, u32[]{:S(2)}) collective-permute-start(bf16[256,2048]{1,0:T(8,128)(2,1)} %collective-permute-done.19), channel_id=1, source_target_pairs={{1,0},{2,1},{5,4},{6,5},{9,8},{10,9},{13,12},{14,13},{17,16},{18,1... | collective-permute-start | bytes 3145736 | tf_op jit(solution)/shard_map/ppermute | solution.py:62
  294.4 44.9 %collective-permute-start.14 = (bf16[256,2048]{1,0:T(8,128)(2,1)}, bf16[256,2048]{1,0:T(8,128)(2,1)}, u32[]{:S(2)}, u32[]{:S(2)}) collective-permute-start(bf16[256,2048]{1,0:T(8,128)(2,1)} %collective-permute-done.13), channel_id=1, source_target_pairs={{1,0},{2,1},{5,4},{6,5},{9,8},{10,9},{13,12},{14,13},{17,16},{18,1... | collective-permute-start | bytes 3145736 | tf_op jit(solution)/shard_map/ppermute | solution.py:62
  295.7 50.0 %collective-permute-start.23 = (bf16[256,2048]{1,0:T(8,128)(2,1)}, bf16[256,2048]{1,0:T(8,128)(2,1)S(1)}, u32[]{:S(2)}, u32[]{:S(2)}) collective-permute-start(bf16[256,2048]{1,0:T(8,128)(2,1)} %collective-permute-done.22), channel_id=1, source_target_pairs={{2,3},{6,7},{10,11},{14,15},{18,19},{22,23},{26,27},{30,31}} | collective-permute-start | bytes 3145736 | tf_op jit(solution)/shard_map/ppermute | solution.py:62
  316.9 44.8 %collective-permute-start.21 = (bf16[256,2048]{1,0:T(8,128)(2,1)}, bf16[256,2048]{1,0:T(8,128)(2,1)S(1)}, u32[]{:S(2)}, u32[]{:S(2)}) collective-permute-start(bf16[256,2048]{1,0:T(8,128)(2,1)} %collective-permute-done.20), channel_id=1, source_target_pairs={{1,0},{5,4},{9,8},{13,12},{17,16},{21,20},{25,24},{29,28}} | collective-permute-start | bytes 3145736 | tf_op jit(solution)/shard_map/ppermute | solution.py:62
  339.4 41.5 %collective-permute-start.15 = (bf16[256,2048]{1,0:T(8,128)(2,1)}, bf16[256,2048]{1,0:T(8,128)(2,1)S(1)}, u32[]{:S(2)}, u32[]{:S(2)}) collective-permute-start(bf16[256,2048]{1,0:T(8,128)(2,1)} %collective-permute-done.14), channel_id=1, source_target_pairs={{1,0},{5,4},{9,8},{13,12},{17,16},{21,20},{25,24},{29,28}} | collective-permute-start | bytes 3145736 | tf_op jit(solution)/shard_map/ppermute | solution.py:62
  508.5 37.5 %collective-permute-start.29 = (bf16[256,2048]{1,0:T(8,128)(2,1)S(1)}, bf16[256,2048]{1,0:T(8,128)(2,1)S(1)}, u32[]{:S(2)}, u32[]{:S(2)}) collective-permute-start(bf16[256,2048]{1,0:T(8,128)(2,1)S(1)} %add_convert_fusion.4), channel_id=1, source_target_pairs={{1,0},{2,1},{3,2},{5,4},{6,5},{7,6},{9,8},{10,9},{11,10},{13,12},{... | collective-permute-start | bytes 3145736 | tf_op jit(solution)/shard_map/ppermute | solution.py:62
  612.5 33.5 %collective-permute-start.35 = (bf16[256,2048]{1,0:T(8,128)(2,1)}, bf16[256,2048]{1,0:T(8,128)(2,1)}, u32[]{:S(2)}, u32[]{:S(2)}) collective-permute-start(bf16[256,2048]{1,0:T(8,128)(2,1)} %add_convert_fusion), channel_id=1, source_target_pairs={{1,0},{2,1},{3,2},{5,4},{6,5},{7,6},{9,8},{10,9},{11,10},{13,12},{... | collective-permute-start | bytes 3145736 | tf_op jit(solution)/shard_map/ppermute | solution.py:62
  697.6 219.4 %reduce-scatter.9.cloned.1.call-start = ((), (), s32[]{:S(2)}) async-start(), calls=%async_computation.10 | async-start | bytes 10485760 | tf_op jit(solution)/shard_map/reduce_scatter | solution.py:165
  714.3 210.3 %reduce-scatter.11.cloned.1.call-start = ((), (), s32[]{:S(2)}) async-start(), calls=%async_computation.11 | async-start | bytes 5242880 | tf_op jit(solution)/shard_map/reduce_scatter | solution.py:165
  732.1 91.8 %collective-permute-start.51 = (bf16[4,256,2048]{2,1,0:T(8,128)(2,1)}, bf16[4,256,2048]{2,1,0:T(8,128)(2,1)}, u32[]{:S(2)}, u32[]{:S(2)}) collective-permute-start(bf16[4,256,2048]{2,1,0:T(8,128)(2,1)} %dynamic-slice_bitcast_fusion.1), channel_id=1, source_target_pairs={{0,4},{4,0},{1,5},{5,1},{2,6},{6,2},{3,7},{7,3},{8,12},{12,8},{9,1... | collective-permute-start | bytes 12582920 | tf_op jit(solution)/shard_map/ppermute | solution.py:163
  832.0 151.0 %reduce-scatter.5.cloned.1.call-start = ((), (), s32[]{:S(2)}) async-start(), calls=%async_computation.8 | async-start | bytes 8192000 | tf_op jit(solution)/shard_map/reduce_scatter | solution.py:165
  834.1 33.7 %collective-permute-start.38 = (bf16[256,1024]{0,1:T(8,128)(2,1)S(1)}, bf16[256,1024]{0,1:T(8,128)(2,1)S(1)}, u32[]{:S(2)}, u32[]{:S(2)}) collective-permute-start(bf16[256,1024]{0,1:T(8,128)(2,1)S(1)} %fusion.52), channel_id=1, source_target_pairs={{1,0},{2,1},{3,2},{5,4},{6,5},{7,6},{9,8},{10,9},{11,10},{13,12},{... | collective-permute-start | bytes 1572872 | tf_op jit(solution)/shard_map/ppermute | solution.py:62
  914.8 46.6 %collective-permute-start.45 = (bf16[64,2048]{1,0:T(8,128)(2,1)}, bf16[64,2048]{1,0:T(8,128)(2,1)}, u32[]{:S(2)}, u32[]{:S(2)}) collective-permute-start(bf16[64,2048]{1,0:T(8,128)(2,1)} %get-tuple-element.64), channel_id=1, source_target_pairs={{0,2},{1,3},{2,0},{3,1},{4,6},{5,7},{6,4},{7,5},{8,10},{9,11},{10,... | collective-permute-start | bytes 786440 | tf_op jit(solution)/shard_map/ppermute | solution.py:66
  915.6 45.9 %collective-permute-start.44 = (bf16[64,2048]{1,0:T(8,128)(2,1)S(1)}, bf16[64,2048]{1,0:T(8,128)(2,1)}, u32[]{:S(2)}, u32[]{:S(2)}) collective-permute-start(bf16[64,2048]{1,0:T(8,128)(2,1)S(1)} %get-tuple-element.62), channel_id=1, source_target_pairs={{0,1},{1,2},{2,3},{3,0},{4,5},{5,6},{6,7},{7,4},{8,9},{9,10},{10,1... | collective-permute-start | bytes 786440 | tf_op jit(solution)/shard_map/ppermute | solution.py:66
  921.4 42.5 %collective-permute-start.48 = (bf16[64,4096]{1,0:T(8,128)(2,1)}, bf16[64,4096]{1,0:T(8,128)(2,1)}, u32[]{:S(2)}, u32[]{:S(2)}) collective-permute-start(bf16[64,4096]{1,0:T(8,128)(2,1)} %get-tuple-element.49), channel_id=1, source_target_pairs={{0,1},{1,2},{2,3},{3,0},{4,5},{5,6},{6,7},{7,4},{8,9},{9,10},{10,1... | collective-permute-start | bytes 1572872 | tf_op jit(solution)/shard_map/ppermute | solution.py:66
  987.7 36.6 %collective-permute-start.41 = (bf16[64,3200]{1,0:T(8,128)(2,1)S(1)}, bf16[64,3200]{1,0:T(8,128)(2,1)}, u32[]{:S(2)}, u32[]{:S(2)}) collective-permute-start(bf16[64,3200]{1,0:T(8,128)(2,1)S(1)} %get-tuple-element.61), channel_id=1, source_target_pairs={{0,2},{1,3},{2,0},{3,1},{4,6},{5,7},{6,4},{7,5},{8,10},{9,11},{10,... | collective-permute-start | bytes 1228808 | tf_op jit(solution)/shard_map/ppermute | solution.py:66
  987.7 36.6 %collective-permute-start.40 = (bf16[64,3200]{1,0:T(8,128)(2,1)S(1)}, bf16[64,3200]{1,0:T(8,128)(2,1)}, u32[]{:S(2)}, u32[]{:S(2)}) collective-permute-start(bf16[64,3200]{1,0:T(8,128)(2,1)S(1)} %get-tuple-element.59), channel_id=1, source_target_pairs={{0,1},{1,2},{2,3},{3,0},{4,5},{5,6},{6,7},{7,4},{8,9},{9,10},{10,1... | collective-permute-start | bytes 1228808 | tf_op jit(solution)/shard_map/ppermute | solution.py:66
  (87 other events, 1700.8 us)
Sparse Core Ops, SparseCore 0:
  44.6 82.2 all-gather.4
  129.4 56.3 all-gather.6
  188.2 54.3 all-gather.10
  245.0 89.8 all-gather.8
  697.7 52.4 reduce-scatter.6
  753.4 86.3 reduce-scatter.8
  842.8 58.2 reduce-scatter.10
  910.3 72.6 reduce-scatter.4

commit v2 on v1

v2 whole, which is shorter than its diff:
```python
import math

import jax
import jax.numpy as jnp
from jax import lax
from jax.experimental import pallas as pl
from jax.experimental.pallas import tpu as pltpu
from jax.sharding import Mesh
from jax.sharding import PartitionSpec as P

HEAD_DIM = 64
EPSILON = 1e-05
ROPE_BASE = 500000.0
MASKED_SCORE = -1e30
LANES = 128
GROUP = 4
SCORE_SCALE = HEAD_DIM**-0.5
KERNEL_MEMORY = 40 * 2**20
FEED_MEMORY = 56 * 2**20
FEED_STEP = 256
BACK_COST = pl.CostEstimate(flops=24_000_000_000, bytes_accessed=10_000_000, transcendentals=0)
COST = pl.CostEstimate(flops=1_000_000, bytes_accessed=1_000_000, transcendentals=0)

LOW = jnp.bfloat16
WIDE = jnp.float32
NN = (((1,), (0,)), ((), ()))
NT = (((1,), (1,)), ((), ()))
TN = (((0,), (0,)), ((), ()))


def dot(left, right, dims):
    return lax.dot_general(left, right, dims, preferred_element_type=WIDE)


def inverse_root(values):
    return lax.rsqrt(jnp.mean(values * values, axis=-1, keepdims=True) + EPSILON)


def norm_back(values, grad_normed):
    scaled = inverse_root(values)
    unit_rows = values * scaled
    return scaled * (
        grad_normed - unit_rows * jnp.mean(grad_normed * unit_rows, axis=-1, keepdims=True)
    )


def tie_kernel(*refs):
    del refs


def after(values, *earlier):
    anywhere = pl.BlockSpec(memory_space=pl.ANY)
    return pl.pallas_call(
        tie_kernel,
        in_specs=[anywhere] * (1 + len(earlier)),
        out_specs=anywhere,
        out_shape=jax.ShapeDtypeStruct(values.shape, values.dtype),
        input_output_aliases={0: 0},
        name="after",
    )(values, *earlier)


def turned(values, cosine, sine, first_half):
    ahead = pltpu.roll(values, LANES - HEAD_DIM // 2, 1)
    behind = pltpu.roll(values, HEAD_DIM // 2, 1)
    return values * cosine + jnp.where(first_half, ahead, behind) * sine


def lane_index():
    return lax.broadcasted_iota(jnp.int32, (1, LANES), 1)


def first_half_lanes():
    return lax.rem(lane_index(), HEAD_DIM) < HEAD_DIM // 2


def placed(block, member, head):
    start = member * GROUP * HEAD_DIM + (head // 2) * LANES
    values = block[:, start : start + LANES]
    if head % 2 != member:
        values = pltpu.roll(values, HEAD_DIM, 1)
    own = (lane_index() >= HEAD_DIM) if member else (lane_index() < HEAD_DIM)
    return jnp.where(own, values, jnp.zeros_like(values))


def forward_kernel(
    raw_ref, cos_ref, sin_ref, key_ref, value_ref, bias_ref, query_ref, out_ref, log_ref
):
    half = first_half_lanes()
    cosine, sine = cos_ref[...], sin_ref[...]
    wide = raw_ref.shape[1]
    block = jnp.concatenate(
        [
            turned(raw_ref[:, c : c + LANES], cosine, sine, half).astype(LOW).astype(WIDE)
            * SCORE_SCALE
            for c in range(0, wide, LANES)
        ],
        1,
    )
    query_ref[...] = block.astype(LOW)
    keys, values = key_ref[...], value_ref[...]
    span = GROUP * HEAD_DIM
    for member in range(2):
        parts = []
        for head in range(GROUP):
            query = placed(block, member, head).astype(LOW)
            scores = dot(keys, query, NT) + bias_ref[...]
            top = jnp.max(scores, 0, keepdims=True)
            exponent = jnp.exp(scores - top)
            total = jnp.sum(exponent, 0, keepdims=True)
            mixed = dot(values, exponent.astype(LOW), TN)
            parts.append(mixed[member * HEAD_DIM : (member + 1) * HEAD_DIM] / total)
            row = member * GROUP + head
            log_ref[row : row + 1, :] = top + jnp.log(total)
        out_ref[:, member * span : (member + 1) * span] = jnp.concatenate(parts, 0).T.astype(LOW)


def backward_kernel(
    query_ref,
    cos_ref,
    sin_ref,
    key_ref,
    value_ref,
    bias_ref,
    grad_ref,
    out_ref,
    log_ref,
    grad_query_ref,
    grad_key_ref,
    grad_value_ref,
):
    half = first_half_lanes()
    cosine, sine = cos_ref[...], -sin_ref[...]
    block = query_ref[...].astype(WIDE)
    grad = grad_ref[...].astype(WIDE)
    product = grad * out_ref[...].astype(WIDE)
    keys, values = key_ref[...], value_ref[...]
    span = GROUP * HEAD_DIM
    grad_keys = grad_values = None
    for member in range(2):
        parts = []
        product_t = product[:, member * span : (member + 1) * span].T
        for head in range(GROUP):
            query = placed(block, member, head).astype(LOW)
            grad_out = placed(grad, member, head).astype(LOW)
            row = member * GROUP + head
            delta = jnp.sum(
                product_t[head * HEAD_DIM : (head + 1) * HEAD_DIM], 0, keepdims=True
            )
            scores = dot(keys, query, NT) + bias_ref[...]
            probs = jnp.exp(scores - log_ref[row : row + 1, :])
            grad_probs = dot(values, grad_out, NT)
            grad_scores = (probs * (grad_probs - delta)).astype(LOW)
            key_part = dot(grad_scores, query, NN)
            value_part = dot(probs.astype(LOW), grad_out, NN)
            grad_keys = key_part if grad_keys is None else grad_keys + key_part
            grad_values = value_part if grad_values is None else grad_values + value_part
            query_part = dot(keys, grad_scores, TN)
            parts.append(query_part[member * HEAD_DIM : (member + 1) * HEAD_DIM] * SCORE_SCALE)
        grad_query = jnp.concatenate(parts, 0).T
        for c in range(0, span, LANES):
            grad_query_ref[:, member * span + c : member * span + c + LANES] = turned(
                grad_query[:, c : c + LANES], cosine, sine, half
            ).astype(LOW)
    grad_key_ref[...] = grad_keys.astype(LOW)
    grad_value_ref[...] = grad_values.astype(LOW)


def turn_kernel(values_ref, cos_ref, sin_ref, out_ref):
    half = first_half_lanes()
    width = values_ref.shape[1]
    for c in range(0, width // 2, LANES):
        out_ref[:, c : c + LANES] = turned(
            values_ref[:, c : c + LANES], cos_ref[...], sin_ref[...], half
        ).astype(LOW)
    out_ref[:, width // 2 :] = values_ref[:, width // 2 :].astype(LOW)


def feed_kernel(
    token_ref, goal_ref, gate_ref, up_ref, down_ref, active_ref, grad_gate_ref, grad_up_ref
):
    gate, up = dot(token_ref[...], gate_ref[...], NN), dot(token_ref[...], up_ref[...], NN)
    grad_active = dot(goal_ref[...], down_ref[...], NT)
    sigmoid = 1.0 / (1.0 + jnp.exp(-gate))
    silu = gate * sigmoid
    active_ref[...] = (silu * up).astype(LOW)
    grad_gate_ref[...] = (grad_active * up * sigmoid * (1.0 + gate * (1.0 - sigmoid))).astype(LOW)
    grad_up_ref[...] = (grad_active * silu).astype(LOW)


def second_kernel(grad_gate_ref, grad_up_ref, gate_ref, up_ref, out_ref):
    out_ref[...] = (
        dot(grad_gate_ref[...], gate_ref[...], NT) + dot(grad_up_ref[...], up_ref[...], NT)
    ).astype(LOW)


def feed_specs(count, width):
    whole = pl.BlockSpec((count, width), lambda i: (0, 0))
    return whole, pl.BlockSpec((count, FEED_STEP), lambda i: (0, i))


def feed(tokens, goal, both, down):
    count, width = tokens.shape
    hidden = down.shape[0]
    steps = hidden // FEED_STEP
    whole, part = feed_specs(count, width)
    return pl.pallas_call(
        feed_kernel,
        grid=(steps,),
        in_specs=[
            whole,
            whole,
            pl.BlockSpec((width, FEED_STEP), lambda i: (0, i)),
            pl.BlockSpec((width, FEED_STEP), lambda i: (0, i + steps)),
            pl.BlockSpec((FEED_STEP, width), lambda i: (i, 0)),
        ],
        out_specs=[part, part, part],
        out_shape=[jax.ShapeDtypeStruct((count, hidden), LOW)] * 3,
        compiler_params=pltpu.CompilerParams(vmem_limit_bytes=FEED_MEMORY),
        cost_estimate=COST,
        name="feed",
    )(tokens, goal, both, both, down)


def feed_back(grad_gate, grad_up, both):
    count, hidden = grad_gate.shape
    width = both.shape[0]
    whole, part = feed_specs(count, hidden)
    return pl.pallas_call(
        second_kernel,
        grid=(width // FEED_STEP,),
        in_specs=[
            whole,
            whole,
            pl.BlockSpec((FEED_STEP, hidden), lambda i: (i, 0)),
            pl.BlockSpec((FEED_STEP, hidden), lambda i: (i, 1)),
        ],
        out_specs=part,
        out_shape=jax.ShapeDtypeStruct((count, width), LOW),
        compiler_params=pltpu.CompilerParams(vmem_limit_bytes=FEED_MEMORY),
        cost_estimate=COST,
        name="feed_back",
    )(grad_gate, grad_up, both, both)


def weight_kernel(shared, parts, core_ref, *refs):
    del core_ref
    sides = max(shared) + 1
    lefts, rest = refs[: sides * parts], refs[sides * parts :]
    rights, out_ref = rest[: len(shared) * parts], rest[-1]
    came_ref = rest[-2] if len(rest) > len(shared) * parts + 1 else None
    for kind, side in enumerate(shared):

        @pl.when(pl.program_id(1) == kind)
        def _():
            total = None
            for part in range(parts):
                term = dot(
                    lefts[side * parts + part][...], rights[kind * parts + part][...], TN
                )
                total = term if total is None else total + term
            if came_ref is not None:
                total = total + came_ref[...].astype(WIDE)
            out_ref[...] = total.astype(LOW)


def weight_rows(lefts, rights, shared, index, chips, n_core, came=None):
    tokens, columns = rights[0][0].shape
    kinds, parts = len(rights), len(rights[0])
    size = lefts[0][0].shape[1] // (chips * n_core)
    left = pl.BlockSpec((tokens, size), lambda i, g, core: (0, i * n_core + core[0]))
    right = pl.BlockSpec((tokens, columns), lambda i, g, core: (0, 0))
    out = pl.BlockSpec((size, columns), lambda i, g, core: (i * kinds + g, 0))
    return pl.pallas_call(
        lambda *refs: weight_kernel(shared, parts, *refs),
        grid_spec=pltpu.PrefetchScalarGridSpec(
            num_scalar_prefetch=1,
            grid=(chips, kinds),
            in_specs=[left] * (parts * len(lefts))
            + [right] * (kinds * parts)
            + ([] if came is None else [out]),
            out_specs=out,
        ),
        out_shape=jax.ShapeDtypeStruct((chips * kinds * size, columns), LOW),
        compiler_params=pltpu.CompilerParams(vmem_limit_bytes=FEED_MEMORY),
        cost_estimate=pl.CostEstimate(
            flops=2 * chips * kinds * size * columns * tokens * parts,
            bytes_accessed=2 * chips * kinds * size * columns,
            transcendentals=0,
        ),
        name="weight_rows",
    )(
        jnp.reshape(index, (1,)).astype(jnp.int32),
        *(part for side in lefts for part in side),
        *(part for kind in rights for part in kind),
        *([] if came is None else [came]),
    )


def fixed_block(shape):
    return pl.BlockSpec(shape, lambda i: (0, 0))


def attention_blocks(count, length, steps):
    span = 2 * GROUP * HEAD_DIM
    return (
        pl.BlockSpec((count, span), lambda i: (0, i)),
        pl.BlockSpec((length, LANES), lambda i: (0, i)),
        pl.BlockSpec((length, LANES), lambda i: (0, i + steps)),
        pl.BlockSpec((2 * GROUP, count), lambda i: (i, 0)),
    )


def attend(raw, cosine, sine, pair, bias):
    count, length = raw.shape[0], pair.shape[0]
    steps = pair.shape[1] // 2 // LANES
    wide, key, value, rows = attention_blocks(count, length, steps)
    table = fixed_block((count, LANES))
    return pl.pallas_call(
        forward_kernel,
        grid=(steps,),
        in_specs=[wide, table, table, key, value, fixed_block((length, count))],
        out_specs=[wide, wide, rows],
        out_shape=[
            jax.ShapeDtypeStruct(raw.shape, LOW),
            jax.ShapeDtypeStruct(raw.shape, LOW),
            jax.ShapeDtypeStruct((steps * 2 * GROUP, count), WIDE),
        ],
        compiler_params=pltpu.CompilerParams(vmem_limit_bytes=KERNEL_MEMORY),
        cost_estimate=COST,
        name="attend",
    )(raw, cosine, sine, pair, pair, bias)


def attend_back(query, cosine, sine, pair, bias, grad, out, log_total):
    count, length = query.shape[0], pair.shape[0]
    steps = pair.shape[1] // 2 // LANES
    wide, key, value, rows = attention_blocks(count, length, steps)
    table = fixed_block((count, LANES))
    half = jax.ShapeDtypeStruct((length, steps * LANES), LOW)
    return pl.pallas_call(
        backward_kernel,
        grid=(steps,),
        in_specs=[wide, table, table, key, value, fixed_block((length, count)), wide, wide, rows],
        out_specs=[wide, key, key],
        out_shape=[jax.ShapeDtypeStruct(query.shape, LOW), half, half],
        compiler_params=pltpu.CompilerParams(vmem_limit_bytes=KERNEL_MEMORY),
        cost_estimate=BACK_COST,
        name="attend_back",
    )(query, cosine, sine, pair, pair, bias, grad, out, log_total)


def turn_pair(values, cosine, sine):
    return pl.pallas_call(
        turn_kernel, out_shape=jax.ShapeDtypeStruct(values.shape, LOW), name="turn_pair"
    )(values, cosine, sine)


def shift(values, count, step, senders):
    pairs = [(i, i + step) for i in senders if 0 <= i + step < count]
    return lax.ppermute(values, "ctx", pairs)


def rotate(values, count, step):
    return lax.ppermute(values, "ctx", [(i, (i + step) % count) for i in range(count)])


def line_slot(up, down, count, me, r):
    return up[0] if r == 0 else jnp.where(me >= r, up[r], down[count - r])


def line_chains(own, count):
    up, down = [own], [own]
    for s in range(1, count):
        up.append(shift(up[-1], count, 1, range(s - 1, count)))
        down.append(shift(down[-1], count, -1, range(0, count - s + 1)))
    return up, down


def line_groups(count):
    first = [r for r in range(count) if r == 0 or max(r, count - r) < count - 1]
    groups = [first, [r for r in range(count) if r not in first]]
    return [group for group in groups if group]


def line_step(slots, count, step, came):
    up, down = slots[step], slots[count - step]
    if came is not None:
        up = (up.astype(WIDE) + came[0].astype(WIDE)).astype(LOW)
        down = (down.astype(WIDE) + came[1].astype(WIDE)).astype(LOW)
    return up, down


def line_send(pair, count, step):
    up = shift(pair[0], count, 1, range(0, step))
    return up, shift(pair[1], count, -1, range(count - step, count))


def line_gather_up(own, count):
    return [own] + [shift(own, count, s, range(count)) for s in range(1, count)]


def in_order(slots, count, me):
    out = jnp.zeros((count, *slots[0].shape), slots[0].dtype)
    for r in range(count):
        out = lax.dynamic_update_index_in_dim(out, slots[r], lax.rem(me - r + count, count), 0)
    return out


CHIPS = ("y", "x")
PLANES = ("y", "x", "core")
SWAP = [(0, 1), (1, 0)]


def pick(values, index, axis):
    return lax.dynamic_index_in_dim(values, index, axis, keepdims=False)


def small_square():
    return lax.axis_size("y") == 2 and lax.axis_size("x") == 2 and lax.axis_size("core") == 2


def plane_gather(values):
    return lax.all_gather(values, PLANES, axis=0, tiled=True)


def core_columns(values, index):
    n_core, chips = lax.axis_size("core"), lax.axis_size(CHIPS)
    size = values.shape[1] // (chips * n_core)
    return jnp.concatenate(
        [
            lax.dynamic_slice_in_dim(values, (chip * n_core + index) * size, size, 1)
            for chip in range(chips)
        ],
        1,
    )


def core_term(left, right):
    if lax.axis_size("core") == 1:
        return None
    return dot(core_columns(left, 1 - lax.axis_index("core")), right, TN).astype(LOW)


def core_summed(left, right, sent=None):
    if lax.axis_size("core") == 1:
        return dot(left, right, TN).astype(LOW)
    sent = core_term(left, right) if sent is None else sent
    came = lax.ppermute(sent, "core", SWAP)
    own = core_columns(left, lax.axis_index("core"))
    return (dot(own, right, TN) + came.astype(WIDE)).astype(LOW)


def group_terms(lefts, rights, shared):
    n_core, chips = lax.axis_size("core"), lax.axis_size(CHIPS)
    core = lax.axis_index("core")
    size = lefts[0][0].shape[1] // (chips * n_core)
    if n_core == 2 and size % LANES == 0:
        sent = weight_rows(lefts, rights, shared, 1 - core, chips, n_core)

        def summed(tied, last=()):
            came = lax.ppermute(after(sent, *tied), "core", SWAP)
            came = after(came, *last) if last else came
            return weight_rows(lefts, rights, shared, core, chips, n_core, came)

        return sent, summed
    each = [
        core_summed(jnp.concatenate(lefts[side], 0), jnp.concatenate(kind, 0))
        for kind, side in zip(rights, shared)
    ]
    each = jnp.concatenate([values.reshape(chips, 1, size, -1) for values in each], 1)
    each = each.reshape(chips * len(rights) * size, -1)
    return each, lambda tied, last=(): each


def chip_scatter(values):
    return lax.psum_scatter(values, CHIPS, scatter_dimension=0, tiled=True)


def chip_scatter_steps(values, *between):
    if not small_square():
        return chip_scatter(values)
    columns = values.shape[1]
    y, x = lax.axis_index("y"), lax.axis_index("x")
    parts = values.reshape(2, 2, -1, columns)
    half = parts.shape[2] // 2
    add = lambda a, b: (a.astype(WIDE) + b.astype(WIDE)).astype(LOW)
    top, bottom = parts[:, :, :half], parts[:, :, half:]
    top_came = lax.ppermute(pick(top, 1 - x, 1), "x", SWAP)
    bottom_came = lax.ppermute(pick(bottom, 1 - y, 0), "y", SWAP)
    top = after(add(pick(top, x, 1), top_came), *between)
    bottom = add(pick(bottom, y, 0), bottom_came)
    top_came = lax.ppermute(pick(top, 1 - y, 0), "y", SWAP)
    bottom_came = lax.ppermute(pick(bottom, 1 - x, 0), "x", SWAP)
    top = add(pick(top, y, 0), top_came)
    bottom = add(pick(bottom, x, 0), bottom_came)
    return jnp.concatenate([top, bottom], 0)


def per_device(
    inputs,
    cotangent,
    segment_ids,
    real_entry_flags,
    attention_gain,
    feedforward_gain,
    query_weight,
    key_weight,
    value_weight,
    output_weight,
    gate_weight,
    up_weight,
    down_weight,
):
    n_ctx = lax.axis_size("ctx")
    n_dp = lax.axis_size(PLANES)
    me = lax.axis_index("ctx")
    entry_count, width = inputs.shape
    query_width = query_weight.shape[1]
    pair_width = key_weight.shape[1]
    hidden_units = gate_weight.shape[1]
    rows = gate_weight.shape[0]
    hidden_rows = down_weight.shape[0]
    hidden_chunk = hidden_units // n_ctx

    def ctx_rows_gather(values):
        slots = [values] + [rotate(values, n_ctx, r) for r in range(1, n_ctx)]
        return in_order(slots, n_ctx, me).reshape(n_ctx * rows, -1)

    gains = jnp.pad(
        jnp.stack([attention_gain, feedforward_gain], 1), ((0, 0), (0, LANES - 2))
    )
    pair_low = jnp.concatenate([key_weight, value_weight, gains], 1).astype(LOW)
    pair_rows = ctx_rows_gather(pair_low)
    pair_full = plane_gather(pair_rows)

    branch_low = jnp.concatenate([query_weight, output_weight], 1).astype(LOW)
    branch_rows = ctx_rows_gather(after(branch_low, pair_rows))
    branch_full = plane_gather(branch_rows)

    both = jnp.stack([gate_weight, up_weight], 1).astype(LOW)
    both = both.reshape(rows, 2, n_dp, n_ctx, hidden_rows)
    chunk_for = lambda place: pick(both, place, 3).reshape(rows, 2 * hidden_chunk)

    gain_first = pair_full[:, 2 * pair_width].astype(WIDE)
    gain_second = pair_full[:, 2 * pair_width + 1].astype(WIDE)
    pair_weight = pair_full[:, : 2 * pair_width]
    query_full = branch_full[:, :query_width]
    output_full = branch_full[:, query_width:]

    spans = segment_ids[0]
    reality = real_entry_flags[0]
    opening = me * entry_count
    places = opening + jnp.arange(entry_count, dtype=jnp.int32)
    own_spans = lax.dynamic_slice_in_dim(spans, opening, entry_count)
    doc_starts = jnp.sum((spans[None, :] < own_spans[:, None]).astype(jnp.int32), axis=1)
    offsets = (places - doc_starts).astype(WIDE)
    frequency = ROPE_BASE ** (
        -(jnp.arange(HEAD_DIM // 2, dtype=WIDE) * 2.0 / HEAD_DIM)
    )
    angle = offsets[:, None] * frequency[None, :]
    cosine, sine = jnp.cos(angle), jnp.sin(angle)
    cosine = jnp.concatenate([cosine] * 4, 1)
    sine = jnp.concatenate([-sine, sine] * 2, 1)
    key_places, key_spans, key_reality = [], [], []
    for r in range(n_ctx):
        start = (me - r) * entry_count
        key_places.append(start + jnp.arange(entry_count, dtype=jnp.int32))
        start = jnp.maximum(start, 0)
        key_spans.append(lax.dynamic_slice_in_dim(spans, start, entry_count))
        key_reality.append(lax.dynamic_slice_in_dim(reality, start, entry_count))
    key_places = jnp.concatenate(key_places)[:, None]
    key_spans = jnp.concatenate(key_spans)[:, None]
    key_reality = jnp.concatenate(key_reality)[:, None]
    allowed = (
        (own_spans[None, :] == key_spans)
        & (key_places <= places[None, :])
        & (key_places >= 0)
        & (key_reality == 1)
    ) | (key_places == places[None, :])
    bias = jnp.where(allowed, 0.0, MASKED_SCORE).astype(WIDE)

    tokens_wide = inputs.astype(WIDE)
    unit_first = tokens_wide * inverse_root(tokens_wide)
    first_hidden = (unit_first * gain_first).astype(LOW)
    both_slots = [chunk_for(me)] + [
        rotate(after(chunk_for(lax.rem(me + r, n_ctx)), branch_rows), n_ctx, r)
        for r in range(1, n_ctx)
    ]
    both_rows = in_order(both_slots, n_ctx, me).reshape(n_ctx * rows, 2 * hidden_chunk)
    both_full = plane_gather(both_rows)
    down_full = plane_gather(after(down_weight.astype(LOW), branch_rows))
    pair_own = turn_pair(dot(first_hidden, pair_weight, NN), cosine, sine)
    pair_all = jnp.concatenate(line_gather_up(after(pair_own, both_rows), n_ctx), 0)
    cot_sent = after(cotangent, pair_all)
    cot_slots = [cotangent] + [rotate(cot_sent, n_ctx, r) for r in range(1, n_ctx)]
    raw_query = dot(first_hidden, query_full, NN)
    query, attended, log_total = attend(raw_query, cosine, sine, pair_all, bias)

    residual = tokens_wide + dot(attended, output_full, NN)
    unit_second = residual * inverse_root(residual)
    second_hidden = (unit_second * gain_second).astype(LOW)
    up_chain, down_chain = line_chains(after(second_hidden, *cot_slots[1:]), n_ctx)
    groups = line_groups(n_ctx)
    hidden, cot, active, gates, ups = [], [], [], [], []
    second_slots, down_slots = [None] * n_ctx, [None] * n_ctx
    for group in groups:
        tokens = jnp.concatenate(
            [line_slot(up_chain, down_chain, n_ctx, me, r) for r in group], 0
        )
        goal = jnp.concatenate([cot_slots[r] for r in group], 0)
        if active:
            goal = after(goal, active[-1])
        group_active, grad_gate, grad_up = feed(tokens, goal, both_full, down_full)
        second = feed_back(grad_gate, grad_up, both_full)
        for k, r in enumerate(group):
            second_slots[r] = second[k * entry_count : (k + 1) * entry_count]
        for kept, value in zip(
            (hidden, cot, active, gates, ups), (tokens, goal, group_active, grad_gate, grad_up)
        ):
            kept.append(value)

    def down_terms(k, *tied):
        down_out = dot(after(active[k], *tied), down_full, NN).astype(LOW)
        for i, r in enumerate(groups[k]):
            down_slots[r] = down_out[i * entry_count : (i + 1) * entry_count]
        return down_out

    first = line_step(second_slots, n_ctx, 1, None)
    came, steps = line_send(first, n_ctx, 1), [first]
    early = down_terms(-1, *first)
    for step in range(2, n_ctx):
        sent = line_step(second_slots, n_ctx, step, came)
        if step == 2:
            sent = after(sent[0], early), sent[1]
        steps.append(sent)
        came = line_send(sent, n_ctx, step)
    gates[0] = after(gates[0], *steps[min(1, n_ctx - 2)])
    feed_sent, feed_summed = group_terms([hidden, active], [gates, ups, cot], [0, 0, 1])
    if len(groups) > 1:
        late = down_terms(0, *steps[-1])
        came = after(came[0], late), came[1]
    grad_second = second_slots[0].astype(WIDE) + came[0].astype(WIDE) + came[1].astype(WIDE)
    down_sent = tuple(
        after(values, grad_second) for values in line_step(down_slots, n_ctx, 1, None)
    )
    feed_part = feed_summed(steps[-1], down_sent)
    in_slots = lambda values: [
        values[r * entry_count : (r + 1) * entry_count] for r in range(n_ctx)
    ]
    feed_rows = chip_scatter(feed_part).reshape(3, n_ctx * rows, hidden_chunk)
    both_grad_rows = feed_rows[:2]
    down_weight_grad = feed_rows[2].astype(WIDE)

    both_grad_parts = both_grad_rows.reshape(2, n_ctx, rows, hidden_chunk)
    part_for = lambda place: pick(both_grad_parts, place, 1).reshape(2 * rows, hidden_chunk)
    grad_slots = [part_for(me)] + [
        rotate(part_for(lax.rem(me + r, n_ctx)), n_ctx, r) for r in range(1, n_ctx)
    ]

    second_gain_term = jnp.sum(grad_second * unit_second, axis=0)
    grad_residual = cotangent.astype(WIDE) + norm_back(residual, grad_second * gain_second)
    grad_branch = grad_residual.astype(LOW)
    grad_attended = after(dot(grad_branch, output_full, NT).astype(LOW), feed_part)
    down_came = None
    for step in range(1, n_ctx - 1):
        if step > 1:
            down_sent = line_step(down_slots, n_ctx, step, down_came)
            grad_attended = after(grad_attended, *down_sent)
        down_came = line_send(down_sent, n_ctx, step)
    grad_query, key_part, value_part = attend_back(
        query, cosine, sine, pair_all, bias, grad_attended, attended, log_total
    )
    pair_part = jnp.concatenate([key_part, value_part], 1)
    pair_part = jnp.concatenate([key_part, value_part], 1)
    if down_came is not None:
        down_came = tuple(after(values, grad_query) for values in down_came)
        down_sent = line_step(down_slots, n_ctx, n_ctx - 1, down_came)
    pair_part = after(pair_part, *down_sent)
    pair_slots = in_slots(pair_part)
    came, steps = None, []
    for step in range(1, n_ctx):
        sent = pair_slots[n_ctx - step]
        if came is not None:
            sent = (sent.astype(WIDE) + came.astype(WIDE)).astype(LOW)
        steps.append(sent)
        came = shift(sent, n_ctx, -1, range(n_ctx - step, n_ctx))
    pair_grad = pair_slots[0].astype(WIDE) + came.astype(WIDE)
    _, branch_summed = group_terms(
        [[attended], [first_hidden]],
        [[after(grad_branch, steps[min(1, n_ctx - 2)])], [grad_query]],
        [0, 1],
    )
    branch_terms = branch_summed([steps[-1]])
    grad_pair = turn_pair(after(pair_grad, grad_slots[n_ctx // 2]), cosine, -sine)
    grad_first = dot(grad_query, query_full, NT) + dot(grad_pair, pair_weight, NT)
    first_gain_term = jnp.sum(grad_first * unit_first, axis=0)
    input_grad = (grad_residual + norm_back(tokens_wide, grad_first * gain_first)).astype(LOW)

    def ctx_rows_scatter(values, *earlier):
        parts = values.reshape(n_ctx, -1, values.shape[1])
        total = pick(parts, me, 0).astype(WIDE)
        for r in range(1, n_ctx):
            came = rotate(pick(parts, lax.rem(me + r, n_ctx), 0), n_ctx, r)
            total = total + (after(came, *earlier) if earlier else came).astype(WIDE)
        return total

    branch_part = chip_scatter(branch_terms)
    gain_terms = jnp.pad(
        jnp.stack([first_gain_term, second_gain_term], 1), ((0, 0), (0, LANES - 2))
    ).astype(LOW)
    gain_parts = gain_terms.reshape(lax.axis_size(CHIPS), lax.axis_size("core"), -1, LANES)
    gain_part = pick(gain_parts, lax.axis_index("core"), 1)
    if lax.axis_size("core") == 2:
        gain_came = lax.ppermute(pick(gain_parts, 1 - lax.axis_index("core"), 1), "core", SWAP)
        gain_part = (gain_part.astype(WIDE) + gain_came.astype(WIDE)).astype(LOW)
    pair_terms = jnp.concatenate(
        [core_summed(first_hidden, grad_pair), gain_part.reshape(-1, LANES)], 1
    )
    pair_sum = chip_scatter_steps(pair_terms, *grad_slots[1:])
    pair_weight_grad = ctx_rows_scatter(pair_sum)
    grad_slots[0] = after(grad_slots[0], pair_weight_grad)
    both_grad = in_order(grad_slots, n_ctx, me).reshape(n_ctx, 2, rows, n_dp, hidden_rows)
    both_grad = both_grad.transpose(1, 2, 3, 0, 4).reshape(2, rows, hidden_units).astype(WIDE)
    gate_weight_grad, up_weight_grad = both_grad[0], both_grad[1]
    branch_part = after(branch_part, *grad_slots[1:]).reshape(2, n_ctx, rows, width)
    branch_part = branch_part.transpose(1, 0, 2, 3).reshape(n_ctx * 2 * rows, width)
    branch_grad = ctx_rows_scatter(branch_part, pair_sum).reshape(2, rows, width)
    down_sent = after(down_sent[0], pair_sum), down_sent[1]
    came = line_send(down_sent, n_ctx, n_ctx - 1)
    down_value = down_slots[0].astype(WIDE) + came[0].astype(WIDE) + came[1].astype(WIDE)
    block_output = (residual + down_value).astype(LOW)
    return (
        block_output,
        input_grad,
        pair_weight_grad[:, 2 * pair_width],
        pair_weight_grad[:, 2 * pair_width + 1],
        branch_grad[1],
        pair_weight_grad[:, :pair_width],
        pair_weight_grad[:, pair_width : 2 * pair_width],
        branch_grad[0],
        gate_weight_grad,
        up_weight_grad,
        down_weight_grad,
    )


def solution(mesh):
    n_dp, n_ctx = mesh.shape["dp"], mesh.shape["ctx"]
    n_core = 2 if n_dp % 2 == 0 else 1
    n_chips = n_dp // n_core
    n_y = math.isqrt(n_chips)
    while n_chips % n_y:
        n_y -= 1
    axes = ("y", "x", "core", "ctx")
    fine = Mesh(mesh.devices.reshape(n_y, n_chips // n_y, n_core, n_ctx), axes)
    matrix = P(axes, None)
    vector = P(axes)
    per_sequence = P(PLANES, None)
    return jax.shard_map(
        per_device,
        mesh=fine,
        in_specs=(matrix, matrix, per_sequence, per_sequence, vector, vector) + (matrix,) * 7,
        out_specs=(matrix, matrix, vector, vector) + (matrix,) * 7,
        check_vma=False,
    )
```

time: 1040 us -> 909 us (0.87); the launches traced: 1040 us -> 892 us
  Pallas kernels: 0 us -> 191 us
  matrix products: 244 us -> 63.5 us
  waiting for transfers between devices: 416 us -> 315 us
  other arithmetic: 157 us -> 68.2 us
  starting transfers between devices: 128 us -> 170 us
    pallas_call x0 -> x45, Pallas kernels: none -> 191 us  [the longest x4 68.5 us: weight_rows(): pl.pallas_call(lambda *refs: weight_kernel(shared, parts, *refs), grid_sp...]
    dot_general x21 -> x10, matrix products: 244 us -> 63.5 us  [dot(): return lax.dot_general(left, right, dims, preferred_element_type=WIDE)]
    ppermute x30 -> x24, waiting for transfers between devices: 265 us -> 102 us  [shift(): return lax.ppermute(values, 'ctx', pairs)]
    convert_element_type x18 -> x16, other arithmetic: 92.1 us -> 26.8 us  [the longest x4 13.1 us: line_step(): up = (up.astype(WIDE) + came[0].astype(WIDE)).astype(LOW)]
    ppermute x4 -> x8, waiting for transfers between devices: 16.2 us -> 42.9 us  [the longest x2 13.5 us: summed(): came = lax.ppermute(after(sent, *tied), 'core', SWAP)]
    reduce_scatter x4 -> x2, waiting for transfers between devices: 2.56 us -> 24.6 us  [chip_scatter(): return lax.psum_scatter(values, CHIPS, scatter_dimension=0, tiled=True)]
    ppermute x18 -> x21, starting transfers between devices: 44 us -> 64.4 us  [rotate(): lax.ppermute(values, 'ctx', [(i, (i + step) % count) for i in range(count)])]
    squeeze x6, local copies, waits for them, and re-layouts: 19.1 us -> 2.31 us  [pick(): return lax.dynamic_index_in_dim(values, index, axis, keepdims=False)]
  transfers between devices with their start and end apart: 60 -> 59, of which waited for: 29 -> 32; matrix products, arithmetic and copies ran while one was open for 35% -> 18% of each run, Pallas kernels for 0% -> 15%
where the time goes in v2:
time: 909 us; the launch traced here: 892 us
  waiting for transfers between devices  315 us (35%)
  Pallas kernels  191 us (21%)
  starting transfers between devices  170 us (19%)
  local copies, waits for them, and re-layouts  68.6 us (8%)
  other arithmetic  68.2 us (8%)
  matrix products  63.5 us (7%)
  between operations  15.9 us (2%)
    ppermute x21, waiting for transfers between devices, rotate(): lax.ppermute(values, 'ctx', [(i, (i + step) % count) for i in range(count)])  145 us
    ppermute x24, waiting for transfers between devices, shift(): return lax.ppermute(values, 'ctx', pairs)  102 us
    ppermute x24, starting transfers between devices, shift(): return lax.ppermute(values, 'ctx', pairs)  98.8 us
    pallas_call x4, Pallas kernels, weight_rows(): pl.pallas_call(lambda *refs: weight_kernel(shared, parts, *refs), grid_sp...  68.5 us
    ppermute x21, starting transfers between devices, rotate(): lax.ppermute(values, 'ctx', [(i, (i + step) % count) for i in range(count)])  64.4 us
    dot_general x10, matrix products, dot(): return lax.dot_general(left, right, dims, preferred_element_type=WIDE)  63.5 us
    pallas_call x2, Pallas kernels, feed(): pl.pallas_call(feed_kernel, grid=(steps,), in_specs=[whole, whole, pl.Blo...  40.7 us
    pallas_call x2, Pallas kernels, feed_back(): pl.pallas_call(second_kernel, grid=(width // FEED_STEP,), in_specs=[whole...  30.4 us
  transfers between devices with their start and end apart: 59, of which 32 were waited for; matrix products, arithmetic and copies ran while one was open for 18% of the time, Pallas kernels for 15%

profile of v2, /device:TPU:0, one launch (start us, length us, event | category | flops | bytes accessed | tf_op | source)
XLA Modules:
  0.0 891.7 jit_solution(14891683254582020507)
XLA Ops:
  33.5 11.7 %collective-permute-done.3 = bf16[64,4096]{1,0:T(8,128)(2,1)S(1)} collective-permute-done((bf16[64,4096]{1,0:T(8,128)(2,1)}, bf16[64,4096]{1,0:T(8,128)(2,1)S(1)}, u32[]{:S(2)}, u32[]{:S(2)}) %collective-permute-start.3) | collective-permute-done | bytes 524320 | tf_op jit(solution)/shard_map/ppermute | solution.py:365
  45.2 20.6 %collective-permute-done.4 = bf16[64,4096]{1,0:T(8,128)(2,1)S(1)} collective-permute-done((bf16[64,4096]{1,0:T(8,128)(2,1)}, bf16[64,4096]{1,0:T(8,128)(2,1)S(1)}, u32[]{:S(2)}, u32[]{:S(2)}) %collective-permute-start.4) | collective-permute-done | bytes 524320 | tf_op jit(solution)/shard_map/ppermute | solution.py:365
  103.2 21.2 %collective-permute-done.7 = bf16[64,4096]{1,0:T(8,128)(2,1)S(1)} collective-permute-done((bf16[64,4096]{1,0:T(8,128)(2,1)}, bf16[64,4096]{1,0:T(8,128)(2,1)S(1)}, u32[]{:S(2)}, u32[]{:S(2)}) %collective-permute-start.7) | collective-permute-done | bytes 524320 | tf_op jit(solution)/shard_map/ppermute | solution.py:365
  138.5 14.2 %collective-permute-start.11 = (bf16[256,1024]{1,0:T(8,128)(2,1)}, bf16[256,1024]{1,0:T(8,128)(2,1)S(1)}, u32[]{:S(2)}, u32[]{:S(2)}) collective-permute-start(bf16[256,1024]{1,0:T(8,128)(2,1)} %after.37), channel_id=1, source_target_pairs={{0,3},{4,7},{8,11},{12,15},{16,19},{20,23},{24,27},{28,31}} | collective-permute-start | bytes 1572872 | tf_op jit(solution)/shard_map/ppermute | solution.py:361
  187.9 12.7 %collective-permute-start.12 = (bf16[256,2048]{1,0:T(8,128)(2,1)}, bf16[256,2048]{1,0:T(8,128)(2,1)}, u32[]{:S(2)}, u32[]{:S(2)}) collective-permute-start(bf16[256,2048]{1,0:T(8,128)(2,1)} %after.38), channel_id=1, source_target_pairs={{0,1},{1,2},{2,3},{3,0},{4,5},{5,6},{6,7},{7,4},{8,9},{9,10},{10,1... | collective-permute-start | bytes 3145736 | tf_op jit(solution)/shard_map/ppermute | solution.py:365
  211.7 23.8 %attend.1 = (bf16[256,2048]{1,0:T(8,128)(2,1)S(1)}, bf16[256,2048]{1,0:T(8,128)(2,1)S(1)}, f32[32,256]{1,0:T(8,128)S(1)}) custom-call(f32[256,2048]{1,0:T(8,128)S(1)} %fusion.6.raw_ref, f32[256,128]{1,0:T(8,128)S(1)} %copy-done.8, f32[256,128]{1,0:T(8,128)S(1)} %copy-done.9, bf16[1024,1024]{1,0:T(8,128)(2,1)S(1)} %copy-done, bf16[1024,1024]{1,0:T(8,128)(2,1)S(1)} %copy-done, ...), custom_call_target="tpu_custom_call" | custom-call | flops 1000000 | bytes 1000000 | tf_op jit(solution)/shard_map/attend/pallas_call | solution.py:319
  245.5 15.3 %collective-permute-done.13.refs_2_ = bf16[256,2048]{1,0:T(8,128)(2,1)} collective-permute-done((bf16[256,2048]{1,0:T(8,128)(2,1)}, bf16[256,2048]{1,0:T(8,128)(2,1)}, u32[]{:S(2)}, u32[]{:S(2)}) %collective-permute-start.13) | collective-permute-done | bytes 1048608 | tf_op jit(solution)/shard_map/ppermute | solution.py:365
  268.5 27.7 %collective-permute-start.15 = (bf16[256,2048]{1,0:T(8,128)(2,1)}, bf16[256,2048]{1,0:T(8,128)(2,1)}, u32[]{:S(2)}, u32[]{:S(2)}) collective-permute-start(bf16[256,2048]{1,0:T(8,128)(2,1)} %after.39), channel_id=1, source_target_pairs={{0,1},{1,2},{2,3},{4,5},{5,6},{6,7},{8,9},{9,10},{10,11},{12,13},{... | collective-permute-start | bytes 3145736 | tf_op jit(solution)/shard_map/ppermute | solution.py:361
  297.4 19.8 %collective-permute-done.15 = bf16[256,2048]{1,0:T(8,128)(2,1)} collective-permute-done((bf16[256,2048]{1,0:T(8,128)(2,1)}, bf16[256,2048]{1,0:T(8,128)(2,1)}, u32[]{:S(2)}, u32[]{:S(2)}) %collective-permute-start.15) | collective-permute-done | bytes 1048608 | tf_op jit(solution)/shard_map/ppermute | solution.py:361
  331.9 15.7 %collective-permute-done.18 = bf16[256,2048]{1,0:T(8,128)(2,1)} collective-permute-done((bf16[256,2048]{1,0:T(8,128)(2,1)}, bf16[256,2048]{1,0:T(8,128)(2,1)}, u32[]{:S(2)}, u32[]{:S(2)}) %collective-permute-start.18) | collective-permute-done | bytes 1048608 | tf_op jit(solution)/shard_map/ppermute | solution.py:361
  352.0 20.3 %feed.2 = (bf16[512,2048]{1,0:T(8,128)(2,1)}, bf16[512,2048]{1,0:T(8,128)(2,1)}, bf16[512,2048]{1,0:T(8,128)(2,1)}) custom-call(bf16[512,2048]{1,0:T(8,128)(2,1)} %pad_maximum_fusion.1.token_ref.refs_1_, bf16[512,2048]{1,0:T(8,128)(2,1)} %constant_dynamic-update-slice_fusion.1.goal_ref.refs_9_, ...), custom_call_target="tpu_custom_call" | custom-call | flops 1000000 | bytes 1000000 | tf_op jit(solution)/shard_map/feed/pallas_call | solution.py:207
  372.4 15.2 %feed_back.3 = bf16[512,2048]{1,0:T(8,128)(2,1)} custom-call(bf16[512,2048]{1,0:T(8,128)(2,1)} %get-tuple-element.27.grad_gate_ref.refs_0_, bf16[512,2048]{1,0:T(8,128)(2,1)} %get-tuple-element.28.grad_up_ref.refs_7_, bf16[2048,4096]{1,0:T(8,128)(2,1)} %all-gather.9.cloned.1.call-done.gate_ref.up_ref, ...), custom_call_target="tpu_custom_call" | custom-call | flops 1000000 | bytes 1000000 | tf_op jit(solution)/shard_map/feed_back/pallas_call | solution.py:229
  391.9 20.4 %feed.3 = (bf16[512,2048]{1,0:T(8,128)(2,1)}, bf16[512,2048]{1,0:T(8,128)(2,1)}, bf16[512,2048]{1,0:T(8,128)(2,1)}) custom-call(bf16[512,2048]{1,0:T(8,128)(2,1)} %pad_maximum_fusion.2.token_ref.refs_2_, bf16[512,2048]{1,0:T(8,128)(2,1)} %after.41.goal_ref.refs_10_, bf16[2048,4096]{1,0:T(8,128)(2,1)} %all-gather.9.cloned.1.call-done.gate_ref.up_ref, ...), custom_call_target="tpu_custom_call" | custom-call | flops 1000000 | bytes 1000000 | tf_op jit(solution)/shard_map/feed/pallas_call | solution.py:207
  412.2 15.2 %feed_back.2 = bf16[512,2048]{1,0:T(8,128)(2,1)} custom-call(bf16[512,2048]{1,0:T(8,128)(2,1)} %get-tuple-element.25.grad_gate_ref.refs_6_, bf16[512,2048]{1,0:T(8,128)(2,1)} %get-tuple-element.26.grad_up_ref.refs_8_, bf16[2048,4096]{1,0:T(8,128)(2,1)} %all-gather.9.cloned.1.call-done.gate_ref.up_ref, ...), custom_call_target="tpu_custom_call" | custom-call | flops 1000000 | bytes 1000000 | tf_op jit(solution)/shard_map/feed_back/pallas_call | solution.py:229
  466.8 23.0 %weight_rows.4.refs_0_ = bf16[3072,2048]{1,0:T(8,128)(2,1)} custom-call(s32[1]{0:T(128)} %bitcast.29.refs_0_, bf16[512,2048]{1,0:T(8,128)(2,1)} %pad_maximum_fusion.1.token_ref.refs_1_, bf16[512,2048]{1,0:T(8,128)(2,1)} %pad_maximum_fusion.2.token_ref.refs_2_, bf16[512,2048]{1,0:T(8,128)(2,1)} %get-tuple-element.24.refs_1_.refs_3_, ...), custom_call_target="tpu_custom_call" | custom-call | flops 12884901888 | bytes 12582912 | tf_op jit(solution)/shard_map/weight_rows/pallas_call | solution.py:274
  517.5 12.3 %collective-permute-done.25.refs_0_ = bf16[256,2048]{1,0:T(8,128)(2,1)} collective-permute-done((bf16[256,2048]{1,0:T(8,128)(2,1)}, bf16[256,2048]{1,0:T(8,128)(2,1)}, u32[]{:S(2)}, u32[]{:S(2)}) %collective-permute-start.25) | collective-permute-done | bytes 1048608 | tf_op jit(solution)/shard_map/ppermute | solution.py:361
  534.3 24.5 %weight_rows.5.refs_1_ = bf16[3072,2048]{1,0:T(8,128)(2,1)} custom-call(s32[1]{0:T(128)} %bitcast.28.refs_0_, bf16[512,2048]{1,0:T(8,128)(2,1)} %pad_maximum_fusion.1.token_ref.refs_1_, bf16[512,2048]{1,0:T(8,128)(2,1)} %pad_maximum_fusion.2.token_ref.refs_2_, bf16[512,2048]{1,0:T(8,128)(2,1)} %get-tuple-element.24.refs_1_.refs_3_, ...), custom_call_target="tpu_custom_call" | custom-call | flops 12884901888 | bytes 12582912 | tf_op jit(solution)/shard_map/weight_rows/pallas_call | solution.py:274
  600.0 22.6 %attend_back.1 = (bf16[256,2048]{1,0:T(8,128)(2,1)S(1)}, bf16[1024,512]{1,0:T(8,128)(2,1)S(1)}, bf16[1024,512]{1,0:T(8,128)(2,1)S(1)}) custom-call(bf16[256,2048]{1,0:T(8,128)(2,1)S(1)} %copy-done.15, f32[256,128]{1,0:T(8,128)S(1)} %copy-done.8, f32[256,128]{1,0:T(8,128)S(1)} %copy-done.9, bf16[1024,1024]{1,0:T(8,128)(2,1)S(1)} %copy-done, ...), custom_call_target="tpu_custom_call" | custom-call | flops 24000000000 | bytes 10000000 | tf_op jit(solution)/shard_map/attend_back/pallas_call | solution.py:341
  647.2 13.5 %collective-permute-done.49.refs_5_ = bf16[2048,2048]{1,0:T(8,128)(2,1)} collective-permute-done((bf16[2048,2048]{1,0:T(8,128)(2,1)}, bf16[2048,2048]{1,0:T(8,128)(2,1)}, u32[]{:S(2)}, u32[]{:S(2)}) %collective-permute-start.49) | collective-permute-done | bytes 8388640 | tf_op jit(solution)/shard_map/ppermute | solution.py:462
  660.7 11.9 %weight_rows.7 = bf16[2048,2048]{1,0:T(8,128)(2,1)} custom-call(s32[1]{0:T(128)} %bitcast.28.refs_0_, bf16[256,2048]{1,0:T(8,128)(2,1)} %copy-done.4, bf16[256,2048]{1,0:T(8,128)(2,1)} %copy-done.25, bf16[256,2048]{1,0:T(8,128)(2,1)} %after.59.refs_3_, bf16[256,2048]{1,0:T(8,128)(2,1)} %copy-done.1, bf16[2048,2048]{1,0:T(8,128)(2,1)} %collective-permute-done.49.refs_5_), custom_call_target="tpu_custom_call" | custom-call | flops 2147483648 | bytes 8388608 | tf_op jit(solution)/shard_map/weight_rows/pallas_call | solution.py:274
  712.4 17.9 %collective-permute-done.35.refs_1_.refs_2_ = bf16[128,2048]{1,0:T(8,128)(2,1)} collective-permute-done((bf16[128,2048]{1,0:T(8,128)(2,1)}, bf16[128,2048]{1,0:T(8,128)(2,1)}, u32[]{:S(2)}, u32[]{:S(2)}) %collective-permute-start.35) | collective-permute-done | bytes 524320 | tf_op jit(solution)/shard_map/ppermute | solution.py:365
  762.1 14.5 %reduce-scatter.5.cloned.1.call-done.refs_0_ = bf16[512,2048]{1,0:T(8,128)(2,1)} async-done(((bf16[2048,2048]{1,0:T(8,128)(2,1)}), bf16[512,2048]{1,0:T(8,128)(2,1)}) %reduce-scatter.5.cloned.1.call-update) | async-done | bytes 2097168 | tf_op jit(solution)/shard_map/reduce_scatter | solution.py:477
  797.6 12.7 %collective-permute-done.38 = bf16[2,128,1152]{2,1,0:T(8,128)(2,1)S(1)} collective-permute-done((bf16[2,128,1152]{2,1,0:T(8,128)(2,1)S(1)}, bf16[2,128,1152]{2,1,0:T(8,128)(2,1)S(1)}, u32[]{:S(2)}, u32[]{:S(2)}) %collective-permute-start.38) | collective-permute-done | bytes 589856 | tf_op jit(solution)/shard_map/ppermute | solution.py:489
  837.9 17.4 %collective-permute-done.48 = bf16[64,1152]{1,0:T(8,128)(2,1)S(1)} collective-permute-done((bf16[64,1152]{1,0:T(8,128)(2,1)S(1)}, bf16[64,1152]{1,0:T(8,128)(2,1)S(1)}, u32[]{:S(2)}, u32[]{:S(2)}) %collective-permute-start.48) | collective-permute-done | bytes 147488 | tf_op jit(solution)/shard_map/ppermute | solution.py:365
  (407 shorter events, 451.6 us)
Async XLA Ops:
  7.2 121.8 %all-gather.5.cloned.1.call-start = ((), (), s32[]{:S(2)}) async-start(), calls=%async_computation.2 | async-start | bytes 5308416 | tf_op jit(solution)/shard_map/all_gather | solution.py:424
  26.3 179.2 %all-gather.7.cloned.1.call-start = ((), (), s32[]{:S(2)}) async-start(), calls=%async_computation.3 | async-start | bytes 18874368 | tf_op jit(solution)/shard_map/all_gather | solution.py:424
  30.8 35.0 %collective-permute-start.4 = (bf16[64,4096]{1,0:T(8,128)(2,1)}, bf16[64,4096]{1,0:T(8,128)(2,1)S(1)}, u32[]{:S(2)}, u32[]{:S(2)}) collective-permute-start(bf16[64,4096]{1,0:T(8,128)(2,1)} %after.33), channel_id=1, source_target_pairs={{0,2},{1,3},{2,0},{3,1},{4,6},{5,7},{6,4},{7,5},{8,10},{9,11},{10,... | collective-permute-start | bytes 1572872 | tf_op jit(solution)/shard_map/ppermute | solution.py:365
  67.3 284.7 %all-gather.11.cloned.1.call-start = ((), (), s32[]{:S(2)}) async-start(), calls=%async_computation.5 | async-start | bytes 9437184 | tf_op jit(solution)/shard_map/all_gather | solution.py:424
  70.1 281.9 %all-gather.9.cloned.1.call-start = ((), (), s32[]{:S(2)}) async-start(), calls=%async_computation.4 | async-start | bytes 18874368 | tf_op jit(solution)/shard_map/all_gather | solution.py:424
  125.9 558.2 %reduce-scatter.3.cloned.1.call-start = ((), (), s32[]{:S(2)}) async-start(), calls=%async_computation.6 | async-start | bytes 15728640 | tf_op jit(solution)/shard_map/reduce_scatter | solution.py:477
  187.9 57.6 %collective-permute-start.12 = (bf16[256,2048]{1,0:T(8,128)(2,1)}, bf16[256,2048]{1,0:T(8,128)(2,1)}, u32[]{:S(2)}, u32[]{:S(2)}) collective-permute-start(bf16[256,2048]{1,0:T(8,128)(2,1)} %after.38), channel_id=1, source_target_pairs={{0,1},{1,2},{2,3},{3,0},{4,5},{5,6},{6,7},{7,4},{8,9},{9,10},{10,1... | collective-permute-start | bytes 3145736 | tf_op jit(solution)/shard_map/ppermute | solution.py:365
  200.7 60.1 %collective-permute-start.13 = (bf16[256,2048]{1,0:T(8,128)(2,1)}, bf16[256,2048]{1,0:T(8,128)(2,1)}, u32[]{:S(2)}, u32[]{:S(2)}) collective-permute-start(bf16[256,2048]{1,0:T(8,128)(2,1)} %after.38), channel_id=1, source_target_pairs={{0,2},{1,3},{2,0},{3,1},{4,6},{5,7},{6,4},{7,5},{8,10},{9,11},{10,... | collective-permute-start | bytes 3145736 | tf_op jit(solution)/shard_map/ppermute | solution.py:365
  202.5 66.0 %collective-permute-start.14 = (bf16[256,2048]{1,0:T(8,128)(2,1)}, bf16[256,2048]{1,0:T(8,128)(2,1)}, u32[]{:S(2)}, u32[]{:S(2)}) collective-permute-start(bf16[256,2048]{1,0:T(8,128)(2,1)} %after.38), channel_id=1, source_target_pairs={{0,3},{1,0},{2,1},{3,2},{4,7},{5,4},{6,5},{7,6},{8,11},{9,8},{10,9... | collective-permute-start | bytes 3145736 | tf_op jit(solution)/shard_map/ppermute | solution.py:365
  268.5 48.8 %collective-permute-start.15 = (bf16[256,2048]{1,0:T(8,128)(2,1)}, bf16[256,2048]{1,0:T(8,128)(2,1)}, u32[]{:S(2)}, u32[]{:S(2)}) collective-permute-start(bf16[256,2048]{1,0:T(8,128)(2,1)} %after.39), channel_id=1, source_target_pairs={{0,1},{1,2},{2,3},{4,5},{5,6},{6,7},{8,9},{9,10},{10,11},{12,13},{... | collective-permute-start | bytes 3145736 | tf_op jit(solution)/shard_map/ppermute | solution.py:361
  327.8 59.8 %collective-permute-start.20 = (bf16[256,2048]{1,0:T(8,128)(2,1)}, bf16[256,2048]{1,0:T(8,128)(2,1)}, u32[]{:S(2)}, u32[]{:S(2)}) collective-permute-start(bf16[256,2048]{1,0:T(8,128)(2,1)} %collective-permute-done.16), channel_id=1, source_target_pairs={{2,3},{6,7},{10,11},{14,15},{18,19},{22,23},{26,27},{30,31}} | collective-permute-start | bytes 3145736 | tf_op jit(solution)/shard_map/ppermute | solution.py:361
  347.6 41.4 %collective-permute-start.19 = (bf16[256,2048]{1,0:T(8,128)(2,1)}, bf16[256,2048]{1,0:T(8,128)(2,1)}, u32[]{:S(2)}, u32[]{:S(2)}) collective-permute-start(bf16[256,2048]{1,0:T(8,128)(2,1)} %collective-permute-done.18), channel_id=1, source_target_pairs={{1,0},{5,4},{9,8},{13,12},{17,16},{21,20},{25,24},{29,28}} | collective-permute-start | bytes 3145736 | tf_op jit(solution)/shard_map/ppermute | solution.py:361
  493.7 40.6 %collective-permute-start.29 = (bf16[3072,2048]{1,0:T(8,128)(2,1)}, bf16[3072,2048]{1,0:T(8,128)(2,1)}, u32[]{:S(2)}, u32[]{:S(2)}) collective-permute-start(bf16[3072,2048]{1,0:T(8,128)(2,1)} %after.48), channel_id=1, source_target_pairs={{0,4},{4,0},{1,5},{5,1},{2,6},{6,2},{3,7},{7,3},{8,12},{12,8},{9,1... | collective-permute-start | bytes 37748744 | tf_op jit(solution)/shard_map/ppermute | solution.py:462
  558.9 217.7 %reduce-scatter.5.cloned.1.call-start = ((), (), s32[]{:S(2)}) async-start(), calls=%async_computation.7 | async-start | bytes 10485760 | tf_op jit(solution)/shard_map/reduce_scatter | solution.py:477
  588.0 37.6 %collective-permute-start.28 = (bf16[256,2048]{1,0:T(8,128)(2,1)}, bf16[256,2048]{1,0:T(8,128)(2,1)}, u32[]{:S(2)}, u32[]{:S(2)}) collective-permute-start(bf16[256,2048]{1,0:T(8,128)(2,1)} %get-tuple-element.59.refs_1_), channel_id=1, source_target_pairs={{0,1},{1,2},{4,5},{5,6},{8,9},{9,10},{12,13},{13,14},{16,17},{17,1... | collective-permute-start | bytes 3145736 | tf_op jit(solution)/shard_map/ppermute | solution.py:361
  687.0 43.3 %collective-permute-start.35 = (bf16[128,2048]{1,0:T(8,128)(2,1)}, bf16[128,2048]{1,0:T(8,128)(2,1)}, u32[]{:S(2)}, u32[]{:S(2)}) collective-permute-start(bf16[128,2048]{1,0:T(8,128)(2,1)} %bitcast.31), channel_id=1, source_target_pairs={{0,2},{1,3},{2,0},{3,1},{4,6},{5,7},{6,4},{7,5},{8,10},{9,11},{10,... | collective-permute-start | bytes 1572872 | tf_op jit(solution)/shard_map/ppermute | solution.py:365
  698.7 180.6 %collective-permute-start.45 = (bf16[256,2048]{1,0:T(8,128)(2,1)}, bf16[256,2048]{1,0:T(8,128)(2,1)}, u32[]{:S(2)}, u32[]{:S(2)}) collective-permute-start(bf16[256,2048]{1,0:T(8,128)(2,1)} %get-tuple-element.58.refs_2_), channel_id=1, source_target_pairs={{1,0},{2,1},{3,2},{5,4},{6,5},{7,6},{9,8},{10,9},{11,10},{13,12},{... | collective-permute-start | bytes 3145736 | tf_op jit(solution)/shard_map/ppermute | solution.py:361
  708.5 45.6 %collective-permute-start.39 = (bf16[128,2048]{1,0:T(8,128)(2,1)}, bf16[128,2048]{1,0:T(8,128)(2,1)}, u32[]{:S(2)}, u32[]{:S(2)}) collective-permute-start(bf16[128,2048]{1,0:T(8,128)(2,1)} %bitcast.39), channel_id=1, source_target_pairs={{0,1},{1,2},{2,3},{3,0},{4,5},{5,6},{6,7},{7,4},{8,9},{9,10},{10,1... | collective-permute-start | bytes 1572872 | tf_op jit(solution)/shard_map/ppermute | solution.py:365
  710.9 51.2 %collective-permute-start.40 = (bf16[128,2048]{1,0:T(8,128)(2,1)}, bf16[128,2048]{1,0:T(8,128)(2,1)}, u32[]{:S(2)}, u32[]{:S(2)}) collective-permute-start(bf16[128,2048]{1,0:T(8,128)(2,1)} %bitcast.40), channel_id=1, source_target_pairs={{0,3},{1,0},{2,1},{3,2},{4,7},{5,4},{6,5},{7,6},{8,11},{9,8},{10,9... | collective-permute-start | bytes 1572872 | tf_op jit(solution)/shard_map/ppermute | solution.py:365
  736.1 42.3 %collective-permute-start.36 = (bf16[1024,1024]{1,0:T(8,128)(2,1)}, bf16[1024,1024]{1,0:T(8,128)(2,1)}, u32[]{:S(2)}, u32[]{:S(2)}) collective-permute-start(bf16[1024,1024]{1,0:T(8,128)(2,1)} %convolution_convert_fusion.2), channel_id=1, source_target_pairs={{0,4},{4,0},{1,5},{5,1},{2,6},{6,2},{3,7},{7,3},{8,12},{12,8},{9,1... | collective-permute-start | bytes 6291464 | tf_op jit(solution)/shard_map/ppermute | solution.py:449
  783.5 47.0 %collective-permute-start.52 = (bf16[128,2048]{1,0:T(8,128)(2,1)}, bf16[128,2048]{1,0:T(8,128)(2,1)}, u32[]{:S(2)}, u32[]{:S(2)}) collective-permute-start(bf16[128,2048]{1,0:T(8,128)(2,1)} %get-tuple-element.53), channel_id=1, source_target_pairs={{0,3},{1,0},{2,1},{3,2},{4,7},{5,4},{6,5},{7,6},{8,11},{9,8},{10,9... | collective-permute-start | bytes 1572872 | tf_op jit(solution)/shard_map/ppermute | solution.py:365
  786.8 48.0 %collective-permute-start.51 = (bf16[128,2048]{1,0:T(8,128)(2,1)}, bf16[128,2048]{1,0:T(8,128)(2,1)}, u32[]{:S(2)}, u32[]{:S(2)}) collective-permute-start(bf16[128,2048]{1,0:T(8,128)(2,1)} %get-tuple-element.54), channel_id=1, source_target_pairs={{0,2},{1,3},{2,0},{3,1},{4,6},{5,7},{6,4},{7,5},{8,10},{9,11},{10,... | collective-permute-start | bytes 1572872 | tf_op jit(solution)/shard_map/ppermute | solution.py:365
  786.8 48.0 %collective-permute-start.50 = (bf16[128,2048]{1,0:T(8,128)(2,1)}, bf16[128,2048]{1,0:T(8,128)(2,1)}, u32[]{:S(2)}, u32[]{:S(2)}) collective-permute-start(bf16[128,2048]{1,0:T(8,128)(2,1)} %get-tuple-element.52), channel_id=1, source_target_pairs={{0,1},{1,2},{2,3},{3,0},{4,5},{5,6},{6,7},{7,4},{8,9},{9,10},{10,1... | collective-permute-start | bytes 1572872 | tf_op jit(solution)/shard_map/ppermute | solution.py:365
  825.9 53.4 %collective-permute-start.44 = (bf16[256,2048]{1,0:T(8,128)(2,1)}, bf16[256,2048]{1,0:T(8,128)(2,1)}, u32[]{:S(2)}, u32[]{:S(2)}) collective-permute-start(bf16[256,2048]{1,0:T(8,128)(2,1)} %after.58), channel_id=1, source_target_pairs={{0,1},{1,2},{2,3},{4,5},{5,6},{6,7},{8,9},{9,10},{10,11},{12,13},{... | collective-permute-start | bytes 3145736 | tf_op jit(solution)/shard_map/ppermute | solution.py:361
  (98 other events, 1438.8 us)
Sparse Core Ops, SparseCore 0:
  26.4 41.2 all-gather.4
  70.1 98.2 all-gather.6
  170.3 54.3 all-gather.10
  227.0 89.8 all-gather.8
  559.0 125.0 reduce-scatter.2
  687.0 89.5 reduce-scatter.4

commit v3 on v2

--- a/solution.py
+++ b/solution.py
@@ -612,16 +612,23 @@
         if active:
             goal = after(goal, active[-1])
         group_active, grad_gate, grad_up = feed(tokens, goal, both_full, down_full)
-        second = feed_back(grad_gate, grad_up, both_full)
-        for k, r in enumerate(group):
-            second_slots[r] = second[k * entry_count : (k + 1) * entry_count]
         for kept, value in zip(
             (hidden, cot, active, gates, ups), (tokens, goal, group_active, grad_gate, grad_up)
         ):
             kept.append(value)
 
+    second = ()
+    for k in reversed(range(len(groups))):
+        if k < len(groups) - 1:
+            ups[k] = after(ups[k], second)
+        second = feed_back(gates[k], ups[k], both_full)
+        for i, r in enumerate(groups[k]):
+            second_slots[r] = second[i * entry_count : (i + 1) * entry_count]
+
     def down_terms(k, *tied):
-        down_out = dot(after(active[k], *tied), down_full, NN).astype(LOW)
+        if tied:
+            active[k] = after(active[k], *tied)
+        down_out = dot(active[k], down_full, NN).astype(LOW)
         for i, r in enumerate(groups[k]):
             down_slots[r] = down_out[i * entry_count : (i + 1) * entry_count]
         return down_out
@@ -638,7 +645,7 @@
     gates[0] = after(gates[0], *steps[min(1, n_ctx - 2)])
     feed_sent, feed_summed = group_terms([hidden, active], [gates, ups, cot], [0, 0, 1])
     if len(groups) > 1:
-        late = down_terms(0, *steps[-1])
+        late = down_terms(0)
         came = after(came[0], late), came[1]
     grad_second = second_slots[0].astype(WIDE) + came[0].astype(WIDE) + came[1].astype(WIDE)
     down_sent = tuple(
@@ -692,18 +699,16 @@
         [0, 1],
     )
     branch_terms = branch_summed([steps[-1]])
-    grad_pair = turn_pair(after(pair_grad, grad_slots[n_ctx // 2]), cosine, -sine)
+    grad_pair = turn_pair(after(pair_grad, grad_slots[1]), cosine, -sine)
     grad_first = dot(grad_query, query_full, NT) + dot(grad_pair, pair_weight, NT)
     first_gain_term = jnp.sum(grad_first * unit_first, axis=0)
     input_grad = (grad_residual + norm_back(tokens_wide, grad_first * gain_first)).astype(LOW)
 
     def ctx_rows_scatter(values, *earlier):
         parts = values.reshape(n_ctx, -1, values.shape[1])
-        total = pick(parts, me, 0).astype(WIDE)
-        for r in range(1, n_ctx):
-            came = rotate(pick(parts, lax.rem(me + r, n_ctx), 0), n_ctx, r)
-            total = total + (after(came, *earlier) if earlier else came).astype(WIDE)
-        return total
+        own = pick(parts, me, 0)
+        came = [rotate(pick(parts, lax.rem(me + r, n_ctx), 0), n_ctx, r) for r in range(1, n_ctx)]
+        return [own] + [after(values, *earlier) for values in came]
 
     branch_part = chip_scatter(branch_terms)
     gain_terms = jnp.pad(
@@ -718,15 +723,18 @@
         [core_summed(first_hidden, grad_pair), gain_part.reshape(-1, LANES)], 1
     )
     pair_sum = chip_scatter_steps(pair_terms, *grad_slots[1:])
-    pair_weight_grad = ctx_rows_scatter(pair_sum)
-    grad_slots[0] = after(grad_slots[0], pair_weight_grad)
+    branch_part = after(branch_part, pair_sum, *grad_slots[1:]).reshape(2, n_ctx, rows, width)
+    branch_part = branch_part.transpose(1, 0, 2, 3).reshape(n_ctx * 2 * rows, width)
+    total = lambda parts: sum(part.astype(WIDE) for part in parts)
+    arrived = ctx_rows_scatter(branch_part, pair_sum)
+    pair_weight_grad = total(ctx_rows_scatter(pair_sum, arrived[1]))
+    grad_slots[0] = after(grad_slots[0], arrived[1])
     both_grad = in_order(grad_slots, n_ctx, me).reshape(n_ctx, 2, rows, n_dp, hidden_rows)
     both_grad = both_grad.transpose(1, 2, 3, 0, 4).reshape(2, rows, hidden_units).astype(WIDE)
     gate_weight_grad, up_weight_grad = both_grad[0], both_grad[1]
-    branch_part = after(branch_part, *grad_slots[1:]).reshape(2, n_ctx, rows, width)
-    branch_part = branch_part.transpose(1, 0, 2, 3).reshape(n_ctx * 2 * rows, width)
-    branch_grad = ctx_rows_scatter(branch_part, pair_sum).reshape(2, rows, width)
-    down_sent = after(down_sent[0], pair_sum), down_sent[1]
+    arrived[2:] = [after(values, gate_weight_grad) for values in arrived[2:]]
+    branch_grad = total(arrived).reshape(2, rows, width)
+    down_sent = after(down_sent[0], pair_terms), down_sent[1]
     came = line_send(down_sent, n_ctx, n_ctx - 1)
     down_value = down_slots[0].astype(WIDE) + came[0].astype(WIDE) + came[1].astype(WIDE)
     block_output = (residual + down_value).astype(LOW)

time: 909 us -> 870 us (0.957)
  waiting for transfers between devices: 315 us -> 291 us
    ppermute x21, waiting for transfers between devices: 145 us -> 128 us  [rotate(): lax.ppermute(values, 'ctx', [(i, (i + step) % count) for i in range(count)])]
    reduce_scatter x2, waiting for transfers between devices: 24.6 us -> 10.1 us  [chip_scatter(): return lax.psum_scatter(values, CHIPS, scatter_dimension=0, tiled=True)]
    ppermute x1, waiting for transfers between devices: 12.7 us -> 22.8 us  [chip_scatter_steps(): top_came = lax.ppermute(pick(top, 1 - x, 1), 'x', SWAP)]
    unnamed x131 -> x147, local copies, waits for them, and re-layouts: 26 us -> 23.3 us
  transfers between devices with their start and end apart: 59 -> 59, of which waited for: 32 -> 26; matrix products, arithmetic and copies ran while one was open for 18% -> 18% of each run, Pallas kernels for 15% -> 15%
where the time goes in v3:
time: 870 us; the launch traced here: 860 us
  waiting for transfers between devices  291 us (33%)
  Pallas kernels  191 us (22%)
  starting transfers between devices  166 us (19%)
  other arithmetic  71.3 us (8%)
  matrix products  62.7 us (7%)
  local copies, waits for them, and re-layouts  61.4 us (7%)
  between operations  16 us (2%)
    ppermute x21, waiting for transfers between devices, rotate(): lax.ppermute(values, 'ctx', [(i, (i + step) % count) for i in range(count)])  128 us
    ppermute x24, waiting for transfers between devices, shift(): return lax.ppermute(values, 'ctx', pairs)  95.7 us
    ppermute x24, starting transfers between devices, shift(): return lax.ppermute(values, 'ctx', pairs)  91.3 us
    ppermute x21, starting transfers between devices, rotate(): lax.ppermute(values, 'ctx', [(i, (i + step) % count) for i in range(count)])  69.4 us
    pallas_call x4, Pallas kernels, weight_rows(): pl.pallas_call(lambda *refs: weight_kernel(shared, parts, *refs), grid_sp...  68.6 us
    dot_general x10, matrix products, dot(): return lax.dot_general(left, right, dims, preferred_element_type=WIDE)  62.7 us
    pallas_call x2, Pallas kernels, feed(): pl.pallas_call(feed_kernel, grid=(steps,), in_specs=[whole, whole, pl.Blo...  40.7 us
    pallas_call x2, Pallas kernels, feed_back(): pl.pallas_call(second_kernel, grid=(width // FEED_STEP,), in_specs=[whole...  30.6 us
  transfers between devices with their start and end apart: 59, of which 26 were waited for; matrix products, arithmetic and copies ran while one was open for 18% of the time, Pallas kernels for 15%

profile of v3, /device:TPU:0, one launch (start us, length us, event | category | flops | bytes accessed | tf_op | source)
XLA Modules:
  0.0 860.2 jit_solution(6802534425099452723)
XLA Ops:
  33.5 11.7 %collective-permute-done.3 = bf16[64,4096]{1,0:T(8,128)(2,1)S(1)} collective-permute-done((bf16[64,4096]{1,0:T(8,128)(2,1)}, bf16[64,4096]{1,0:T(8,128)(2,1)S(1)}, u32[]{:S(2)}, u32[]{:S(2)}) %collective-permute-start.3) | collective-permute-done | bytes 524320 | tf_op jit(solution)/shard_map/ppermute | solution.py:365
  45.2 20.6 %collective-permute-done.4 = bf16[64,4096]{1,0:T(8,128)(2,1)S(1)} collective-permute-done((bf16[64,4096]{1,0:T(8,128)(2,1)}, bf16[64,4096]{1,0:T(8,128)(2,1)S(1)}, u32[]{:S(2)}, u32[]{:S(2)}) %collective-permute-start.4) | collective-permute-done | bytes 524320 | tf_op jit(solution)/shard_map/ppermute | solution.py:365
  76.6 11.6 %collective-permute-start.6 = (bf16[64,4096]{1,0:T(8,128)(2,1)}, bf16[64,4096]{1,0:T(8,128)(2,1)S(1)}, u32[]{:S(2)}, u32[]{:S(2)}) collective-permute-start(bf16[64,4096]{1,0:T(8,128)(2,1)} %after.39), channel_id=1, source_target_pairs={{0,1},{1,2},{2,3},{3,0},{4,5},{5,6},{6,7},{7,4},{8,9},{9,10},{10,1... | collective-permute-start | bytes 1572872 | tf_op jit(solution)/shard_map/ppermute | solution.py:365
  103.2 21.2 %collective-permute-done.7 = bf16[64,4096]{1,0:T(8,128)(2,1)S(1)} collective-permute-done((bf16[64,4096]{1,0:T(8,128)(2,1)}, bf16[64,4096]{1,0:T(8,128)(2,1)S(1)}, u32[]{:S(2)}, u32[]{:S(2)}) %collective-permute-start.7) | collective-permute-done | bytes 524320 | tf_op jit(solution)/shard_map/ppermute | solution.py:365
  138.6 14.2 %collective-permute-start.11 = (bf16[256,1024]{1,0:T(8,128)(2,1)}, bf16[256,1024]{1,0:T(8,128)(2,1)S(1)}, u32[]{:S(2)}, u32[]{:S(2)}) collective-permute-start(bf16[256,1024]{1,0:T(8,128)(2,1)} %after.42), channel_id=1, source_target_pairs={{0,3},{4,7},{8,11},{12,15},{16,19},{20,23},{24,27},{28,31}} | collective-permute-start | bytes 1572872 | tf_op jit(solution)/shard_map/ppermute | solution.py:361
  165.5 11.2 %collective-permute-done.10 = bf16[256,1024]{1,0:T(8,128)(2,1)S(1)} collective-permute-done((bf16[256,1024]{1,0:T(8,128)(2,1)}, bf16[256,1024]{1,0:T(8,128)(2,1)S(1)}, u32[]{:S(2)}, u32[]{:S(2)}) %collective-permute-start.10) | collective-permute-done | bytes 524320 | tf_op jit(solution)/shard_map/ppermute | solution.py:361
  187.9 12.7 %collective-permute-start.12 = (bf16[256,2048]{1,0:T(8,128)(2,1)}, bf16[256,2048]{1,0:T(8,128)(2,1)}, u32[]{:S(2)}, u32[]{:S(2)}) collective-permute-start(bf16[256,2048]{1,0:T(8,128)(2,1)} %after.43), channel_id=1, source_target_pairs={{0,1},{1,2},{2,3},{3,0},{4,5},{5,6},{6,7},{7,4},{8,9},{9,10},{10,1... | collective-permute-start | bytes 3145736 | tf_op jit(solution)/shard_map/ppermute | solution.py:365
  211.7 23.8 %attend.1 = (bf16[256,2048]{1,0:T(8,128)(2,1)S(1)}, bf16[256,2048]{1,0:T(8,128)(2,1)S(1)}, f32[32,256]{1,0:T(8,128)S(1)}) custom-call(f32[256,2048]{1,0:T(8,128)S(1)} %fusion.6.raw_ref, f32[256,128]{1,0:T(8,128)S(1)} %copy-done.8, f32[256,128]{1,0:T(8,128)S(1)} %copy-done.9, bf16[1024,1024]{1,0:T(8,128)(2,1)S(1)} %copy-done, bf16[1024,1024]{1,0:T(8,128)(2,1)S(1)} %copy-done, ...), custom_call_target="tpu_custom_call" | custom-call | flops 1000000 | bytes 1000000 | tf_op jit(solution)/shard_map/attend/pallas_call | solution.py:319
  245.4 15.4 %collective-permute-done.13.refs_2_ = bf16[256,2048]{1,0:T(8,128)(2,1)} collective-permute-done((bf16[256,2048]{1,0:T(8,128)(2,1)}, bf16[256,2048]{1,0:T(8,128)(2,1)}, u32[]{:S(2)}, u32[]{:S(2)}) %collective-permute-start.13) | collective-permute-done | bytes 1048608 | tf_op jit(solution)/shard_map/ppermute | solution.py:365
  268.5 27.7 %collective-permute-start.15 = (bf16[256,2048]{1,0:T(8,128)(2,1)}, bf16[256,2048]{1,0:T(8,128)(2,1)}, u32[]{:S(2)}, u32[]{:S(2)}) collective-permute-start(bf16[256,2048]{1,0:T(8,128)(2,1)} %after.44), channel_id=1, source_target_pairs={{0,1},{1,2},{2,3},{4,5},{5,6},{6,7},{8,9},{9,10},{10,11},{12,13},{... | collective-permute-start | bytes 3145736 | tf_op jit(solution)/shard_map/ppermute | solution.py:361
  297.5 19.8 %collective-permute-done.15 = bf16[256,2048]{1,0:T(8,128)(2,1)} collective-permute-done((bf16[256,2048]{1,0:T(8,128)(2,1)}, bf16[256,2048]{1,0:T(8,128)(2,1)}, u32[]{:S(2)}, u32[]{:S(2)}) %collective-permute-start.15) | collective-permute-done | bytes 1048608 | tf_op jit(solution)/shard_map/ppermute | solution.py:361
  331.8 15.8 %collective-permute-done.18 = bf16[256,2048]{1,0:T(8,128)(2,1)} collective-permute-done((bf16[256,2048]{1,0:T(8,128)(2,1)}, bf16[256,2048]{1,0:T(8,128)(2,1)}, u32[]{:S(2)}, u32[]{:S(2)}) %collective-permute-start.18) | collective-permute-done | bytes 1048608 | tf_op jit(solution)/shard_map/ppermute | solution.py:361
  352.1 20.3 %feed.2 = (bf16[512,2048]{1,0:T(8,128)(2,1)}, bf16[512,2048]{1,0:T(8,128)(2,1)}, bf16[512,2048]{1,0:T(8,128)(2,1)}) custom-call(bf16[512,2048]{1,0:T(8,128)(2,1)} %pad_maximum_fusion.2.token_ref.refs_1_, bf16[512,2048]{1,0:T(8,128)(2,1)} %constant_dynamic-update-slice_fusion.1.goal_ref.refs_9_, ...), custom_call_target="tpu_custom_call" | custom-call | flops 1000000 | bytes 1000000 | tf_op jit(solution)/shard_map/feed/pallas_call | solution.py:207
  376.7 20.4 %feed.3 = (bf16[512,2048]{1,0:T(8,128)(2,1)}, bf16[512,2048]{1,0:T(8,128)(2,1)}, bf16[512,2048]{1,0:T(8,128)(2,1)}) custom-call(bf16[512,2048]{1,0:T(8,128)(2,1)} %pad_maximum_fusion.3.token_ref.refs_2_, bf16[512,2048]{1,0:T(8,128)(2,1)} %after.46.goal_ref.refs_10_, bf16[2048,4096]{1,0:T(8,128)(2,1)} %all-gather.9.cloned.1.call-done.gate_ref.up_ref, ...), custom_call_target="tpu_custom_call" | custom-call | flops 1000000 | bytes 1000000 | tf_op jit(solution)/shard_map/feed/pallas_call | solution.py:207
  397.1 15.2 %feed_back.2.refs_1_ = bf16[512,2048]{1,0:T(8,128)(2,1)} custom-call(bf16[512,2048]{1,0:T(8,128)(2,1)} %get-tuple-element.26.grad_gate_ref.refs_6_, bf16[512,2048]{1,0:T(8,128)(2,1)} %get-tuple-element.27.grad_up_ref.refs_8_, bf16[2048,4096]{1,0:T(8,128)(2,1)} %all-gather.9.cloned.1.call-done.gate_ref.up_ref, ...), custom_call_target="tpu_custom_call" | custom-call | flops 1000000 | bytes 1000000 | tf_op jit(solution)/shard_map/feed_back/pallas_call | solution.py:229
  423.6 15.3 %feed_back.3 = bf16[512,2048]{1,0:T(8,128)(2,1)} custom-call(bf16[512,2048]{1,0:T(8,128)(2,1)} %get-tuple-element.28.grad_gate_ref.refs_0_, bf16[512,2048]{1,0:T(8,128)(2,1)} %after.48.grad_up_ref.refs_7_, bf16[2048,4096]{1,0:T(8,128)(2,1)} %all-gather.9.cloned.1.call-done.gate_ref.up_ref, bf16[2048,4096]{1,0:T(8,128)(2,1)} %all-gather.9.cloned.1.call-done.gate_ref.up_ref), custom_call_target="tpu_custom_call" | custom-call | flops 1000000 | bytes 1000000 | tf_op jit(solution)/shard_map/feed_back/pallas_call | solution.py:229
  456.1 23.0 %weight_rows.4.refs_0_ = bf16[3072,2048]{1,0:T(8,128)(2,1)} custom-call(s32[1]{0:T(128)} %bitcast.29.refs_0_, bf16[512,2048]{1,0:T(8,128)(2,1)} %pad_maximum_fusion.2.token_ref.refs_1_, bf16[512,2048]{1,0:T(8,128)(2,1)} %pad_maximum_fusion.3.token_ref.refs_2_, bf16[512,2048]{1,0:T(8,128)(2,1)} %get-tuple-element.24.refs_1_.refs_3_, ...), custom_call_target="tpu_custom_call" | custom-call | flops 12884901888 | bytes 12582912 | tf_op jit(solution)/shard_map/weight_rows/pallas_call | solution.py:274
  516.3 24.5 %weight_rows.5.refs_1_ = bf16[3072,2048]{1,0:T(8,128)(2,1)} custom-call(s32[1]{0:T(128)} %bitcast.28.refs_0_, bf16[512,2048]{1,0:T(8,128)(2,1)} %pad_maximum_fusion.2.token_ref.refs_1_, bf16[512,2048]{1,0:T(8,128)(2,1)} %pad_maximum_fusion.3.token_ref.refs_2_, bf16[512,2048]{1,0:T(8,128)(2,1)} %get-tuple-element.24.refs_1_.refs_3_, ...), custom_call_target="tpu_custom_call" | custom-call | flops 12884901888 | bytes 12582912 | tf_op jit(solution)/shard_map/weight_rows/pallas_call | solution.py:274
  581.7 22.6 %attend_back.1 = (bf16[256,2048]{1,0:T(8,128)(2,1)S(1)}, bf16[1024,512]{1,0:T(8,128)(2,1)S(1)}, bf16[1024,512]{1,0:T(8,128)(2,1)S(1)}) custom-call(bf16[256,2048]{1,0:T(8,128)(2,1)S(1)} %copy-done.15, f32[256,128]{1,0:T(8,128)S(1)} %copy-done.8, f32[256,128]{1,0:T(8,128)S(1)} %copy-done.9, bf16[1024,1024]{1,0:T(8,128)(2,1)S(1)} %copy-done, ...), custom_call_target="tpu_custom_call" | custom-call | flops 24000000000 | bytes 10000000 | tf_op jit(solution)/shard_map/attend_back/pallas_call | solution.py:341
  628.9 13.5 %collective-permute-done.47.refs_5_ = bf16[2048,2048]{1,0:T(8,128)(2,1)} collective-permute-done((bf16[2048,2048]{1,0:T(8,128)(2,1)}, bf16[2048,2048]{1,0:T(8,128)(2,1)}, u32[]{:S(2)}, u32[]{:S(2)}) %collective-permute-start.47) | collective-permute-done | bytes 8388640 | tf_op jit(solution)/shard_map/ppermute | solution.py:462
  642.4 11.9 %weight_rows.7 = bf16[2048,2048]{1,0:T(8,128)(2,1)} custom-call(s32[1]{0:T(128)} %bitcast.28.refs_0_, bf16[256,2048]{1,0:T(8,128)(2,1)} %copy-done.4, bf16[256,2048]{1,0:T(8,128)(2,1)} %copy-done.28, bf16[256,2048]{1,0:T(8,128)(2,1)} %after.64.refs_3_, bf16[256,2048]{1,0:T(8,128)(2,1)} %copy-done.1, bf16[2048,2048]{1,0:T(8,128)(2,1)} %collective-permute-done.47.refs_5_), custom_call_target="tpu_custom_call" | custom-call | flops 2147483648 | bytes 8388608 | tf_op jit(solution)/shard_map/weight_rows/pallas_call | solution.py:274
  732.1 15.3 %collective-permute-done.44 = bf16[2,128,1152]{2,1,0:T(8,128)(2,1)} collective-permute-done((bf16[2,128,1152]{2,1,0:T(8,128)(2,1)}, bf16[2,128,1152]{2,1,0:T(8,128)(2,1)}, u32[]{:S(2)}, u32[]{:S(2)}) %collective-permute-start.44) | collective-permute-done | bytes 589856 | tf_op jit(solution)/shard_map/ppermute | solution.py:490
  750.2 22.8 %collective-permute-done.40 = bf16[2,128,1152]{2,1,0:T(8,128)(2,1)S(1)} collective-permute-done((bf16[2,128,1152]{2,1,0:T(8,128)(2,1)S(1)}, bf16[2,128,1152]{2,1,0:T(8,128)(2,1)S(1)}, u32[]{:S(2)}, u32[]{:S(2)}) %collective-permute-start.40) | collective-permute-done | bytes 589856 | tf_op jit(solution)/shard_map/ppermute | solution.py:489
  824.4 21.4 %collective-permute-done.51.refs_0_ = bf16[128,2048]{1,0:T(8,128)(2,1)S(1)} collective-permute-done((bf16[128,2048]{1,0:T(8,128)(2,1)}, bf16[128,2048]{1,0:T(8,128)(2,1)S(1)}, u32[]{:S(2)}, u32[]{:S(2)}) %collective-permute-start.51) | collective-permute-done | bytes 524320 | tf_op jit(solution)/shard_map/ppermute | solution.py:365
  (429 shorter events, 412.1 us)
Async XLA Ops:
  7.2 121.8 %all-gather.5.cloned.1.call-start = ((), (), s32[]{:S(2)}) async-start(), calls=%async_computation.2 | async-start | bytes 5308416 | tf_op jit(solution)/shard_map/all_gather | solution.py:424
  26.3 179.2 %all-gather.7.cloned.1.call-start = ((), (), s32[]{:S(2)}) async-start(), calls=%async_computation.3 | async-start | bytes 18874368 | tf_op jit(solution)/shard_map/all_gather | solution.py:424
  30.8 35.0 %collective-permute-start.4 = (bf16[64,4096]{1,0:T(8,128)(2,1)}, bf16[64,4096]{1,0:T(8,128)(2,1)S(1)}, u32[]{:S(2)}, u32[]{:S(2)}) collective-permute-start(bf16[64,4096]{1,0:T(8,128)(2,1)} %after.38), channel_id=1, source_target_pairs={{0,2},{1,3},{2,0},{3,1},{4,6},{5,7},{6,4},{7,5},{8,10},{9,11},{10,... | collective-permute-start | bytes 1572872 | tf_op jit(solution)/shard_map/ppermute | solution.py:365
  32.5 33.4 %collective-permute-start.5 = (bf16[64,4096]{1,0:T(8,128)(2,1)}, bf16[64,4096]{1,0:T(8,128)(2,1)S(1)}, u32[]{:S(2)}, u32[]{:S(2)}) collective-permute-start(bf16[64,4096]{1,0:T(8,128)(2,1)} %after.38), channel_id=1, source_target_pairs={{0,3},{1,0},{2,1},{3,2},{4,7},{5,4},{6,5},{7,6},{8,11},{9,8},{10,9... | collective-permute-start | bytes 1572872 | tf_op jit(solution)/shard_map/ppermute | solution.py:365
  67.3 284.8 %all-gather.11.cloned.1.call-start = ((), (), s32[]{:S(2)}) async-start(), calls=%async_computation.5 | async-start | bytes 9437184 | tf_op jit(solution)/shard_map/all_gather | solution.py:424
  70.1 282.0 %all-gather.9.cloned.1.call-start = ((), (), s32[]{:S(2)}) async-start(), calls=%async_computation.4 | async-start | bytes 18874368 | tf_op jit(solution)/shard_map/all_gather | solution.py:424
  90.9 33.5 %collective-permute-start.7 = (bf16[64,4096]{1,0:T(8,128)(2,1)}, bf16[64,4096]{1,0:T(8,128)(2,1)S(1)}, u32[]{:S(2)}, u32[]{:S(2)}) collective-permute-start(bf16[64,4096]{1,0:T(8,128)(2,1)} %after.40), channel_id=1, source_target_pairs={{0,2},{1,3},{2,0},{3,1},{4,6},{5,7},{6,4},{7,5},{8,10},{9,11},{10,... | collective-permute-start | bytes 1572872 | tf_op jit(solution)/shard_map/ppermute | solution.py:365
  125.9 539.9 %reduce-scatter.3.cloned.1.call-start = ((), (), s32[]{:S(2)}) async-start(), calls=%async_computation.6 | async-start | bytes 15728640 | tf_op jit(solution)/shard_map/reduce_scatter | solution.py:477
  187.9 57.5 %collective-permute-start.12 = (bf16[256,2048]{1,0:T(8,128)(2,1)}, bf16[256,2048]{1,0:T(8,128)(2,1)}, u32[]{:S(2)}, u32[]{:S(2)}) collective-permute-start(bf16[256,2048]{1,0:T(8,128)(2,1)} %after.43), channel_id=1, source_target_pairs={{0,1},{1,2},{2,3},{3,0},{4,5},{5,6},{6,7},{7,4},{8,9},{9,10},{10,1... | collective-permute-start | bytes 3145736 | tf_op jit(solution)/shard_map/ppermute | solution.py:365
  200.7 60.1 %collective-permute-start.13 = (bf16[256,2048]{1,0:T(8,128)(2,1)}, bf16[256,2048]{1,0:T(8,128)(2,1)}, u32[]{:S(2)}, u32[]{:S(2)}) collective-permute-start(bf16[256,2048]{1,0:T(8,128)(2,1)} %after.43), channel_id=1, source_target_pairs={{0,2},{1,3},{2,0},{3,1},{4,6},{5,7},{6,4},{7,5},{8,10},{9,11},{10,... | collective-permute-start | bytes 3145736 | tf_op jit(solution)/shard_map/ppermute | solution.py:365
  202.5 66.0 %collective-permute-start.14 = (bf16[256,2048]{1,0:T(8,128)(2,1)}, bf16[256,2048]{1,0:T(8,128)(2,1)}, u32[]{:S(2)}, u32[]{:S(2)}) collective-permute-start(bf16[256,2048]{1,0:T(8,128)(2,1)} %after.43), channel_id=1, source_target_pairs={{0,3},{1,0},{2,1},{3,2},{4,7},{5,4},{6,5},{7,6},{8,11},{9,8},{10,9... | collective-permute-start | bytes 3145736 | tf_op jit(solution)/shard_map/ppermute | solution.py:365
  268.5 48.8 %collective-permute-start.15 = (bf16[256,2048]{1,0:T(8,128)(2,1)}, bf16[256,2048]{1,0:T(8,128)(2,1)}, u32[]{:S(2)}, u32[]{:S(2)}) collective-permute-start(bf16[256,2048]{1,0:T(8,128)(2,1)} %after.44), channel_id=1, source_target_pairs={{0,1},{1,2},{2,3},{4,5},{5,6},{6,7},{8,9},{9,10},{10,11},{12,13},{... | collective-permute-start | bytes 3145736 | tf_op jit(solution)/shard_map/ppermute | solution.py:361
  327.8 44.6 %collective-permute-start.20 = (bf16[256,2048]{1,0:T(8,128)(2,1)}, bf16[256,2048]{1,0:T(8,128)(2,1)}, u32[]{:S(2)}, u32[]{:S(2)}) collective-permute-start(bf16[256,2048]{1,0:T(8,128)(2,1)} %collective-permute-done.16), channel_id=1, source_target_pairs={{2,3},{6,7},{10,11},{14,15},{18,19},{22,23},{26,27},{30,31}} | collective-permute-start | bytes 3145736 | tf_op jit(solution)/shard_map/ppermute | solution.py:361
  415.4 32.7 %collective-permute-start.21 = (bf16[256,2048]{1,0:T(8,128)(2,1)}, bf16[256,2048]{1,0:T(8,128)(2,1)}, u32[]{:S(2)}, u32[]{:S(2)}) collective-permute-start(bf16[256,2048]{1,0:T(8,128)(2,1)} %get-tuple-element.68.refs_1_), channel_id=1, source_target_pairs={{0,1},{4,5},{8,9},{12,13},{16,17},{20,21},{24,25},{28,29}} | collective-permute-start | bytes 3145736 | tf_op jit(solution)/shard_map/ppermute | solution.py:361
  482.9 33.5 %collective-permute-start.29 = (bf16[3072,2048]{1,0:T(8,128)(2,1)}, bf16[3072,2048]{1,0:T(8,128)(2,1)}, u32[]{:S(2)}, u32[]{:S(2)}) collective-permute-start(bf16[3072,2048]{1,0:T(8,128)(2,1)} %after.53), channel_id=1, source_target_pairs={{0,4},{4,0},{1,5},{5,1},{2,6},{6,2},{3,7},{7,3},{8,12},{12,8},{9,1... | collective-permute-start | bytes 37748744 | tf_op jit(solution)/shard_map/ppermute | solution.py:462
  540.9 244.1 %reduce-scatter.5.cloned.1.call-start = ((), (), s32[]{:S(2)}) async-start(), calls=%async_computation.7 | async-start | bytes 10485760 | tf_op jit(solution)/shard_map/reduce_scatter | solution.py:477
  569.6 37.6 %collective-permute-start.28 = (bf16[256,2048]{1,0:T(8,128)(2,1)}, bf16[256,2048]{1,0:T(8,128)(2,1)}, u32[]{:S(2)}, u32[]{:S(2)}) collective-permute-start(bf16[256,2048]{1,0:T(8,128)(2,1)} %get-tuple-element.59.refs_1_), channel_id=1, source_target_pairs={{0,1},{1,2},{4,5},{5,6},{8,9},{9,10},{12,13},{13,14},{16,17},{17,1... | collective-permute-start | bytes 3145736 | tf_op jit(solution)/shard_map/ppermute | solution.py:361
  654.4 33.7 %collective-permute-start.34 = (bf16[256,1024]{1,0:T(8,128)(2,1)}, bf16[256,1024]{1,0:T(8,128)(2,1)}, u32[]{:S(2)}, u32[]{:S(2)}) collective-permute-start(bf16[256,1024]{1,0:T(8,128)(2,1)} %add_convert_fusion.6.refs_1_), channel_id=1, source_target_pairs={{1,0},{2,1},{3,2},{5,4},{6,5},{7,6},{9,8},{10,9},{11,10},{13,12},{... | collective-permute-start | bytes 1572872 | tf_op jit(solution)/shard_map/ppermute | solution.py:361
  668.7 33.3 %collective-permute-start.35 = (bf16[128,2048]{1,0:T(8,128)(2,1)}, bf16[128,2048]{1,0:T(8,128)(2,1)}, u32[]{:S(2)}, u32[]{:S(2)}) collective-permute-start(bf16[128,2048]{1,0:T(8,128)(2,1)} %bitcast.31), channel_id=1, source_target_pairs={{0,1},{1,2},{2,3},{3,0},{4,5},{5,6},{6,7},{7,4},{8,9},{9,10},{10,1... | collective-permute-start | bytes 1572872 | tf_op jit(solution)/shard_map/ppermute | solution.py:365
  679.0 111.6 %collective-permute-start.39 = (bf16[256,2048]{1,0:T(8,128)(2,1)}, bf16[256,2048]{1,0:T(8,128)(2,1)}, u32[]{:S(2)}, u32[]{:S(2)}) collective-permute-start(bf16[256,2048]{1,0:T(8,128)(2,1)} %get-tuple-element.58.refs_2_), channel_id=1, source_target_pairs={{1,0},{2,1},{3,2},{5,4},{6,5},{7,6},{9,8},{10,9},{11,10},{13,12},{... | collective-permute-start | bytes 3145736 | tf_op jit(solution)/shard_map/ppermute | solution.py:361
  690.2 84.1 %collective-permute-start.41 = (bf16[128,2048]{1,0:T(8,128)(2,1)}, bf16[128,2048]{1,0:T(8,128)(2,1)}, u32[]{:S(2)}, u32[]{:S(2)}) collective-permute-start(bf16[128,2048]{1,0:T(8,128)(2,1)} %bitcast.40), channel_id=1, source_target_pairs={{0,2},{1,3},{2,0},{3,1},{4,6},{5,7},{6,4},{7,5},{8,10},{9,11},{10,... | collective-permute-start | bytes 1572872 | tf_op jit(solution)/shard_map/ppermute | solution.py:365
  693.5 80.8 %collective-permute-start.42 = (bf16[128,2048]{1,0:T(8,128)(2,1)}, bf16[128,2048]{1,0:T(8,128)(2,1)}, u32[]{:S(2)}, u32[]{:S(2)}) collective-permute-start(bf16[128,2048]{1,0:T(8,128)(2,1)} %bitcast.41), channel_id=1, source_target_pairs={{0,3},{1,0},{2,1},{3,2},{4,7},{5,4},{6,5},{7,6},{8,11},{9,8},{10,9... | collective-permute-start | bytes 1572872 | tf_op jit(solution)/shard_map/ppermute | solution.py:365
  729.7 63.4 %collective-permute-start.38 = (bf16[256,2048]{1,0:T(8,128)(2,1)}, bf16[256,2048]{1,0:T(8,128)(2,1)}, u32[]{:S(2)}, u32[]{:S(2)}) collective-permute-start(bf16[256,2048]{1,0:T(8,128)(2,1)} %after.62), channel_id=1, source_target_pairs={{0,1},{1,2},{2,3},{4,5},{5,6},{6,7},{8,9},{9,10},{10,11},{12,13},{... | collective-permute-start | bytes 3145736 | tf_op jit(solution)/shard_map/ppermute | solution.py:361
  805.5 40.2 %collective-permute-start.51 = (bf16[128,2048]{1,0:T(8,128)(2,1)}, bf16[128,2048]{1,0:T(8,128)(2,1)S(1)}, u32[]{:S(2)}, u32[]{:S(2)}) collective-permute-start(bf16[128,2048]{1,0:T(8,128)(2,1)} %get-tuple-element.48), channel_id=1, source_target_pairs={{0,2},{1,3},{2,0},{3,1},{4,6},{5,7},{6,4},{7,5},{8,10},{9,11},{10,... | collective-permute-start | bytes 1572872 | tf_op jit(solution)/shard_map/ppermute | solution.py:365
  (107 other events, 1446.9 us)
Sparse Core Ops, SparseCore 0:
  26.4 41.2 all-gather.4
  70.1 98.2 all-gather.6
  170.3 54.3 all-gather.10
  227.0 89.8 all-gather.8
  541.0 124.6 reduce-scatter.2
  668.7 104.7 reduce-scatter.4

commit v4 on v3

--- a/solution.py
+++ b/solution.py
@@ -356,6 +356,31 @@
     )(values, cosine, sine)
 
 
+def spread_kernel(me_ref, *refs):
+    count, out_ref = len(refs) - 1, refs[-1]
+    width = refs[0].shape[1]
+    for r in range(count):
+        place = lax.rem(me_ref[0] - r + count, count)
+        start = pl.multiple_of(place * width, LANES)
+        out_ref[:, pl.ds(start, width)] = refs[r][...].astype(WIDE)
+
+
+def spread(slots, me, kind, rows, blocks):
+    count, width = len(slots), slots[0].shape[1] // blocks
+    part = pl.BlockSpec((rows, width), lambda i, me: (kind, i))
+    return pl.pallas_call(
+        spread_kernel,
+        grid_spec=pltpu.PrefetchScalarGridSpec(
+            num_scalar_prefetch=1,
+            grid=(blocks,),
+            in_specs=[part] * count,
+            out_specs=pl.BlockSpec((rows, count * width), lambda i, me: (0, i)),
+        ),
+        out_shape=jax.ShapeDtypeStruct((rows, blocks * count * width), WIDE),
+        name="spread",
+    )(jnp.reshape(me, (1,)).astype(jnp.int32), *slots)
+
+
 def shift(values, count, step, senders):
     pairs = [(i, i + step) for i in senders if 0 <= i + step < count]
     return lax.ppermute(values, "ctx", pairs)
@@ -479,7 +504,7 @@
 
 def chip_scatter_steps(values, *between):
     if not small_square():
-        return chip_scatter(values)
+        return chip_scatter(values), values
     columns = values.shape[1]
     y, x = lax.axis_index("y"), lax.axis_index("x")
     parts = values.reshape(2, 2, -1, columns)
@@ -490,11 +515,12 @@
     bottom_came = lax.ppermute(pick(bottom, 1 - y, 0), "y", SWAP)
     top = after(add(pick(top, x, 1), top_came), *between)
     bottom = add(pick(bottom, y, 0), bottom_came)
+    middle = pick(bottom, 1 - x, 0)
     top_came = lax.ppermute(pick(top, 1 - y, 0), "y", SWAP)
-    bottom_came = lax.ppermute(pick(bottom, 1 - x, 0), "x", SWAP)
+    bottom_came = lax.ppermute(middle, "x", SWAP)
     top = add(pick(top, y, 0), top_came)
     bottom = add(pick(bottom, x, 0), bottom_came)
-    return jnp.concatenate([top, bottom], 0)
+    return jnp.concatenate([top, bottom], 0), middle
 
 
 def per_device(
@@ -722,17 +748,22 @@
     pair_terms = jnp.concatenate(
         [core_summed(first_hidden, grad_pair), gain_part.reshape(-1, LANES)], 1
     )
-    pair_sum = chip_scatter_steps(pair_terms, *grad_slots[1:])
-    branch_part = after(branch_part, pair_sum, *grad_slots[1:]).reshape(2, n_ctx, rows, width)
+    pair_sum, middle = chip_scatter_steps(pair_terms, *grad_slots[1:])
+    branch_part = after(branch_part, middle, *grad_slots[1:]).reshape(2, n_ctx, rows, width)
     branch_part = branch_part.transpose(1, 0, 2, 3).reshape(n_ctx * 2 * rows, width)
     total = lambda parts: sum(part.astype(WIDE) for part in parts)
     arrived = ctx_rows_scatter(branch_part, pair_sum)
-    pair_weight_grad = total(ctx_rows_scatter(pair_sum, arrived[1]))
     grad_slots[0] = after(grad_slots[0], arrived[1])
-    both_grad = in_order(grad_slots, n_ctx, me).reshape(n_ctx, 2, rows, n_dp, hidden_rows)
-    both_grad = both_grad.transpose(1, 2, 3, 0, 4).reshape(2, rows, hidden_units).astype(WIDE)
-    gate_weight_grad, up_weight_grad = both_grad[0], both_grad[1]
-    arrived[2:] = [after(values, gate_weight_grad) for values in arrived[2:]]
+    if hidden_rows % LANES == 0:
+        gate_weight_grad, up_weight_grad = (
+            spread(grad_slots, me, kind, rows, n_dp) for kind in range(2)
+        )
+    else:
+        both_grad = in_order(grad_slots, n_ctx, me).reshape(n_ctx, 2, rows, n_dp, hidden_rows)
+        both_grad = both_grad.transpose(1, 2, 3, 0, 4).reshape(2, rows, hidden_units)
+        gate_weight_grad, up_weight_grad = both_grad[0].astype(WIDE), both_grad[1].astype(WIDE)
+    pair_weight_grad = total(ctx_rows_scatter(pair_sum, gate_weight_grad, up_weight_grad))
+    arrived[2:] = [after(values, gate_weight_grad, up_weight_grad) for values in arrived[2:]]
     branch_grad = total(arrived).reshape(2, rows, width)
     down_sent = after(down_sent[0], pair_terms), down_sent[1]
     came = line_send(down_sent, n_ctx, n_ctx - 1)

time: 870 us -> 867 us (level)
  waiting for transfers between devices: 291 us -> 273 us
  starting transfers between devices: 166 us -> 182 us
  Pallas kernels: 191 us -> 201 us
  local copies, waits for them, and re-layouts: 61.4 us -> 51.6 us
    ppermute x21, starting transfers between devices: 69.4 us -> 85.1 us  [rotate(): lax.ppermute(values, 'ctx', [(i, (i + step) % count) for i in range(count)])]
    ppermute x21, waiting for transfers between devices: 128 us -> 115 us  [rotate(): lax.ppermute(values, 'ctx', [(i, (i + step) % count) for i in range(count)])]
    pallas_call x0 -> x2, Pallas kernels: none -> 10.1 us  [spread(): pl.pallas_call(spread_kernel, grid_spec=pltpu.PrefetchScalarGridSpec(num_...]
    unnamed x147 -> x156, local copies, waits for them, and re-layouts: 23.3 us -> 25.5 us
  transfers between devices with their start and end apart: 59 -> 59, of which waited for: 26 -> 25; matrix products, arithmetic and copies ran while one was open for 18% -> 16% of each run, Pallas kernels for 15% -> 16%
where the time goes in v4:
time: 867 us; the launch traced here: 856 us
  waiting for transfers between devices  273 us (31%)
  Pallas kernels  201 us (23%)
  starting transfers between devices  182 us (21%)
  other arithmetic  69.5 us (8%)
  matrix products  62.7 us (7%)
  local copies, waits for them, and re-layouts  51.6 us (6%)
  between operations  16 us (2%)
    ppermute x21, waiting for transfers between devices, rotate(): lax.ppermute(values, 'ctx', [(i, (i + step) % count) for i in range(count)])  115 us
    ppermute x24, waiting for transfers between devices, shift(): return lax.ppermute(values, 'ctx', pairs)  95.8 us
    ppermute x24, starting transfers between devices, shift(): return lax.ppermute(values, 'ctx', pairs)  91.4 us
    ppermute x21, starting transfers between devices, rotate(): lax.ppermute(values, 'ctx', [(i, (i + step) % count) for i in range(count)])  85.1 us
    pallas_call x4, Pallas kernels, weight_rows(): pl.pallas_call(lambda *refs: weight_kernel(shared, parts, *refs), grid_sp...  68.5 us
    dot_general x10, matrix products, dot(): return lax.dot_general(left, right, dims, preferred_element_type=WIDE)  62.7 us
    pallas_call x2, Pallas kernels, feed(): pl.pallas_call(feed_kernel, grid=(steps,), in_specs=[whole, whole, pl.Blo...  40.7 us
    pallas_call x2, Pallas kernels, feed_back(): pl.pallas_call(second_kernel, grid=(width // FEED_STEP,), in_specs=[whole...  30.6 us
  transfers between devices with their start and end apart: 59, of which 25 were waited for; matrix products, arithmetic and copies ran while one was open for 16% of the time, Pallas kernels for 16%

profile of v4, /device:TPU:0, one launch (start us, length us, event | category | flops | bytes accessed | tf_op | source)
XLA Modules:
  0.0 855.8 jit_solution(14978473869611889594)
XLA Ops:
  33.5 11.7 %collective-permute-done.3 = bf16[64,4096]{1,0:T(8,128)(2,1)S(1)} collective-permute-done((bf16[64,4096]{1,0:T(8,128)(2,1)}, bf16[64,4096]{1,0:T(8,128)(2,1)S(1)}, u32[]{:S(2)}, u32[]{:S(2)}) %collective-permute-start.3) | collective-permute-done | bytes 524320 | tf_op jit(solution)/shard_map/ppermute | solution.py:390
  45.2 20.6 %collective-permute-done.4 = bf16[64,4096]{1,0:T(8,128)(2,1)S(1)} collective-permute-done((bf16[64,4096]{1,0:T(8,128)(2,1)}, bf16[64,4096]{1,0:T(8,128)(2,1)S(1)}, u32[]{:S(2)}, u32[]{:S(2)}) %collective-permute-start.4) | collective-permute-done | bytes 524320 | tf_op jit(solution)/shard_map/ppermute | solution.py:390
  76.6 11.6 %collective-permute-start.6 = (bf16[64,4096]{1,0:T(8,128)(2,1)}, bf16[64,4096]{1,0:T(8,128)(2,1)S(1)}, u32[]{:S(2)}, u32[]{:S(2)}) collective-permute-start(bf16[64,4096]{1,0:T(8,128)(2,1)} %after.39), channel_id=1, source_target_pairs={{0,1},{1,2},{2,3},{3,0},{4,5},{5,6},{6,7},{7,4},{8,9},{9,10},{10,1... | collective-permute-start | bytes 1572872 | tf_op jit(solution)/shard_map/ppermute | solution.py:390
  103.2 21.2 %collective-permute-done.7 = bf16[64,4096]{1,0:T(8,128)(2,1)S(1)} collective-permute-done((bf16[64,4096]{1,0:T(8,128)(2,1)}, bf16[64,4096]{1,0:T(8,128)(2,1)S(1)}, u32[]{:S(2)}, u32[]{:S(2)}) %collective-permute-start.7) | collective-permute-done | bytes 524320 | tf_op jit(solution)/shard_map/ppermute | solution.py:390
  138.5 14.2 %collective-permute-start.11 = (bf16[256,1024]{1,0:T(8,128)(2,1)}, bf16[256,1024]{1,0:T(8,128)(2,1)S(1)}, u32[]{:S(2)}, u32[]{:S(2)}) collective-permute-start(bf16[256,1024]{1,0:T(8,128)(2,1)} %after.42), channel_id=1, source_target_pairs={{0,3},{4,7},{8,11},{12,15},{16,19},{20,23},{24,27},{28,31}} | collective-permute-start | bytes 1572872 | tf_op jit(solution)/shard_map/ppermute | solution.py:386
  165.5 11.2 %collective-permute-done.10 = bf16[256,1024]{1,0:T(8,128)(2,1)S(1)} collective-permute-done((bf16[256,1024]{1,0:T(8,128)(2,1)}, bf16[256,1024]{1,0:T(8,128)(2,1)S(1)}, u32[]{:S(2)}, u32[]{:S(2)}) %collective-permute-start.10) | collective-permute-done | bytes 524320 | tf_op jit(solution)/shard_map/ppermute | solution.py:386
  187.9 12.7 %collective-permute-start.12 = (bf16[256,2048]{1,0:T(8,128)(2,1)}, bf16[256,2048]{1,0:T(8,128)(2,1)}, u32[]{:S(2)}, u32[]{:S(2)}) collective-permute-start(bf16[256,2048]{1,0:T(8,128)(2,1)} %after.43), channel_id=1, source_target_pairs={{0,1},{1,2},{2,3},{3,0},{4,5},{5,6},{6,7},{7,4},{8,9},{9,10},{10,1... | collective-permute-start | bytes 3145736 | tf_op jit(solution)/shard_map/ppermute | solution.py:390
  211.7 23.8 %attend.1 = (bf16[256,2048]{1,0:T(8,128)(2,1)S(1)}, bf16[256,2048]{1,0:T(8,128)(2,1)S(1)}, f32[32,256]{1,0:T(8,128)S(1)}) custom-call(f32[256,2048]{1,0:T(8,128)S(1)} %fusion.6.raw_ref, f32[256,128]{1,0:T(8,128)S(1)} %copy-done.8, f32[256,128]{1,0:T(8,128)S(1)} %copy-done.9, bf16[1024,1024]{1,0:T(8,128)(2,1)S(1)} %copy-done, bf16[1024,1024]{1,0:T(8,128)(2,1)S(1)} %copy-done, ...), custom_call_target="tpu_custom_call" | custom-call | flops 1000000 | bytes 1000000 | tf_op jit(solution)/shard_map/attend/pallas_call | solution.py:319
  245.5 15.3 %collective-permute-done.13.refs_2_ = bf16[256,2048]{1,0:T(8,128)(2,1)} collective-permute-done((bf16[256,2048]{1,0:T(8,128)(2,1)}, bf16[256,2048]{1,0:T(8,128)(2,1)}, u32[]{:S(2)}, u32[]{:S(2)}) %collective-permute-start.13) | collective-permute-done | bytes 1048608 | tf_op jit(solution)/shard_map/ppermute | solution.py:390
  268.5 27.7 %collective-permute-start.15 = (bf16[256,2048]{1,0:T(8,128)(2,1)}, bf16[256,2048]{1,0:T(8,128)(2,1)}, u32[]{:S(2)}, u32[]{:S(2)}) collective-permute-start(bf16[256,2048]{1,0:T(8,128)(2,1)} %after.44), channel_id=1, source_target_pairs={{0,1},{1,2},{2,3},{4,5},{5,6},{6,7},{8,9},{9,10},{10,11},{12,13},{... | collective-permute-start | bytes 3145736 | tf_op jit(solution)/shard_map/ppermute | solution.py:386
  297.5 19.8 %collective-permute-done.15 = bf16[256,2048]{1,0:T(8,128)(2,1)} collective-permute-done((bf16[256,2048]{1,0:T(8,128)(2,1)}, bf16[256,2048]{1,0:T(8,128)(2,1)}, u32[]{:S(2)}, u32[]{:S(2)}) %collective-permute-start.15) | collective-permute-done | bytes 1048608 | tf_op jit(solution)/shard_map/ppermute | solution.py:386
  331.8 15.8 %collective-permute-done.18 = bf16[256,2048]{1,0:T(8,128)(2,1)} collective-permute-done((bf16[256,2048]{1,0:T(8,128)(2,1)}, bf16[256,2048]{1,0:T(8,128)(2,1)}, u32[]{:S(2)}, u32[]{:S(2)}) %collective-permute-start.18) | collective-permute-done | bytes 1048608 | tf_op jit(solution)/shard_map/ppermute | solution.py:386
  352.3 20.3 %feed.2 = (bf16[512,2048]{1,0:T(8,128)(2,1)}, bf16[512,2048]{1,0:T(8,128)(2,1)}, bf16[512,2048]{1,0:T(8,128)(2,1)}) custom-call(bf16[512,2048]{1,0:T(8,128)(2,1)} %pad_maximum_fusion.2.token_ref.refs_1_, bf16[512,2048]{1,0:T(8,128)(2,1)} %constant_dynamic-update-slice_fusion.1.goal_ref.refs_9_, ...), custom_call_target="tpu_custom_call" | custom-call | flops 1000000 | bytes 1000000 | tf_op jit(solution)/shard_map/feed/pallas_call | solution.py:207
  376.9 20.4 %feed.3 = (bf16[512,2048]{1,0:T(8,128)(2,1)}, bf16[512,2048]{1,0:T(8,128)(2,1)}, bf16[512,2048]{1,0:T(8,128)(2,1)}) custom-call(bf16[512,2048]{1,0:T(8,128)(2,1)} %pad_maximum_fusion.3.token_ref.refs_2_, bf16[512,2048]{1,0:T(8,128)(2,1)} %after.46.goal_ref.refs_10_, bf16[2048,4096]{1,0:T(8,128)(2,1)} %all-gather.9.cloned.1.call-done.gate_ref.up_ref, ...), custom_call_target="tpu_custom_call" | custom-call | flops 1000000 | bytes 1000000 | tf_op jit(solution)/shard_map/feed/pallas_call | solution.py:207
  397.3 15.2 %feed_back.2.refs_1_ = bf16[512,2048]{1,0:T(8,128)(2,1)} custom-call(bf16[512,2048]{1,0:T(8,128)(2,1)} %get-tuple-element.26.grad_gate_ref.refs_6_, bf16[512,2048]{1,0:T(8,128)(2,1)} %get-tuple-element.27.grad_up_ref.refs_8_, bf16[2048,4096]{1,0:T(8,128)(2,1)} %all-gather.9.cloned.1.call-done.gate_ref.up_ref, ...), custom_call_target="tpu_custom_call" | custom-call | flops 1000000 | bytes 1000000 | tf_op jit(solution)/shard_map/feed_back/pallas_call | solution.py:229
  423.9 15.3 %feed_back.3 = bf16[512,2048]{1,0:T(8,128)(2,1)} custom-call(bf16[512,2048]{1,0:T(8,128)(2,1)} %get-tuple-element.28.grad_gate_ref.refs_0_, bf16[512,2048]{1,0:T(8,128)(2,1)} %after.48.grad_up_ref.refs_7_, bf16[2048,4096]{1,0:T(8,128)(2,1)} %all-gather.9.cloned.1.call-done.gate_ref.up_ref, bf16[2048,4096]{1,0:T(8,128)(2,1)} %all-gather.9.cloned.1.call-done.gate_ref.up_ref), custom_call_target="tpu_custom_call" | custom-call | flops 1000000 | bytes 1000000 | tf_op jit(solution)/shard_map/feed_back/pallas_call | solution.py:229
  456.1 23.0 %weight_rows.4.refs_0_ = bf16[3072,2048]{1,0:T(8,128)(2,1)} custom-call(s32[1]{0:T(128)} %bitcast.29.refs_0_, bf16[512,2048]{1,0:T(8,128)(2,1)} %pad_maximum_fusion.2.token_ref.refs_1_, bf16[512,2048]{1,0:T(8,128)(2,1)} %pad_maximum_fusion.3.token_ref.refs_2_, bf16[512,2048]{1,0:T(8,128)(2,1)} %get-tuple-element.24.refs_1_.refs_3_, ...), custom_call_target="tpu_custom_call" | custom-call | flops 12884901888 | bytes 12582912 | tf_op jit(solution)/shard_map/weight_rows/pallas_call | solution.py:274
  516.4 24.5 %weight_rows.5.refs_1_ = bf16[3072,2048]{1,0:T(8,128)(2,1)} custom-call(s32[1]{0:T(128)} %bitcast.28.refs_0_, bf16[512,2048]{1,0:T(8,128)(2,1)} %pad_maximum_fusion.2.token_ref.refs_1_, bf16[512,2048]{1,0:T(8,128)(2,1)} %pad_maximum_fusion.3.token_ref.refs_2_, bf16[512,2048]{1,0:T(8,128)(2,1)} %get-tuple-element.24.refs_1_.refs_3_, ...), custom_call_target="tpu_custom_call" | custom-call | flops 12884901888 | bytes 12582912 | tf_op jit(solution)/shard_map/weight_rows/pallas_call | solution.py:274
  581.7 22.6 %attend_back.1 = (bf16[256,2048]{1,0:T(8,128)(2,1)S(1)}, bf16[1024,512]{1,0:T(8,128)(2,1)S(1)}, bf16[1024,512]{1,0:T(8,128)(2,1)S(1)}) custom-call(bf16[256,2048]{1,0:T(8,128)(2,1)S(1)} %copy-done.15, f32[256,128]{1,0:T(8,128)S(1)} %copy-done.8, f32[256,128]{1,0:T(8,128)S(1)} %copy-done.9, bf16[1024,1024]{1,0:T(8,128)(2,1)S(1)} %copy-done, ...), custom_call_target="tpu_custom_call" | custom-call | flops 24000000000 | bytes 10000000 | tf_op jit(solution)/shard_map/attend_back/pallas_call | solution.py:341
  628.9 13.5 %collective-permute-done.47.refs_5_ = bf16[2048,2048]{1,0:T(8,128)(2,1)} collective-permute-done((bf16[2048,2048]{1,0:T(8,128)(2,1)}, bf16[2048,2048]{1,0:T(8,128)(2,1)}, u32[]{:S(2)}, u32[]{:S(2)}) %collective-permute-start.47) | collective-permute-done | bytes 8388640 | tf_op jit(solution)/shard_map/ppermute | solution.py:487
  642.4 11.9 %weight_rows.7 = bf16[2048,2048]{1,0:T(8,128)(2,1)} custom-call(s32[1]{0:T(128)} %bitcast.28.refs_0_, bf16[256,2048]{1,0:T(8,128)(2,1)} %copy-done.4, bf16[256,2048]{1,0:T(8,128)(2,1)} %copy-done.25, bf16[256,2048]{1,0:T(8,128)(2,1)} %after.64.refs_3_, bf16[256,2048]{1,0:T(8,128)(2,1)} %copy-done.1, bf16[2048,2048]{1,0:T(8,128)(2,1)} %collective-permute-done.47.refs_5_), custom_call_target="tpu_custom_call" | custom-call | flops 2147483648 | bytes 8388608 | tf_op jit(solution)/shard_map/weight_rows/pallas_call | solution.py:274
  732.1 15.3 %collective-permute-done.44 = bf16[2,128,1152]{2,1,0:T(8,128)(2,1)} collective-permute-done((bf16[2,128,1152]{2,1,0:T(8,128)(2,1)}, bf16[2,128,1152]{2,1,0:T(8,128)(2,1)}, u32[]{:S(2)}, u32[]{:S(2)}) %collective-permute-start.44) | collective-permute-done | bytes 589856 | tf_op jit(solution)/shard_map/ppermute | solution.py:515
  750.1 22.7 %collective-permute-done.40 = bf16[2,128,1152]{2,1,0:T(8,128)(2,1)S(1)} collective-permute-done((bf16[2,128,1152]{2,1,0:T(8,128)(2,1)S(1)}, bf16[2,128,1152]{2,1,0:T(8,128)(2,1)S(1)}, u32[]{:S(2)}, u32[]{:S(2)}) %collective-permute-start.40) | collective-permute-done | bytes 589856 | tf_op jit(solution)/shard_map/ppermute | solution.py:514
  799.0 18.5 %collective-permute-start.51 = (bf16[128,2048]{1,0:T(8,128)(2,1)}, bf16[128,2048]{1,0:T(8,128)(2,1)S(1)}, u32[]{:S(2)}, u32[]{:S(2)}) collective-permute-start(bf16[128,2048]{1,0:T(8,128)(2,1)} %get-tuple-element.46), channel_id=1, source_target_pairs={{0,2},{1,3},{2,0},{3,1},{4,6},{5,7},{6,4},{7,5},{8,10},{9,11},{10,... | collective-permute-start | bytes 1572872 | tf_op jit(solution)/shard_map/ppermute | solution.py:390
  (430 shorter events, 410.7 us)
Async XLA Ops:
  7.2 121.8 %all-gather.5.cloned.1.call-start = ((), (), s32[]{:S(2)}) async-start(), calls=%async_computation.2 | async-start | bytes 5308416 | tf_op jit(solution)/shard_map/all_gather | solution.py:449
  26.3 179.2 %all-gather.7.cloned.1.call-start = ((), (), s32[]{:S(2)}) async-start(), calls=%async_computation.3 | async-start | bytes 18874368 | tf_op jit(solution)/shard_map/all_gather | solution.py:449
  30.8 35.0 %collective-permute-start.4 = (bf16[64,4096]{1,0:T(8,128)(2,1)}, bf16[64,4096]{1,0:T(8,128)(2,1)S(1)}, u32[]{:S(2)}, u32[]{:S(2)}) collective-permute-start(bf16[64,4096]{1,0:T(8,128)(2,1)} %after.38), channel_id=1, source_target_pairs={{0,2},{1,3},{2,0},{3,1},{4,6},{5,7},{6,4},{7,5},{8,10},{9,11},{10,... | collective-permute-start | bytes 1572872 | tf_op jit(solution)/shard_map/ppermute | solution.py:390
  67.3 285.0 %all-gather.11.cloned.1.call-start = ((), (), s32[]{:S(2)}) async-start(), calls=%async_computation.5 | async-start | bytes 9437184 | tf_op jit(solution)/shard_map/all_gather | solution.py:449
  70.1 282.1 %all-gather.9.cloned.1.call-start = ((), (), s32[]{:S(2)}) async-start(), calls=%async_computation.4 | async-start | bytes 18874368 | tf_op jit(solution)/shard_map/all_gather | solution.py:449
  90.9 33.5 %collective-permute-start.7 = (bf16[64,4096]{1,0:T(8,128)(2,1)}, bf16[64,4096]{1,0:T(8,128)(2,1)S(1)}, u32[]{:S(2)}, u32[]{:S(2)}) collective-permute-start(bf16[64,4096]{1,0:T(8,128)(2,1)} %after.40), channel_id=1, source_target_pairs={{0,2},{1,3},{2,0},{3,1},{4,6},{5,7},{6,4},{7,5},{8,10},{9,11},{10,... | collective-permute-start | bytes 1572872 | tf_op jit(solution)/shard_map/ppermute | solution.py:390
  125.9 539.8 %reduce-scatter.3.cloned.1.call-start = ((), (), s32[]{:S(2)}) async-start(), calls=%async_computation.6 | async-start | bytes 15728640 | tf_op jit(solution)/shard_map/reduce_scatter | solution.py:502
  187.9 57.5 %collective-permute-start.12 = (bf16[256,2048]{1,0:T(8,128)(2,1)}, bf16[256,2048]{1,0:T(8,128)(2,1)}, u32[]{:S(2)}, u32[]{:S(2)}) collective-permute-start(bf16[256,2048]{1,0:T(8,128)(2,1)} %after.43), channel_id=1, source_target_pairs={{0,1},{1,2},{2,3},{3,0},{4,5},{5,6},{6,7},{7,4},{8,9},{9,10},{10,1... | collective-permute-start | bytes 3145736 | tf_op jit(solution)/shard_map/ppermute | solution.py:390
  200.7 60.1 %collective-permute-start.13 = (bf16[256,2048]{1,0:T(8,128)(2,1)}, bf16[256,2048]{1,0:T(8,128)(2,1)}, u32[]{:S(2)}, u32[]{:S(2)}) collective-permute-start(bf16[256,2048]{1,0:T(8,128)(2,1)} %after.43), channel_id=1, source_target_pairs={{0,2},{1,3},{2,0},{3,1},{4,6},{5,7},{6,4},{7,5},{8,10},{9,11},{10,... | collective-permute-start | bytes 3145736 | tf_op jit(solution)/shard_map/ppermute | solution.py:390
  202.5 66.0 %collective-permute-start.14 = (bf16[256,2048]{1,0:T(8,128)(2,1)}, bf16[256,2048]{1,0:T(8,128)(2,1)}, u32[]{:S(2)}, u32[]{:S(2)}) collective-permute-start(bf16[256,2048]{1,0:T(8,128)(2,1)} %after.43), channel_id=1, source_target_pairs={{0,3},{1,0},{2,1},{3,2},{4,7},{5,4},{6,5},{7,6},{8,11},{9,8},{10,9... | collective-permute-start | bytes 3145736 | tf_op jit(solution)/shard_map/ppermute | solution.py:390
  268.5 48.8 %collective-permute-start.15 = (bf16[256,2048]{1,0:T(8,128)(2,1)}, bf16[256,2048]{1,0:T(8,128)(2,1)}, u32[]{:S(2)}, u32[]{:S(2)}) collective-permute-start(bf16[256,2048]{1,0:T(8,128)(2,1)} %after.44), channel_id=1, source_target_pairs={{0,1},{1,2},{2,3},{4,5},{5,6},{6,7},{8,9},{9,10},{10,11},{12,13},{... | collective-permute-start | bytes 3145736 | tf_op jit(solution)/shard_map/ppermute | solution.py:386
  327.8 44.8 %collective-permute-start.20 = (bf16[256,2048]{1,0:T(8,128)(2,1)}, bf16[256,2048]{1,0:T(8,128)(2,1)}, u32[]{:S(2)}, u32[]{:S(2)}) collective-permute-start(bf16[256,2048]{1,0:T(8,128)(2,1)} %collective-permute-done.16), channel_id=1, source_target_pairs={{2,3},{6,7},{10,11},{14,15},{18,19},{22,23},{26,27},{30,31}} | collective-permute-start | bytes 3145736 | tf_op jit(solution)/shard_map/ppermute | solution.py:386
  540.9 236.1 %reduce-scatter.5.cloned.1.call-start = ((), (), s32[]{:S(2)}) async-start(), calls=%async_computation.7 | async-start | bytes 10485760 | tf_op jit(solution)/shard_map/reduce_scatter | solution.py:502
  569.6 37.6 %collective-permute-start.28 = (bf16[256,2048]{1,0:T(8,128)(2,1)}, bf16[256,2048]{1,0:T(8,128)(2,1)}, u32[]{:S(2)}, u32[]{:S(2)}) collective-permute-start(bf16[256,2048]{1,0:T(8,128)(2,1)} %get-tuple-element.57.refs_1_), channel_id=1, source_target_pairs={{0,1},{1,2},{4,5},{5,6},{8,9},{9,10},{12,13},{13,14},{16,17},{17,1... | collective-permute-start | bytes 3145736 | tf_op jit(solution)/shard_map/ppermute | solution.py:386
  654.3 33.6 %collective-permute-start.34 = (bf16[256,1024]{1,0:T(8,128)(2,1)}, bf16[256,1024]{1,0:T(8,128)(2,1)}, u32[]{:S(2)}, u32[]{:S(2)}) collective-permute-start(bf16[256,1024]{1,0:T(8,128)(2,1)} %add_convert_fusion.6.refs_1_), channel_id=1, source_target_pairs={{1,0},{2,1},{3,2},{5,4},{6,5},{7,6},{9,8},{10,9},{11,10},{13,12},{... | collective-permute-start | bytes 1572872 | tf_op jit(solution)/shard_map/ppermute | solution.py:386
  678.9 110.4 %collective-permute-start.39 = (bf16[256,2048]{1,0:T(8,128)(2,1)}, bf16[256,2048]{1,0:T(8,128)(2,1)}, u32[]{:S(2)}, u32[]{:S(2)}) collective-permute-start(bf16[256,2048]{1,0:T(8,128)(2,1)} %get-tuple-element.56.refs_2_), channel_id=1, source_target_pairs={{1,0},{2,1},{3,2},{5,4},{6,5},{7,6},{9,8},{10,9},{11,10},{13,12},{... | collective-permute-start | bytes 3145736 | tf_op jit(solution)/shard_map/ppermute | solution.py:386
  690.2 84.0 %collective-permute-start.41 = (bf16[128,2048]{1,0:T(8,128)(2,1)}, bf16[128,2048]{1,0:T(8,128)(2,1)}, u32[]{:S(2)}, u32[]{:S(2)}) collective-permute-start(bf16[128,2048]{1,0:T(8,128)(2,1)} %bitcast.40), channel_id=1, source_target_pairs={{0,2},{1,3},{2,0},{3,1},{4,6},{5,7},{6,4},{7,5},{8,10},{9,11},{10,... | collective-permute-start | bytes 1572872 | tf_op jit(solution)/shard_map/ppermute | solution.py:390
  693.5 80.7 %collective-permute-start.42 = (bf16[128,2048]{1,0:T(8,128)(2,1)}, bf16[128,2048]{1,0:T(8,128)(2,1)}, u32[]{:S(2)}, u32[]{:S(2)}) collective-permute-start(bf16[128,2048]{1,0:T(8,128)(2,1)} %bitcast.41), channel_id=1, source_target_pairs={{0,3},{1,0},{2,1},{3,2},{4,7},{5,4},{6,5},{7,6},{8,11},{9,8},{10,9... | collective-permute-start | bytes 1572872 | tf_op jit(solution)/shard_map/ppermute | solution.py:390
  729.6 59.7 %collective-permute-start.38 = (bf16[256,2048]{1,0:T(8,128)(2,1)}, bf16[256,2048]{1,0:T(8,128)(2,1)}, u32[]{:S(2)}, u32[]{:S(2)}) collective-permute-start(bf16[256,2048]{1,0:T(8,128)(2,1)} %after.62), channel_id=1, source_target_pairs={{0,1},{1,2},{2,3},{4,5},{5,6},{6,7},{8,9},{9,10},{10,11},{12,13},{... | collective-permute-start | bytes 3145736 | tf_op jit(solution)/shard_map/ppermute | solution.py:386
  784.6 50.9 %collective-permute-start.52 = (bf16[128,2048]{1,0:T(8,128)(2,1)}, bf16[128,2048]{1,0:T(8,128)(2,1)S(1)}, u32[]{:S(2)}, u32[]{:S(2)}) collective-permute-start(bf16[128,2048]{1,0:T(8,128)(2,1)} %get-tuple-element.47), channel_id=1, source_target_pairs={{0,3},{1,0},{2,1},{3,2},{4,7},{5,4},{6,5},{7,6},{8,11},{9,8},{10,9... | collective-permute-start | bytes 1572872 | tf_op jit(solution)/shard_map/ppermute | solution.py:390
  787.3 40.3 %collective-permute-start.50 = (bf16[64,1152]{1,0:T(8,128)(2,1)}, bf16[64,1152]{1,0:T(8,128)(2,1)S(1)}, u32[]{:S(2)}, u32[]{:S(2)}) collective-permute-start(bf16[64,1152]{1,0:T(8,128)(2,1)} %get-tuple-element.82), channel_id=1, source_target_pairs={{0,3},{1,0},{2,1},{3,2},{4,7},{5,4},{6,5},{7,6},{8,11},{9,8},{10,9... | collective-permute-start | bytes 442376 | tf_op jit(solution)/shard_map/ppermute | solution.py:390
  789.3 43.5 %collective-permute-start.49 = (bf16[64,1152]{1,0:T(8,128)(2,1)}, bf16[64,1152]{1,0:T(8,128)(2,1)S(1)}, u32[]{:S(2)}, u32[]{:S(2)}) collective-permute-start(bf16[64,1152]{1,0:T(8,128)(2,1)} %get-tuple-element.83), channel_id=1, source_target_pairs={{0,2},{1,3},{2,0},{3,1},{4,6},{5,7},{6,4},{7,5},{8,10},{9,11},{10,... | collective-permute-start | bytes 442376 | tf_op jit(solution)/shard_map/ppermute | solution.py:390
  789.3 44.2 %collective-permute-start.46 = (bf16[64,1152]{1,0:T(8,128)(2,1)}, bf16[64,1152]{1,0:T(8,128)(2,1)}, u32[]{:S(2)}, u32[]{:S(2)}) collective-permute-start(bf16[64,1152]{1,0:T(8,128)(2,1)} %get-tuple-element.81), channel_id=1, source_target_pairs={{0,1},{1,2},{2,3},{3,0},{4,5},{5,6},{6,7},{7,4},{8,9},{9,10},{10,1... | collective-permute-start | bytes 442376 | tf_op jit(solution)/shard_map/ppermute | solution.py:390
  799.0 45.0 %collective-permute-start.51 = (bf16[128,2048]{1,0:T(8,128)(2,1)}, bf16[128,2048]{1,0:T(8,128)(2,1)S(1)}, u32[]{:S(2)}, u32[]{:S(2)}) collective-permute-start(bf16[128,2048]{1,0:T(8,128)(2,1)} %get-tuple-element.46), channel_id=1, source_target_pairs={{0,2},{1,3},{2,0},{3,1},{4,6},{5,7},{6,4},{7,5},{8,10},{9,11},{10,... | collective-permute-start | bytes 1572872 | tf_op jit(solution)/shard_map/ppermute | solution.py:390
  (112 other events, 1540.6 us)
Sparse Core Ops, SparseCore 0:
  26.4 41.2 all-gather.4
  70.1 98.2 all-gather.6
  170.3 54.3 all-gather.10
  227.0 89.8 all-gather.8
  541.0 124.6 reduce-scatter.2
  668.6 104.6 reduce-scatter.4

commit v5 on v4

--- a/solution.py
+++ b/solution.py
@@ -677,7 +677,7 @@
     down_sent = tuple(
         after(values, grad_second) for values in line_step(down_slots, n_ctx, 1, None)
     )
-    feed_part = feed_summed(steps[-1], down_sent)
+    feed_part = feed_summed(steps[-1], came)
     in_slots = lambda values: [
         values[r * entry_count : (r + 1) * entry_count] for r in range(n_ctx)
     ]
@@ -725,7 +725,7 @@
         [0, 1],
     )
     branch_terms = branch_summed([steps[-1]])
-    grad_pair = turn_pair(after(pair_grad, grad_slots[1]), cosine, -sine)
+    grad_pair = turn_pair(pair_grad, cosine, -sine)
     grad_first = dot(grad_query, query_full, NT) + dot(grad_pair, pair_weight, NT)
     first_gain_term = jnp.sum(grad_first * unit_first, axis=0)
     input_grad = (grad_residual + norm_back(tokens_wide, grad_first * gain_first)).astype(LOW)

time: 867 us -> 919 us (1.060)
  waiting for transfers between devices: 273 us -> 342 us
  starting transfers between devices: 182 us -> 163 us
    ppermute x21, waiting for transfers between devices: 115 us -> 178 us  [rotate(): lax.ppermute(values, 'ctx', [(i, (i + step) % count) for i in range(count)])]
    ppermute x24, waiting for transfers between devices: 95.8 us -> 122 us  [shift(): return lax.ppermute(values, 'ctx', pairs)]
    ppermute x1, waiting for transfers between devices: 22.7 us -> 0.01 us  [chip_scatter_steps(): top_came = lax.ppermute(pick(top, 1 - x, 1), 'x', SWAP)]
    ppermute x21, starting transfers between devices: 85.1 us -> 67.6 us  [rotate(): lax.ppermute(values, 'ctx', [(i, (i + step) % count) for i in range(count)])]
    reduce_scatter x2, waiting for transfers between devices: 10.1 us -> 0.01 us  [chip_scatter(): return lax.psum_scatter(values, CHIPS, scatter_dimension=0, tiled=True)]
    unnamed x156 -> x148, local copies, waits for them, and re-layouts: 25.5 us -> 25.1 us
  transfers between devices with their start and end apart: 59 -> 59, of which waited for: 25 -> 28; matrix products, arithmetic and copies ran while one was open for 16% -> 16% of each run, Pallas kernels for 16% -> 16%
where the time goes in v5:
time: 919 us; the launch traced here: 905 us
  waiting for transfers between devices  342 us (37%)
  Pallas kernels  201 us (22%)
  starting transfers between devices  163 us (18%)
  other arithmetic  69 us (8%)
  matrix products  62.2 us (7%)
  local copies, waits for them, and re-layouts  52.3 us (6%)
  between operations  15.9 us (2%)
    ppermute x21, waiting for transfers between devices, rotate(): lax.ppermute(values, 'ctx', [(i, (i + step) % count) for i in range(count)])  178 us
    ppermute x24, waiting for transfers between devices, shift(): return lax.ppermute(values, 'ctx', pairs)  122 us
    ppermute x24, starting transfers between devices, shift(): return lax.ppermute(values, 'ctx', pairs)  89.5 us
    pallas_call x4, Pallas kernels, weight_rows(): pl.pallas_call(lambda *refs: weight_kernel(shared, parts, *refs), grid_sp...  68.5 us
    ppermute x21, starting transfers between devices, rotate(): lax.ppermute(values, 'ctx', [(i, (i + step) % count) for i in range(count)])  67.6 us
    dot_general x10, matrix products, dot(): return lax.dot_general(left, right, dims, preferred_element_type=WIDE)  62.2 us
    pallas_call x2, Pallas kernels, feed(): pl.pallas_call(feed_kernel, grid=(steps,), in_specs=[whole, whole, pl.Blo...  40.7 us
    pallas_call x2, Pallas kernels, feed_back(): pl.pallas_call(second_kernel, grid=(width // FEED_STEP,), in_specs=[whole...  30.6 us
  transfers between devices with their start and end apart: 59, of which 28 were waited for; matrix products, arithmetic and copies ran while one was open for 16% of the time, Pallas kernels for 16%

profile of v5, /device:TPU:0, one launch (start us, length us, event | category | flops | bytes accessed | tf_op | source)
XLA Modules:
  0.0 905.4 jit_solution(7270878697183704873)
XLA Ops:
  45.2 20.6 %collective-permute-done.4 = bf16[64,4096]{1,0:T(8,128)(2,1)S(1)} collective-permute-done((bf16[64,4096]{1,0:T(8,128)(2,1)}, bf16[64,4096]{1,0:T(8,128)(2,1)S(1)}, u32[]{:S(2)}, u32[]{:S(2)}) %collective-permute-start.4) | collective-permute-done | bytes 524320 | tf_op jit(solution)/shard_map/ppermute | solution.py:390
  103.2 21.2 %collective-permute-done.7 = bf16[64,4096]{1,0:T(8,128)(2,1)S(1)} collective-permute-done((bf16[64,4096]{1,0:T(8,128)(2,1)}, bf16[64,4096]{1,0:T(8,128)(2,1)S(1)}, u32[]{:S(2)}, u32[]{:S(2)}) %collective-permute-start.7) | collective-permute-done | bytes 524320 | tf_op jit(solution)/shard_map/ppermute | solution.py:390
  138.5 12.8 %collective-permute-start.10 = (bf16[256,1024]{1,0:T(8,128)(2,1)}, bf16[256,1024]{1,0:T(8,128)(2,1)S(1)}, u32[]{:S(2)}, u32[]{:S(2)}) collective-permute-start(bf16[256,1024]{1,0:T(8,128)(2,1)} %after.41), channel_id=1, source_target_pairs={{0,2},{1,3},{4,6},{5,7},{8,10},{9,11},{12,14},{13,15},{16,18},{17,... | collective-permute-start | bytes 1572872 | tf_op jit(solution)/shard_map/ppermute | solution.py:386
  186.9 12.7 %collective-permute-start.12 = (bf16[256,2048]{1,0:T(8,128)(2,1)}, bf16[256,2048]{1,0:T(8,128)(2,1)}, u32[]{:S(2)}, u32[]{:S(2)}) collective-permute-start(bf16[256,2048]{1,0:T(8,128)(2,1)} %after.42), channel_id=1, source_target_pairs={{0,1},{1,2},{2,3},{3,0},{4,5},{5,6},{6,7},{7,4},{8,9},{9,10},{10,1... | collective-permute-start | bytes 3145736 | tf_op jit(solution)/shard_map/ppermute | solution.py:390
  210.8 23.8 %attend.1 = (bf16[256,2048]{1,0:T(8,128)(2,1)S(1)}, bf16[256,2048]{1,0:T(8,128)(2,1)S(1)}, f32[32,256]{1,0:T(8,128)S(1)}) custom-call(f32[256,2048]{1,0:T(8,128)S(1)} %fusion.6.raw_ref, f32[256,128]{1,0:T(8,128)S(1)} %copy-done.8, f32[256,128]{1,0:T(8,128)S(1)} %copy-done.9, bf16[1024,1024]{1,0:T(8,128)(2,1)S(1)} %copy-done, bf16[1024,1024]{1,0:T(8,128)(2,1)S(1)} %copy-done, ...), custom_call_target="tpu_custom_call" | custom-call | flops 1000000 | bytes 1000000 | tf_op jit(solution)/shard_map/attend/pallas_call | solution.py:319
  244.8 15.3 %collective-permute-done.13.refs_2_ = bf16[256,2048]{1,0:T(8,128)(2,1)} collective-permute-done((bf16[256,2048]{1,0:T(8,128)(2,1)}, bf16[256,2048]{1,0:T(8,128)(2,1)}, u32[]{:S(2)}, u32[]{:S(2)}) %collective-permute-start.13) | collective-permute-done | bytes 1048608 | tf_op jit(solution)/shard_map/ppermute | solution.py:390
  268.8 28.4 %collective-permute-start.15 = (bf16[256,2048]{1,0:T(8,128)(2,1)}, bf16[256,2048]{1,0:T(8,128)(2,1)}, u32[]{:S(2)}, u32[]{:S(2)}) collective-permute-start(bf16[256,2048]{1,0:T(8,128)(2,1)} %after.43), channel_id=1, source_target_pairs={{0,1},{1,2},{2,3},{4,5},{5,6},{6,7},{8,9},{9,10},{10,11},{12,13},{... | collective-permute-start | bytes 3145736 | tf_op jit(solution)/shard_map/ppermute | solution.py:386
  297.2 19.8 %collective-permute-done.17 = bf16[256,2048]{1,0:T(8,128)(2,1)} collective-permute-done((bf16[256,2048]{1,0:T(8,128)(2,1)}, bf16[256,2048]{1,0:T(8,128)(2,1)}, u32[]{:S(2)}, u32[]{:S(2)}) %collective-permute-start.17) | collective-permute-done | bytes 1048608 | tf_op jit(solution)/shard_map/ppermute | solution.py:386
  324.0 18.6 %collective-permute-done.18 = bf16[256,2048]{1,0:T(8,128)(2,1)} collective-permute-done((bf16[256,2048]{1,0:T(8,128)(2,1)}, bf16[256,2048]{1,0:T(8,128)(2,1)}, u32[]{:S(2)}, u32[]{:S(2)}) %collective-permute-start.18) | collective-permute-done | bytes 1048608 | tf_op jit(solution)/shard_map/ppermute | solution.py:386
  351.4 20.3 %feed.2 = (bf16[512,2048]{1,0:T(8,128)(2,1)}, bf16[512,2048]{1,0:T(8,128)(2,1)}, bf16[512,2048]{1,0:T(8,128)(2,1)}) custom-call(bf16[512,2048]{1,0:T(8,128)(2,1)} %pad_maximum_fusion.2.token_ref.refs_1_, bf16[512,2048]{1,0:T(8,128)(2,1)} %constant_dynamic-update-slice_fusion.1.goal_ref.refs_9_, ...), custom_call_target="tpu_custom_call" | custom-call | flops 1000000 | bytes 1000000 | tf_op jit(solution)/shard_map/feed/pallas_call | solution.py:207
  376.1 20.4 %feed.3 = (bf16[512,2048]{1,0:T(8,128)(2,1)}, bf16[512,2048]{1,0:T(8,128)(2,1)}, bf16[512,2048]{1,0:T(8,128)(2,1)}) custom-call(bf16[512,2048]{1,0:T(8,128)(2,1)} %pad_maximum_fusion.3.token_ref.refs_2_, bf16[512,2048]{1,0:T(8,128)(2,1)} %after.45.goal_ref.refs_10_, bf16[2048,4096]{1,0:T(8,128)(2,1)} %all-gather.9.cloned.1.call-done.gate_ref.up_ref, ...), custom_call_target="tpu_custom_call" | custom-call | flops 1000000 | bytes 1000000 | tf_op jit(solution)/shard_map/feed/pallas_call | solution.py:207
  396.5 15.2 %feed_back.2.refs_1_ = bf16[512,2048]{1,0:T(8,128)(2,1)} custom-call(bf16[512,2048]{1,0:T(8,128)(2,1)} %get-tuple-element.26.grad_gate_ref.refs_6_, bf16[512,2048]{1,0:T(8,128)(2,1)} %get-tuple-element.27.grad_up_ref.refs_8_, bf16[2048,4096]{1,0:T(8,128)(2,1)} %all-gather.9.cloned.1.call-done.gate_ref.up_ref, ...), custom_call_target="tpu_custom_call" | custom-call | flops 1000000 | bytes 1000000 | tf_op jit(solution)/shard_map/feed_back/pallas_call | solution.py:229
  423.0 15.3 %feed_back.3 = bf16[512,2048]{1,0:T(8,128)(2,1)} custom-call(bf16[512,2048]{1,0:T(8,128)(2,1)} %get-tuple-element.28.grad_gate_ref.refs_0_, bf16[512,2048]{1,0:T(8,128)(2,1)} %after.47.grad_up_ref.refs_7_, bf16[2048,4096]{1,0:T(8,128)(2,1)} %all-gather.9.cloned.1.call-done.gate_ref.up_ref, bf16[2048,4096]{1,0:T(8,128)(2,1)} %all-gather.9.cloned.1.call-done.gate_ref.up_ref), custom_call_target="tpu_custom_call" | custom-call | flops 1000000 | bytes 1000000 | tf_op jit(solution)/shard_map/feed_back/pallas_call | solution.py:229
  455.2 23.0 %weight_rows.4.refs_0_ = bf16[3072,2048]{1,0:T(8,128)(2,1)} custom-call(s32[1]{0:T(128)} %bitcast.29.refs_0_, bf16[512,2048]{1,0:T(8,128)(2,1)} %pad_maximum_fusion.2.token_ref.refs_1_, bf16[512,2048]{1,0:T(8,128)(2,1)} %pad_maximum_fusion.3.token_ref.refs_2_, bf16[512,2048]{1,0:T(8,128)(2,1)} %get-tuple-element.24.refs_1_.refs_3_, ...), custom_call_target="tpu_custom_call" | custom-call | flops 12884901888 | bytes 12582912 | tf_op jit(solution)/shard_map/weight_rows/pallas_call | solution.py:274
  512.0 24.5 %weight_rows.5.refs_1_ = bf16[3072,2048]{1,0:T(8,128)(2,1)} custom-call(s32[1]{0:T(128)} %bitcast.28.refs_0_, bf16[512,2048]{1,0:T(8,128)(2,1)} %pad_maximum_fusion.2.token_ref.refs_1_, bf16[512,2048]{1,0:T(8,128)(2,1)} %pad_maximum_fusion.3.token_ref.refs_2_, bf16[512,2048]{1,0:T(8,128)(2,1)} %get-tuple-element.24.refs_1_.refs_3_, ...), custom_call_target="tpu_custom_call" | custom-call | flops 12884901888 | bytes 12582912 | tf_op jit(solution)/shard_map/weight_rows/pallas_call | solution.py:274
  558.5 12.0 %collective-permute-done.27 = bf16[256,2048]{1,0:T(8,128)(2,1)S(1)} collective-permute-done((bf16[256,2048]{1,0:T(8,128)(2,1)}, bf16[256,2048]{1,0:T(8,128)(2,1)S(1)}, u32[]{:S(2)}, u32[]{:S(2)}) %collective-permute-start.27) | collective-permute-done | bytes 1048608 | tf_op jit(solution)/shard_map/ppermute | solution.py:386
  585.7 22.6 %attend_back.1 = (bf16[256,2048]{1,0:T(8,128)(2,1)S(1)}, bf16[1024,512]{1,0:T(8,128)(2,1)S(1)}, bf16[1024,512]{1,0:T(8,128)(2,1)S(1)}) custom-call(bf16[256,2048]{1,0:T(8,128)(2,1)S(1)} %copy-done.15, f32[256,128]{1,0:T(8,128)S(1)} %copy-done.8, f32[256,128]{1,0:T(8,128)S(1)} %copy-done.9, bf16[1024,1024]{1,0:T(8,128)(2,1)S(1)} %copy-done, ...), custom_call_target="tpu_custom_call" | custom-call | flops 24000000000 | bytes 10000000 | tf_op jit(solution)/shard_map/attend_back/pallas_call | solution.py:341
  633.2 13.5 %collective-permute-done.47.refs_5_ = bf16[2048,2048]{1,0:T(8,128)(2,1)} collective-permute-done((bf16[2048,2048]{1,0:T(8,128)(2,1)}, bf16[2048,2048]{1,0:T(8,128)(2,1)}, u32[]{:S(2)}, u32[]{:S(2)}) %collective-permute-start.47) | collective-permute-done | bytes 8388640 | tf_op jit(solution)/shard_map/ppermute | solution.py:487
  660.9 27.1 %collective-permute-done.34 = bf16[256,1024]{1,0:T(8,128)(2,1)} collective-permute-done((bf16[256,1024]{1,0:T(8,128)(2,1)}, bf16[256,1024]{1,0:T(8,128)(2,1)}, u32[]{:S(2)}, u32[]{:S(2)}) %collective-permute-start.34) | collective-permute-done | bytes 524320 | tf_op jit(solution)/shard_map/ppermute | solution.py:386
  715.8 22.9 %collective-permute-done.44 = bf16[2,128,1152]{2,1,0:T(8,128)(2,1)S(1)} collective-permute-done((bf16[2,128,1152]{2,1,0:T(8,128)(2,1)S(1)}, bf16[2,128,1152]{2,1,0:T(8,128)(2,1)S(1)}, u32[]{:S(2)}, u32[]{:S(2)}) %collective-permute-start.44) | collective-permute-done | bytes 589856 | tf_op jit(solution)/shard_map/ppermute | solution.py:515
  760.2 21.2 %collective-permute-done.40.refs_1_.refs_2_ = bf16[128,2048]{1,0:T(8,128)(2,1)} collective-permute-done((bf16[128,2048]{1,0:T(8,128)(2,1)S(1)}, bf16[128,2048]{1,0:T(8,128)(2,1)}, u32[]{:S(2)}, u32[]{:S(2)}) %collective-permute-start.40) | collective-permute-done | bytes 524320 | tf_op jit(solution)/shard_map/ppermute | solution.py:390
  812.0 12.6 %collective-permute-start.46 = (bf16[64,1152]{1,0:T(8,128)(2,1)}, bf16[64,1152]{1,0:T(8,128)(2,1)}, u32[]{:S(2)}, u32[]{:S(2)}) collective-permute-start(bf16[64,1152]{1,0:T(8,128)(2,1)} %get-tuple-element.81), channel_id=1, source_target_pairs={{0,1},{1,2},{2,3},{3,0},{4,5},{5,6},{6,7},{7,4},{8,9},{9,10},{10,1... | collective-permute-start | bytes 442376 | tf_op jit(solution)/shard_map/ppermute | solution.py:390
  834.6 23.7 %collective-permute-done.48.refs_0_ = bf16[128,2048]{1,0:T(8,128)(2,1)S(1)} collective-permute-done((bf16[128,2048]{1,0:T(8,128)(2,1)S(1)}, bf16[128,2048]{1,0:T(8,128)(2,1)S(1)}, u32[]{:S(2)}, u32[]{:S(2)}) %collective-permute-start.48) | collective-permute-done | bytes 524320 | tf_op jit(solution)/shard_map/ppermute | solution.py:390
  874.9 18.9 %collective-permute-done.52.refs_0_ = bf16[128,2048]{1,0:T(8,128)(2,1)S(1)} collective-permute-done((bf16[128,2048]{1,0:T(8,128)(2,1)}, bf16[128,2048]{1,0:T(8,128)(2,1)S(1)}, u32[]{:S(2)}, u32[]{:S(2)}) %collective-permute-start.52) | collective-permute-done | bytes 524320 | tf_op jit(solution)/shard_map/ppermute | solution.py:390
  (421 shorter events, 423.1 us)
Async XLA Ops:
  7.2 121.8 %all-gather.5.cloned.1.call-start = ((), (), s32[]{:S(2)}) async-start(), calls=%async_computation.2 | async-start | bytes 5308416 | tf_op jit(solution)/shard_map/all_gather | solution.py:449
  26.3 178.3 %all-gather.7.cloned.1.call-start = ((), (), s32[]{:S(2)}) async-start(), calls=%async_computation.3 | async-start | bytes 18874368 | tf_op jit(solution)/shard_map/all_gather | solution.py:449
  30.8 35.0 %collective-permute-start.4 = (bf16[64,4096]{1,0:T(8,128)(2,1)}, bf16[64,4096]{1,0:T(8,128)(2,1)S(1)}, u32[]{:S(2)}, u32[]{:S(2)}) collective-permute-start(bf16[64,4096]{1,0:T(8,128)(2,1)} %after.37), channel_id=1, source_target_pairs={{0,2},{1,3},{2,0},{3,1},{4,6},{5,7},{6,4},{7,5},{8,10},{9,11},{10,... | collective-permute-start | bytes 1572872 | tf_op jit(solution)/shard_map/ppermute | solution.py:390
  67.3 284.1 %all-gather.11.cloned.1.call-start = ((), (), s32[]{:S(2)}) async-start(), calls=%async_computation.5 | async-start | bytes 9437184 | tf_op jit(solution)/shard_map/all_gather | solution.py:449
  70.1 281.3 %all-gather.9.cloned.1.call-start = ((), (), s32[]{:S(2)}) async-start(), calls=%async_computation.4 | async-start | bytes 18874368 | tf_op jit(solution)/shard_map/all_gather | solution.py:449
  125.9 621.5 %reduce-scatter.3.cloned.1.call-start = ((), (), s32[]{:S(2)}) async-start(), calls=%async_computation.6 | async-start | bytes 15728640 | tf_op jit(solution)/shard_map/reduce_scatter | solution.py:502
  186.9 57.9 %collective-permute-start.12 = (bf16[256,2048]{1,0:T(8,128)(2,1)}, bf16[256,2048]{1,0:T(8,128)(2,1)}, u32[]{:S(2)}, u32[]{:S(2)}) collective-permute-start(bf16[256,2048]{1,0:T(8,128)(2,1)} %after.42), channel_id=1, source_target_pairs={{0,1},{1,2},{2,3},{3,0},{4,5},{5,6},{6,7},{7,4},{8,9},{9,10},{10,1... | collective-permute-start | bytes 3145736 | tf_op jit(solution)/shard_map/ppermute | solution.py:390
  199.6 60.5 %collective-permute-start.13 = (bf16[256,2048]{1,0:T(8,128)(2,1)}, bf16[256,2048]{1,0:T(8,128)(2,1)}, u32[]{:S(2)}, u32[]{:S(2)}) collective-permute-start(bf16[256,2048]{1,0:T(8,128)(2,1)} %after.42), channel_id=1, source_target_pairs={{0,2},{1,3},{2,0},{3,1},{4,6},{5,7},{6,4},{7,5},{8,10},{9,11},{10,... | collective-permute-start | bytes 3145736 | tf_op jit(solution)/shard_map/ppermute | solution.py:390
  201.6 66.0 %collective-permute-start.14 = (bf16[256,2048]{1,0:T(8,128)(2,1)}, bf16[256,2048]{1,0:T(8,128)(2,1)}, u32[]{:S(2)}, u32[]{:S(2)}) collective-permute-start(bf16[256,2048]{1,0:T(8,128)(2,1)} %after.42), channel_id=1, source_target_pairs={{0,3},{1,0},{2,1},{3,2},{4,7},{5,4},{6,5},{7,6},{8,11},{9,8},{10,9... | collective-permute-start | bytes 3145736 | tf_op jit(solution)/shard_map/ppermute | solution.py:390
  267.5 49.4 %collective-permute-start.17 = (bf16[256,2048]{1,0:T(8,128)(2,1)}, bf16[256,2048]{1,0:T(8,128)(2,1)}, u32[]{:S(2)}, u32[]{:S(2)}) collective-permute-start(bf16[256,2048]{1,0:T(8,128)(2,1)} %after.43), channel_id=1, source_target_pairs={{1,0},{2,1},{3,2},{5,4},{6,5},{7,6},{9,8},{10,9},{11,10},{13,12},{... | collective-permute-start | bytes 3145736 | tf_op jit(solution)/shard_map/ppermute | solution.py:386
  268.8 49.4 %collective-permute-start.15 = (bf16[256,2048]{1,0:T(8,128)(2,1)}, bf16[256,2048]{1,0:T(8,128)(2,1)}, u32[]{:S(2)}, u32[]{:S(2)}) collective-permute-start(bf16[256,2048]{1,0:T(8,128)(2,1)} %after.43), channel_id=1, source_target_pairs={{0,1},{1,2},{2,3},{4,5},{5,6},{6,7},{8,9},{9,10},{10,11},{12,13},{... | collective-permute-start | bytes 3145736 | tf_op jit(solution)/shard_map/ppermute | solution.py:386
  536.6 291.6 %reduce-scatter.5.cloned.1.call-start = ((), (), s32[]{:S(2)}) async-start(), calls=%async_computation.7 | async-start | bytes 10485760 | tf_op jit(solution)/shard_map/reduce_scatter | solution.py:502
  573.8 37.4 %collective-permute-start.31 = (bf16[256,2048]{1,0:T(8,128)(2,1)}, bf16[256,2048]{1,0:T(8,128)(2,1)}, u32[]{:S(2)}, u32[]{:S(2)}) collective-permute-start(bf16[256,2048]{1,0:T(8,128)(2,1)} %get-tuple-element.58.refs_2_), channel_id=1, source_target_pairs={{2,1},{3,2},{6,5},{7,6},{10,9},{11,10},{14,13},{15,14},{18,17},{19... | collective-permute-start | bytes 3145736 | tf_op jit(solution)/shard_map/ppermute | solution.py:386
  575.4 35.8 %collective-permute-start.28 = (bf16[256,2048]{1,0:T(8,128)(2,1)}, bf16[256,2048]{1,0:T(8,128)(2,1)}, u32[]{:S(2)}, u32[]{:S(2)}) collective-permute-start(bf16[256,2048]{1,0:T(8,128)(2,1)} %get-tuple-element.57.refs_1_), channel_id=1, source_target_pairs={{0,1},{1,2},{4,5},{5,6},{8,9},{9,10},{12,13},{13,14},{16,17},{17,1... | collective-permute-start | bytes 3145736 | tf_op jit(solution)/shard_map/ppermute | solution.py:386
  708.6 95.4 %collective-permute-start.38 = (bf16[256,2048]{1,0:T(8,128)(2,1)}, bf16[256,2048]{1,0:T(8,128)(2,1)}, u32[]{:S(2)}, u32[]{:S(2)}) collective-permute-start(bf16[256,2048]{1,0:T(8,128)(2,1)} %get-tuple-element.56.refs_2_), channel_id=1, source_target_pairs={{1,0},{2,1},{3,2},{5,4},{6,5},{7,6},{9,8},{10,9},{11,10},{13,12},{... | collective-permute-start | bytes 3145736 | tf_op jit(solution)/shard_map/ppermute | solution.py:386
  714.1 36.4 %collective-permute-start.39 = (bf16[2,128,1152]{2,1,0:T(8,128)(2,1)S(1)}, bf16[2,128,1152]{2,1,0:T(8,128)(2,1)S(1)}, u32[]{:S(2)}, u32[]{:S(2)}) collective-permute-start(bf16[2,128,1152]{2,1,0:T(8,128)(2,1)S(1)} %dynamic-slice_bitcast_fusion), channel_id=1, source_target_pairs={{0,8},{8,0},{1,9},{9,1},{2,10},{10,2},{3,11},{11,3},{4,12},{12,4},... | collective-permute-start | bytes 1769480 | tf_op jit(solution)/shard_map/ppermute | solution.py:514
  743.0 61.0 %collective-permute-start.37 = (bf16[256,2048]{1,0:T(8,128)(2,1)}, bf16[256,2048]{1,0:T(8,128)(2,1)}, u32[]{:S(2)}, u32[]{:S(2)}) collective-permute-start(bf16[256,2048]{1,0:T(8,128)(2,1)} %after.60), channel_id=1, source_target_pairs={{0,1},{1,2},{2,3},{4,5},{5,6},{6,7},{8,9},{9,10},{10,11},{12,13},{... | collective-permute-start | bytes 3145736 | tf_op jit(solution)/shard_map/ppermute | solution.py:386
  750.5 42.2 %collective-permute-start.41 = (bf16[128,2048]{1,0:T(8,128)(2,1)S(1)}, bf16[128,2048]{1,0:T(8,128)(2,1)}, u32[]{:S(2)}, u32[]{:S(2)}) collective-permute-start(bf16[128,2048]{1,0:T(8,128)(2,1)S(1)} %bitcast.165), channel_id=1, source_target_pairs={{0,2},{1,3},{2,0},{3,1},{4,6},{5,7},{6,4},{7,5},{8,10},{9,11},{10,... | collective-permute-start | bytes 1572872 | tf_op jit(solution)/shard_map/ppermute | solution.py:390
  754.7 47.7 %collective-permute-start.42 = (bf16[128,2048]{1,0:T(8,128)(2,1)S(1)}, bf16[128,2048]{1,0:T(8,128)(2,1)}, u32[]{:S(2)}, u32[]{:S(2)}) collective-permute-start(bf16[128,2048]{1,0:T(8,128)(2,1)S(1)} %bitcast.164), channel_id=1, source_target_pairs={{0,3},{1,0},{2,1},{3,2},{4,7},{5,4},{6,5},{7,6},{8,11},{9,8},{10,9... | collective-permute-start | bytes 1572872 | tf_op jit(solution)/shard_map/ppermute | solution.py:390
  812.0 57.2 %collective-permute-start.46 = (bf16[64,1152]{1,0:T(8,128)(2,1)}, bf16[64,1152]{1,0:T(8,128)(2,1)}, u32[]{:S(2)}, u32[]{:S(2)}) collective-permute-start(bf16[64,1152]{1,0:T(8,128)(2,1)} %get-tuple-element.81), channel_id=1, source_target_pairs={{0,1},{1,2},{2,3},{3,0},{4,5},{5,6},{6,7},{7,4},{8,9},{9,10},{10,1... | collective-permute-start | bytes 442376 | tf_op jit(solution)/shard_map/ppermute | solution.py:390
  824.6 44.6 %collective-permute-start.49 = (bf16[64,1152]{1,0:T(8,128)(2,1)}, bf16[64,1152]{1,0:T(8,128)(2,1)S(1)}, u32[]{:S(2)}, u32[]{:S(2)}) collective-permute-start(bf16[64,1152]{1,0:T(8,128)(2,1)} %get-tuple-element.83), channel_id=1, source_target_pairs={{0,2},{1,3},{2,0},{3,1},{4,6},{5,7},{6,4},{7,5},{8,10},{9,11},{10,... | collective-permute-start | bytes 442376 | tf_op jit(solution)/shard_map/ppermute | solution.py:390
  828.1 41.8 %collective-permute-start.50 = (bf16[64,1152]{1,0:T(8,128)(2,1)}, bf16[64,1152]{1,0:T(8,128)(2,1)S(1)}, u32[]{:S(2)}, u32[]{:S(2)}) collective-permute-start(bf16[64,1152]{1,0:T(8,128)(2,1)} %get-tuple-element.82), channel_id=1, source_target_pairs={{0,3},{1,0},{2,1},{3,2},{4,7},{5,4},{6,5},{7,6},{8,11},{9,8},{10,9... | collective-permute-start | bytes 442376 | tf_op jit(solution)/shard_map/ppermute | solution.py:390
  831.0 41.7 %collective-permute-start.51 = (bf16[128,2048]{1,0:T(8,128)(2,1)}, bf16[128,2048]{1,0:T(8,128)(2,1)S(1)}, u32[]{:S(2)}, u32[]{:S(2)}) collective-permute-start(bf16[128,2048]{1,0:T(8,128)(2,1)} %get-tuple-element.46), channel_id=1, source_target_pairs={{0,2},{1,3},{2,0},{3,1},{4,6},{5,7},{6,4},{7,5},{8,10},{9,11},{10,... | collective-permute-start | bytes 1572872 | tf_op jit(solution)/shard_map/ppermute | solution.py:390
  859.1 34.7 %collective-permute-start.52 = (bf16[128,2048]{1,0:T(8,128)(2,1)}, bf16[128,2048]{1,0:T(8,128)(2,1)S(1)}, u32[]{:S(2)}, u32[]{:S(2)}) collective-permute-start(bf16[128,2048]{1,0:T(8,128)(2,1)} %get-tuple-element.47), channel_id=1, source_target_pairs={{0,3},{1,0},{2,1},{3,2},{4,7},{5,4},{6,5},{7,6},{8,11},{9,8},{10,9... | collective-permute-start | bytes 1572872 | tf_op jit(solution)/shard_map/ppermute | solution.py:390
  (108 other events, 1598.5 us)
Sparse Core Ops, SparseCore 0:
  26.4 41.2 all-gather.4
  70.1 98.2 all-gather.6
  170.3 54.3 all-gather.10
  227.0 89.8 all-gather.8
  536.7 120.6 reduce-scatter.2
  660.3 112.1 reduce-scatter.4
